TPU v7x, 32 devices: a whole 2x2x4 slice. The times are simulated.
32 devices in a mesh: stream: 8 (over z, x), tm: 4 (over y, core).
Axes of the slice: x: 2, y: 2, z: 4, core: 2. Of those that a mesh axis runs over, the one named last changes fastest.
Arguments:
- hidden: bfloat16 [16, 512, 1024], P('stream', 'tm'), may hold values from -6 to 6
- memory: bfloat16 [16, 512, 1024], P('stream', 'tm'), may hold values from -6 to 6
- compressed: bfloat16 [16, 512, 1024], P('stream', 'tm'), may hold values from -6 to 6
- reset_flag: int32 [16], P('stream'), may hold values from 0 to 1, as said below
- boundary: int32 [16, 512], P('stream'), may hold values from 0 to 1
- query_weight: bfloat16 [1024, 1024], P('stream'), may hold values from -0.1875 to 0.1875
- key_weight: bfloat16 [1024, 1024], P('stream'), may hold values from -0.1875 to 0.1875
- value_weight: bfloat16 [1024, 1024], P('stream'), may hold values from -0.1875 to 0.1875
- output_weight: bfloat16 [1024, 1024], P('stream'), may hold values from -3 to 3
- up_weight: bfloat16 [1024, 4096], P('stream'), may hold values from -0.1875 to 0.1875
- down_weight: bfloat16 [4096, 1024], P('stream'), may hold values from -0.09375 to 0.09375
- conv_weight: bfloat16 [4, 1024, 1024], P(None, 'stream'), may hold values from -0.09375 to 0.09375
- attn_gain: bfloat16 [1024], P('stream'), may hold values from 0.099609375 to 1.8984375
- ffn_gain: bfloat16 [1024], P('stream'), may hold values from 0.099609375 to 1.8984375
- grad_out: bfloat16 [16, 512, 1024], P('stream', 'tm'), may hold values from -6 to 6
- grad_fresh: bfloat16 [16, 256, 1024], P('stream', 'tm'), may hold values from -6 to 6
Outputs:
- layer_out: bfloat16 [16, 512, 1024], P('stream', 'tm')
- fresh_memory: bfloat16 [16, 256, 1024], P('stream', 'tm')
- grad_input: float32 [16, 512, 1024], P('stream', 'tm')
- query_grad: float32 [1024, 1024], P('stream')
- key_grad: float32 [1024, 1024], P('stream')
- value_grad: float32 [1024, 1024], P('stream')
- output_grad: float32 [1024, 1024], P('stream')
- up_grad: float32 [1024, 4096], P('stream')
- down_grad: float32 [4096, 1024], P('stream')
- conv_grad: float32 [4, 1024, 1024], P(None, 'stream')
- attn_gain_grad: float32 [1024], P('stream')
- ffn_gain_grad: float32 [1024], P('stream')
Inputs may be any that keep to these rules, and one draw needn't show every extreme that they name: In every aligned group of 2 streams at least one stream has reset_flag 0 and no boundary.
All inputs are finite; a program needn't handle non-finite values.
Results may differ from a plain program's by a relative error of at most 0.013.
Values may be sent and summed in bfloat16 or wider, within the bound.
A program may use at most 256 MiB of HBM per device.

v0:
```python
import jax
import jax.numpy as jnp
from jax import lax
from jax.sharding import PartitionSpec as P

HEADS = 8
HEAD_DIM = 128
SEG = 512
MEM = 512
CMEM = 512


def with_halo(array, sides, width):
    for axis, dim in sides:
        size, length = (lax.axis_size(axis), array.shape[dim])
        up = [(i, (i + 1) % size) for i in range(size - 1)]
        down = [(j, i) for i, j in up]
        last = lax.slice_in_dim(array, length - width, length, axis=dim)
        leading = lax.slice_in_dim(array, 0, width, axis=dim)
        before = lax.ppermute(last, axis, up)
        after = lax.ppermute(leading, axis, down)
        array = jnp.concatenate([before, array, after], axis=dim)
    return array


def normalize(matrix, scaling):
    center = matrix - jnp.mean(matrix, axis=-1, keepdims=True)
    spread = jnp.mean(center * center, axis=-1, keepdims=True)
    return center * lax.rsqrt(spread + 1e-05) * scaling


def rotate(tensor, places):
    half_dim = tensor.shape[-1] // 2
    frequency = 10000.0 ** (-jnp.arange(half_dim).astype(jnp.float32) * 2.0 / tensor.shape[-1])
    angles = places[:, None] * frequency[None, :]
    cosine = jnp.cos(angles)[:, None, :]
    sines = jnp.sin(angles)[:, None, :]
    first_half = tensor[..., :half_dim]
    second = tensor[..., half_dim:]
    return jnp.concatenate(
        [first_half * cosine - second * sines, first_half * sines + second * cosine], axis=-1
    )


def exact_gelu(preact):
    return jax.nn.gelu(preact, approximate=False)


def per_device(
    hidden,
    memory,
    compressed,
    reset_flag,
    boundary,
    query_weight,
    key_weight,
    value_weight,
    output_weight,
    up_weight,
    down_weight,
    conv_weight,
    attn_gain,
    ffn_gain,
    grad_out,
    grad_fresh,
):
    streams, seg_rows, model_width = hidden.shape
    comp_rows = compressed.shape[1]
    mem_rows = memory.shape[1]
    front_rows = comp_rows + mem_rows
    local_rows = front_rows + seg_rows
    key_count = CMEM + MEM + SEG
    time_rank = lax.axis_index("tm")
    gathered = (
        lax.all_gather(query_weight, "stream", axis=0, tiled=True),
        lax.all_gather(key_weight, "stream", axis=0, tiled=True),
        lax.all_gather(value_weight, "stream", axis=0, tiled=True),
        lax.all_gather(output_weight, "stream", axis=0, tiled=True),
        lax.all_gather(up_weight, "stream", axis=0, tiled=True),
        lax.all_gather(down_weight, "stream", axis=0, tiled=True),
        lax.all_gather(conv_weight, "stream", axis=1, tiled=True),
        lax.all_gather(attn_gain, "stream", axis=0, tiled=True),
        lax.all_gather(ffn_gain, "stream", axis=0, tiled=True),
    )
    (
        query_full,
        key_full,
        value_full,
        output_full,
        up_full,
        down_full,
        conv_full,
        attn_scale,
        ffn_scale,
    ) = gathered
    comp_places = time_rank * comp_rows + jnp.arange(comp_rows)
    mem_places = CMEM + time_rank * mem_rows + jnp.arange(mem_rows)
    seg_spots = time_rank * seg_rows + jnp.arange(seg_rows)
    seg_places = CMEM + MEM + seg_spots
    places = jnp.concatenate([comp_places, mem_places, seg_places]).astype(jnp.float32)
    query_places = seg_places.astype(jnp.float32)
    score_scale = HEAD_DIM ** (-0.5)
    context = jnp.concatenate([compressed, memory, hidden], axis=1).astype(jnp.float32)
    normed, norm_back = jax.vjp(normalize, context, attn_scale.astype(jnp.float32))
    normed_low = normed.astype(jnp.bfloat16)
    query_raw = jnp.dot(normed_low[:, front_rows:], query_full, preferred_element_type=jnp.float32)
    query_low = (
        rotate(query_raw.reshape(streams, seg_rows, HEADS, HEAD_DIM), query_places) * score_scale
    ).astype(jnp.bfloat16)
    key_raw = jnp.dot(normed_low, key_full, preferred_element_type=jnp.float32)
    key_low = (
        rotate(key_raw.reshape(streams, local_rows, HEADS, HEAD_DIM), places)
        .astype(jnp.bfloat16)
        .reshape(streams, local_rows, model_width)
    )
    value_low = jnp.dot(normed_low, value_full, preferred_element_type=jnp.float32).astype(
        jnp.bfloat16
    )
    pieces = (
        lax.all_gather(key_low[:, :comp_rows], "tm", axis=1, tiled=True),
        lax.all_gather(key_low[:, comp_rows:front_rows], "tm", axis=1, tiled=True),
        lax.all_gather(key_low[:, front_rows:], "tm", axis=1, tiled=True),
        lax.all_gather(value_low[:, :comp_rows], "tm", axis=1, tiled=True),
        lax.all_gather(value_low[:, comp_rows:front_rows], "tm", axis=1, tiled=True),
        lax.all_gather(value_low[:, front_rows:], "tm", axis=1, tiled=True),
    )
    all_keys = jnp.concatenate([pieces[0], pieces[1], pieces[2]], axis=1).reshape(
        streams, key_count, HEADS, HEAD_DIM
    )
    all_values = jnp.concatenate([pieces[3], pieces[4], pieces[5]], axis=1).reshape(
        streams, key_count, HEADS, HEAD_DIM
    )
    documents = jnp.cumsum(boundary, axis=1)
    query_docs = lax.dynamic_slice_in_dim(documents, time_rank * seg_rows, seg_rows, 1)
    memory_ok = (reset_flag[:, None] == 0) & (query_docs == 0)
    local_ok = (jnp.arange(SEG)[None, None, :] <= seg_spots[None, :, None]) & (
        documents[:, None, :] == query_docs[:, :, None]
    )
    visible = jnp.concatenate(
        [jnp.broadcast_to(memory_ok[:, :, None], (streams, seg_rows, CMEM + MEM)), local_ok], axis=2
    )

    def masked_scores():
        raw_scores = jnp.einsum(
            "sqhd,skhd->shqk", query_low, all_keys, preferred_element_type=jnp.float32
        )
        return jnp.where(visible[:, None], raw_scores, -1e30)

    scores = masked_scores()
    row_max = jnp.max(scores, axis=-1, keepdims=True)
    shifted = jnp.exp(scores - row_max)
    row_sum = jnp.sum(shifted, axis=-1, keepdims=True)
    log_norm = row_max + jnp.log(row_sum)
    attention_low = (shifted / row_sum).astype(jnp.bfloat16)
    attended = jnp.einsum(
        "shqk,skhd->sqhd", attention_low, all_values, preferred_element_type=jnp.float32
    )
    attended = attended.reshape(streams, seg_rows, model_width).astype(jnp.bfloat16)
    middle = hidden.astype(jnp.float32) + jnp.dot(
        attended, output_full, preferred_element_type=jnp.float32
    )
    normed_ffn, ffn_back = jax.vjp(normalize, middle, ffn_scale.astype(jnp.float32))
    normed_ffn_low = normed_ffn.astype(jnp.bfloat16)
    preact = jnp.dot(normed_ffn_low, up_full, preferred_element_type=jnp.float32)
    activated, gelu_back = jax.vjp(exact_gelu, preact)
    activated_low = activated.astype(jnp.bfloat16)
    layer_out = (
        middle + jnp.dot(activated_low, down_full, preferred_element_type=jnp.float32)
    ).astype(jnp.bfloat16)
    rimmed = with_halo(memory, (("tm", 1),), 1)
    stacked = jnp.concatenate(
        [rimmed[:, offset : offset + mem_rows : 2] for offset in range(4)], axis=2
    )
    fresh_memory = jnp.dot(
        stacked, conv_full.reshape(4 * model_width, model_width), preferred_element_type=jnp.float32
    ).astype(jnp.bfloat16)
    regathered = (
        lax.all_gather(query_weight, "stream", axis=0, tiled=True),
        lax.all_gather(key_weight, "stream", axis=0, tiled=True),
        lax.all_gather(value_weight, "stream", axis=0, tiled=True),
        lax.all_gather(output_weight, "stream", axis=0, tiled=True),
        lax.all_gather(up_weight, "stream", axis=0, tiled=True),
        lax.all_gather(down_weight, "stream", axis=0, tiled=True),
        lax.all_gather(conv_weight, "stream", axis=1, tiled=True),
        lax.all_gather(attn_gain, "stream", axis=0, tiled=True),
        lax.all_gather(ffn_gain, "stream", axis=0, tiled=True),
    )
    (
        query_full,
        key_full,
        value_full,
        output_full,
        up_full,
        down_full,
        conv_full,
        attn_scale,
        ffn_scale,
    ) = regathered
    grad_act = jnp.dot(grad_out, down_full.T, preferred_element_type=jnp.float32)
    down_grad = jnp.einsum(
        "sra,srb->ab", activated_low, grad_out, preferred_element_type=jnp.float32
    )
    grad_pre = gelu_back(grad_act)[0].astype(jnp.bfloat16)
    up_grad = jnp.einsum(
        "sra,srb->ab", normed_ffn_low, grad_pre, preferred_element_type=jnp.float32
    )
    grad_normed_ffn = jnp.dot(grad_pre, up_full.T, preferred_element_type=jnp.float32)
    grad_middle_part, ffn_gain_grad = ffn_back(grad_normed_ffn)
    grad_middle = grad_out.astype(jnp.float32) + grad_middle_part
    conv_grad = jnp.einsum(
        "src,srd->cd", stacked, grad_fresh, preferred_element_type=jnp.float32
    ).reshape(4, model_width, model_width)
    grad_mid_low = grad_middle.astype(jnp.bfloat16)
    output_grad = jnp.einsum(
        "sra,srb->ab", attended, grad_mid_low, preferred_element_type=jnp.float32
    )
    grad_attended = jnp.dot(grad_mid_low, output_full.T, preferred_element_type=jnp.float32).astype(
        jnp.bfloat16
    )
    grad_attended = grad_attended.reshape(streams, seg_rows, HEADS, HEAD_DIM)
    attention = jnp.exp(masked_scores() - log_norm)
    grad_probs = jnp.einsum(
        "sqhd,skhd->shqk", grad_attended, all_values, preferred_element_type=jnp.float32
    )
    inner_sum = jnp.sum(attention * grad_probs, axis=-1, keepdims=True)
    grad_scores = (attention * (grad_probs - inner_sum)).astype(jnp.bfloat16)
    grad_query_rot = jnp.einsum(
        "shqk,skhd->sqhd", grad_scores, all_keys, preferred_element_type=jnp.float32
    )
    attention_low = attention.astype(jnp.bfloat16)
    grad_key_rot = jnp.einsum(
        "shqk,sqhd->skhd", grad_scores, query_low, preferred_element_type=jnp.float32
    ).reshape(streams, key_count, model_width)
    grad_value_all = jnp.einsum(
        "shqk,sqhd->skhd", attention_low, grad_attended, preferred_element_type=jnp.float32
    ).reshape(streams, key_count, model_width)
    returned = (
        lax.psum_scatter(grad_key_rot[:, :CMEM], "tm", scatter_dimension=1, tiled=True),
        lax.psum_scatter(grad_key_rot[:, CMEM : CMEM + MEM], "tm", scatter_dimension=1, tiled=True),
        lax.psum_scatter(grad_key_rot[:, CMEM + MEM :], "tm", scatter_dimension=1, tiled=True),
        lax.psum_scatter(grad_value_all[:, :CMEM], "tm", scatter_dimension=1, tiled=True),
        lax.psum_scatter(
            grad_value_all[:, CMEM : CMEM + MEM], "tm", scatter_dimension=1, tiled=True
        ),
        lax.psum_scatter(grad_value_all[:, CMEM + MEM :], "tm", scatter_dimension=1, tiled=True),
    )
    grad_key_local = jnp.concatenate([returned[0], returned[1], returned[2]], axis=1)
    grad_value_low = jnp.concatenate([returned[3], returned[4], returned[5]], axis=1).astype(
        jnp.bfloat16
    )
    grad_key_low = (
        rotate(grad_key_local.reshape(streams, local_rows, HEADS, HEAD_DIM), -places)
        .astype(jnp.bfloat16)
        .reshape(streams, local_rows, model_width)
    )
    grad_query_low = (
        (rotate(grad_query_rot, -query_places) * score_scale)
        .astype(jnp.bfloat16)
        .reshape(streams, seg_rows, model_width)
    )
    query_grad = jnp.einsum(
        "src,srd->cd",
        normed_low[:, front_rows:],
        grad_query_low,
        preferred_element_type=jnp.float32,
    )
    key_grad = jnp.einsum(
        "src,srd->cd", normed_low, grad_key_low, preferred_element_type=jnp.float32
    )
    value_grad = jnp.einsum(
        "src,srd->cd", normed_low, grad_value_low, preferred_element_type=jnp.float32
    )
    grad_normed = jnp.dot(grad_key_low, key_full.T, preferred_element_type=jnp.float32) + jnp.dot(
        grad_value_low, value_full.T, preferred_element_type=jnp.float32
    )
    grad_normed = grad_normed.at[:, front_rows:].add(
        jnp.dot(grad_query_low, query_full.T, preferred_element_type=jnp.float32)
    )
    grad_context, attn_gain_grad = norm_back(grad_normed)
    grad_input = grad_middle + grad_context[:, front_rows:]
    owned_part = (
        lax.psum_scatter(query_grad, "stream", scatter_dimension=0, tiled=True),
        lax.psum_scatter(key_grad, "stream", scatter_dimension=0, tiled=True),
        lax.psum_scatter(value_grad, "stream", scatter_dimension=0, tiled=True),
        lax.psum_scatter(output_grad, "stream", scatter_dimension=0, tiled=True),
        lax.psum_scatter(up_grad, "stream", scatter_dimension=0, tiled=True),
        lax.psum_scatter(down_grad, "stream", scatter_dimension=0, tiled=True),
        lax.psum_scatter(conv_grad, "stream", scatter_dimension=1, tiled=True),
        lax.psum_scatter(attn_gain_grad, "stream", scatter_dimension=0, tiled=True),
        lax.psum_scatter(ffn_gain_grad, "stream", scatter_dimension=0, tiled=True),
    )
    summed = lax.psum(
        (
            owned_part[0],
            owned_part[1],
            owned_part[2],
            owned_part[3],
            owned_part[4],
            owned_part[5],
            owned_part[6],
            owned_part[7],
            owned_part[8],
        ),
        "tm",
    )
    return (
        layer_out,
        fresh_memory,
        grad_input,
        summed[0],
        summed[1],
        summed[2],
        summed[3],
        summed[4],
        summed[5],
        summed[6],
        summed[7],
        summed[8],
    )


def solution(mesh):
    in_specs = (
        P("stream", "tm", None),
        P("stream", "tm", None),
        P("stream", "tm", None),
        P("stream"),
        P("stream", None),
        P("stream", None),
        P("stream", None),
        P("stream", None),
        P("stream", None),
        P("stream", None),
        P("stream", None),
        P(None, "stream", None),
        P("stream"),
        P("stream"),
        P("stream", "tm", None),
        P("stream", "tm", None),
    )
    out_specs = (
        P("stream", "tm", None),
        P("stream", "tm", None),
        P("stream", "tm", None),
        P("stream", None),
        P("stream", None),
        P("stream", None),
        P("stream", None),
        P("stream", None),
        P("stream", None),
        P(None, "stream", None),
        P("stream"),
        P("stream"),
    )
    return jax.shard_map(
        per_device, mesh=mesh, in_specs=in_specs, out_specs=out_specs, check_vma=False
    )
```

profile of v0, /device:TPU:26, one launch (start us, length us, event | category | flops | bytes accessed | tf_op | source)
XLA Modules:
  0.0 2463.6 jit_solution(17866219609660106920)
XLA Ops:
  9.5 16.1 all-gather
  33.1 24.9 %all-gather.26.cloned.1.call-done = bf16[1024,1024]{1,0:T(8,128)(2,1)} async-done(((bf16[128,1024]{1,0:T(8,128)(2,1)}), bf16[1024,1024]{1,0:T(8,128)(2,1)}) %all-gather.26.cloned.1.call-update) | async-done | bytes 2097168 | tf_op jit(solution)/shard_map/all_gather | solution.py:76
  72.5 35.5 %all-gather.16.cloned.1.call-done = bf16[1024,1024]{1,0:T(8,128)(2,1)} async-done(((bf16[128,1024]{1,0:T(8,128)(2,1)}), bf16[1024,1024]{1,0:T(8,128)(2,1)}) %all-gather.16.cloned.1.call-update) | async-done | bytes 2097168 | tf_op jit(solution)/shard_map/all_gather | solution.py:77
  117.7 16.7 all-gather.1
  135.5 22.5 all-gather.24.cloned.1.call-done
  161.7 22.0 all-gather.28.cloned.1.call-done
  183.7 24.8 %all-gather.30.cloned.1.call-done = bf16[2,512,1024]{1,2,0:T(8,128)(2,1)} async-done(((bf16[2,128,1024]{1,2,0:T(8,128)(2,1)}), bf16[2,512,1024]{1,2,0:T(8,128)(2,1)}) %all-gather.30.cloned.1.call-update) | async-done | bytes 2097168 | tf_op jit(solution)/shard_map/all_gather | solution.py:121
  208.6 24.9 %all-gather.32.cloned.1.call-done = bf16[2,512,1024]{1,2,0:T(8,128)(2,1)} async-done(((bf16[2,128,1024]{1,2,0:T(8,128)(2,1)}), bf16[2,512,1024]{1,2,0:T(8,128)(2,1)}) %all-gather.32.cloned.1.call-update) | async-done | bytes 2097168 | tf_op jit(solution)/shard_map/all_gather | solution.py:122
  247.2 11.0 all-gather.18.cloned.1.call-done
  258.2 24.8 %all-gather.20.cloned.1.call-done = bf16[2,512,1024]{2,1,0:T(8,128)(2,1)} async-done(((bf16[2,128,1024]{2,1,0:T(8,128)(2,1)}), bf16[2,512,1024]{2,1,0:T(8,128)(2,1)}) %all-gather.20.cloned.1.call-update) | async-done | bytes 2097168 | tf_op jit(solution)/shard_map/all_gather | solution.py:124
  283.0 24.8 %all-gather.22.cloned.1.call-done = bf16[2,512,1024]{2,1,0:T(8,128)(2,1)} async-done(((bf16[2,128,1024]{2,1,0:T(8,128)(2,1)}), bf16[2,512,1024]{2,1,0:T(8,128)(2,1)}) %all-gather.22.cloned.1.call-update) | async-done | bytes 2097168 | tf_op jit(solution)/shard_map/all_gather | solution.py:125
  307.7 8.7 fusion.80
  316.4 40.2 %all-gather.34.cloned.1.call-done = bf16[1024,1024]{1,0:T(8,128)(2,1)} async-done(((bf16[128,1024]{1,0:T(8,128)(2,1)}), bf16[1024,1024]{1,0:T(8,128)(2,1)}) %all-gather.34.cloned.1.call-update) | async-done | bytes 2097168 | tf_op jit(solution)/shard_map/all_gather | solution.py:78
  359.3 122.4 %all-gather.36.cloned.1.call-done = bf16[1024,4096]{1,0:T(8,128)(2,1)} async-done(((bf16[128,4096]{1,0:T(8,128)(2,1)}), bf16[1024,4096]{1,0:T(8,128)(2,1)}) %all-gather.36.cloned.1.call-update) | async-done | bytes 8388624 | tf_op jit(solution)/shard_map/all_gather | solution.py:79
  481.7 7.1 fusion.87
  490.7 20.7 multiply_convert_fusion.1
  511.4 95.4 %all-gather.38.cloned.1.call-done = bf16[4096,1024]{1,0:T(8,128)(2,1)} async-done(((bf16[512,1024]{1,0:T(8,128)(2,1)}), bf16[4096,1024]{1,0:T(8,128)(2,1)}) %all-gather.38.cloned.1.call-update) | async-done | bytes 8388624 | tf_op jit(solution)/shard_map/all_gather | solution.py:80
  606.8 11.3 add_convert_fusion
  618.1 7.3 multiply_reduce_fusion.1
  630.4 11.9 fusion.10
  642.2 9.8 fusion.105
  662.9 5.4 copy.113
  668.4 11.7 multiply_reduce_fusion
  680.2 9.4 multiply_convert_fusion
  689.7 6.5 fusion.113
  696.2 9.8 fusion.106
  707.2 6.7 convolution_bitcast_fusion.6
  728.1 22.2 reduce-scatter.22.cloned.1.call-done
  752.4 44.8 %reduce-scatter.24.cloned.1.call-done = f32[2,128,1024]{2,1,0:T(8,128)} async-done(((f32[2,512,1024]{2,1,0:T(8,128)}), f32[2,128,1024]{2,1,0:T(8,128)}) %reduce-scatter.24.cloned.1.call-update) | async-done | bytes 1048592 | tf_op jit(solution)/shard_map/reduce_scatter | solution.py:245
  804.6 39.7 %reduce-scatter.14.cloned.1.call-done = f32[2,128,1024]{1,2,0:T(8,128)} async-done(((f32[2,512,1024]{1,2,0:T(8,128)}), f32[2,128,1024]{1,2,0:T(8,128)}) %reduce-scatter.14.cloned.1.call-update) | async-done | bytes 1048592 | tf_op jit(solution)/shard_map/reduce_scatter | solution.py:238
  844.3 46.9 %reduce-scatter.16.cloned.1.call-done = f32[2,128,1024]{1,2,0:T(8,128)} async-done(((f32[2,512,1024]{1,2,0:T(8,128)}), f32[2,128,1024]{1,2,0:T(8,128)}) %reduce-scatter.16.cloned.1.call-update) | async-done | bytes 1048592 | tf_op jit(solution)/shard_map/reduce_scatter | solution.py:239
  891.3 47.1 %reduce-scatter.18.cloned.1.call-done = f32[2,128,1024]{1,2,0:T(8,128)} async-done(((f32[2,512,1024]{1,2,0:T(8,128)}), f32[2,128,1024]{1,2,0:T(8,128)}) %reduce-scatter.18.cloned.1.call-update) | async-done | bytes 1048592 | tf_op jit(solution)/shard_map/reduce_scatter | solution.py:240
  972.6 9.1 fusion.91
  981.9 9.9 convolution_bitcast_fusion.1
  992.9 9.8 convolution_bitcast_fusion
  1004.7 24.2 reduce-scatter.26.cloned.1.call-done
  1028.9 91.6 %reduce-scatter.32.cloned.1.call-done = f32[128,1024]{1,0:T(8,128)} async-done(((f32[1024,1024]{1,0:T(8,128)}), f32[128,1024]{1,0:T(8,128)}) %reduce-scatter.32.cloned.1.call-update) | async-done | bytes 524304 | tf_op jit(solution)/shard_map/reduce_scatter | solution.py:285
  1120.5 91.5 %reduce-scatter.30.cloned.1.call-done = f32[128,1024]{1,0:T(8,128)} async-done(((f32[1024,1024]{1,0:T(8,128)}), f32[128,1024]{1,0:T(8,128)}) %reduce-scatter.30.cloned.1.call-update) | async-done | bytes 524304 | tf_op jit(solution)/shard_map/reduce_scatter | solution.py:284
  1212.0 91.7 %reduce-scatter.28.cloned.1.call-done = f32[128,1024]{1,0:T(8,128)} async-done(((f32[1024,1024]{1,0:T(8,128)}), f32[128,1024]{1,0:T(8,128)}) %reduce-scatter.28.cloned.1.call-update) | async-done | bytes 524304 | tf_op jit(solution)/shard_map/reduce_scatter | solution.py:283
  1303.7 284.9 %reduce-scatter.38.cloned.1.call-done = f32[4,128,1024]{2,1,0:T(8,128)} async-done(((f32[4,1024,1024]{2,1,0:T(8,128)}), f32[4,128,1024]{2,1,0:T(8,128)}) %reduce-scatter.38.cloned.1.call-update) | async-done | bytes 2097168 | tf_op jit(solution)/shard_map/reduce_scatter | solution.py:288
  1588.6 285.8 %reduce-scatter.34.cloned.1.call-done = f32[128,4096]{1,0:T(8,128)} async-done(((f32[1024,4096]{1,0:T(8,128)}), f32[128,4096]{1,0:T(8,128)}) %reduce-scatter.34.cloned.1.call-update) | async-done | bytes 2097168 | tf_op jit(solution)/shard_map/reduce_scatter | solution.py:286
  1874.4 285.5 %reduce-scatter.36.cloned.1.call-done = f32[512,1024]{1,0:T(8,128)} async-done(((f32[4096,1024]{1,0:T(8,128)}), f32[512,1024]{1,0:T(8,128)}) %reduce-scatter.36.cloned.1.call-update) | async-done | bytes 2097168 | tf_op jit(solution)/shard_map/reduce_scatter | solution.py:287
  2160.0 125.2 %all-gather.40.cloned.1.call-done = bf16[4,1024,1024]{2,1,0:T(8,128)(2,1)} async-done(((bf16[4,128,1024]{2,1,0:T(8,128)(2,1)}), bf16[4,1024,1024]{2,1,0:T(8,128)(2,1)}) %all-gather.40.cloned.1.call-update) | async-done | bytes 8388624 | tf_op jit(solution)/shard_map/all_gather | solution.py:81
  2285.2 5.5 convolution_convert_fusion
  2290.7 6.7 fusion.74
  2305.2 18.9 all-reduce.2
  2328.1 6.7 all-reduce.3
  2337.3 107.5 %all-reduce.7.cloned.1.call-done = (f32[128,1024]{1,0:T(8,128)}, f32[128,1024]{1,0:T(8,128)}, f32[128,1024]{1,0:T(8,128)}, f32[128,1024]{1,0:T(8,128)}, f32[128,...) async-done(((f32[128,1024]{1,0:T(8,128)}, f32[128,1024]{1,0:T(8,128)}, f32[128,1024]{1,0:T(8,128)}, f32[128,1024]{1,0:T(8,128)}, f32[128,4096]{1,0:T(8,128)}, ...) | async-done | bytes 8388624 | tf_op jit(solution)/shard_map/psum | solution.py:292
  (274 shorter events, 159.9 us)
Async XLA Ops:
  7.2 965.4 %copy-start = (bf16[2,64,1024]{2,1,0:T(8,128)(2,1)S(1)}, bf16[2,64,1024]{2,1,0:T(8,128)(2,1)}, u32[]{:S(2)}) copy-start(bf16[2,64,1024]{2,1,0:T(8,128)(2,1)} %param.33) | copy-start | bytes 786436
  7.2 24.2 copy-start.6
  7.2 24.2 copy-start.4
  7.2 24.2 copy-start.11
  7.2 50.8 %all-gather.26.cloned.1.call-start = ((), (), s32[]{:S(2)}) async-start(), calls=%async_computation.18 | async-start | bytes 2359296 | tf_op jit(solution)/shard_map/all_gather | solution.py:76
  8.0 100.0 %all-gather.16.cloned.1.call-start = ((), (), s32[]{:S(2)}) async-start(), calls=%async_computation.13 | async-start | bytes 2359296 | tf_op jit(solution)/shard_map/all_gather | solution.py:77
  8.7 149.2 %all-gather.24.cloned.1.call-start = ((), (), s32[]{:S(2)}) async-start(), calls=%async_computation.17 | async-start | bytes 2359296 | tf_op jit(solution)/shard_map/all_gather | solution.py:75
  9.4 174.3 %all-gather.28.cloned.1.call-start = ((), (), s32[]{:S(2)}) async-start(), calls=%async_computation.19 | async-start | bytes 2621440 | tf_op jit(solution)/shard_map/all_gather | solution.py:120
  25.6 7.5 copy-start.43
  27.3 34.6 %copy-start.41 = (f32[2,384]{1,0:T(2,128)}, f32[2,384]{1,0:T(2,128)S(1)}, u32[]{:S(2)}) copy-start(f32[2,384]{1,0:T(2,128)S(1)} %broadcast_multiply_fusion) | copy-start | bytes 9220
  29.3 32.7 %copy-start.47 = (f32[2,384]{1,0:T(2,128)}, f32[2,384]{1,0:T(2,128)S(1)}, u32[]{:S(2)}) copy-start(f32[2,384]{1,0:T(2,128)S(1)} %fusion.38) | copy-start | bytes 9220
  29.3 32.6 %copy-start.45 = (f32[2,384]{1,0:T(2,128)}, f32[2,384]{1,0:T(2,128)S(1)}, u32[]{:S(2)}) copy-start(f32[2,384]{1,0:T(2,128)S(1)} %fusion.92) | copy-start | bytes 9220
  71.3 137.3 %all-gather.30.cloned.1.call-start = ((), (), s32[]{:S(2)}) async-start(), calls=%async_computation.20 | async-start | bytes 2621440 | tf_op jit(solution)/shard_map/all_gather | solution.py:121
  71.9 161.6 %all-gather.32.cloned.1.call-start = ((), (), s32[]{:S(2)}) async-start(), calls=%async_computation.21 | async-start | bytes 2621440 | tf_op jit(solution)/shard_map/all_gather | solution.py:122
  72.4 185.7 %all-gather.18.cloned.1.call-start = ((), (), s32[]{:S(2)}) async-start(), calls=%async_computation.14 | async-start | bytes 2621440 | tf_op jit(solution)/shard_map/all_gather | solution.py:123
  111.9 22.5 copy-start.56
  113.1 169.9 %all-gather.20.cloned.1.call-start = ((), (), s32[]{:S(2)}) async-start(), calls=%async_computation.15 | async-start | bytes 2621440 | tf_op jit(solution)/shard_map/all_gather | solution.py:124
  113.8 193.9 %all-gather.22.cloned.1.call-start = ((), (), s32[]{:S(2)}) async-start(), calls=%async_computation.16 | async-start | bytes 2621440 | tf_op jit(solution)/shard_map/all_gather | solution.py:125
  114.6 242.0 %all-gather.34.cloned.1.call-start = ((), (), s32[]{:S(2)}) async-start(), calls=%async_computation.22 | async-start | bytes 2359296 | tf_op jit(solution)/shard_map/all_gather | solution.py:78
  115.2 366.5 %all-gather.36.cloned.1.call-start = ((), (), s32[]{:S(2)}) async-start(), calls=%async_computation.23 | async-start | bytes 9437184 | tf_op jit(solution)/shard_map/all_gather | solution.py:79
  115.9 490.9 %all-gather.38.cloned.1.call-start = ((), (), s32[]{:S(2)}) async-start(), calls=%async_computation.24 | async-start | bytes 9437184 | tf_op jit(solution)/shard_map/all_gather | solution.py:80
  116.5 609.5 %reduce-scatter.20.cloned.1.call-start = ((), (), s32[]{:S(2)}) async-start(), calls=%async_computation.29 | async-start | bytes 5242880 | tf_op jit(solution)/shard_map/reduce_scatter | solution.py:241
  135.4 172.3 %copy-start.9 = (pred[2,128,1536]{2,1,0:T(8,128)(4,1)}, pred[2,128,1536]{2,1,0:T(8,128)(4,1)S(1)}, u32[]{:S(2)}) copy-start(pred[2,128,1536]{2,1,0:T(8,128)(4,1)S(1)} %pad_add_fusion) | copy-start | bytes 1179652
  161.7 75.3 %copy-start.14 = (bf16[2,128,8,128]{3,1,2,0:T(8,128)(2,1)}, bf16[2,128,8,128]{3,1,2,0:T(8,128)(2,1)S(1)}, u32[]{:S(2)}) copy-start(bf16[2,128,8,128]{3,1,2,0:T(8,128)(2,1)S(1)} %fusion.84) | copy-start | bytes 1572868
  316.4 172.3 %copy-start.25 = (bf16[2,8,128,128]{3,2,1,0:T(8,128)(2,1)}, bf16[2,8,128,128]{3,2,1,0:T(8,128)(2,1)S(1)}, u32[]{:S(2)}) copy-start(bf16[2,8,128,128]{3,2,1,0:T(8,128)(2,1)S(1)} %fusion.80) | copy-start | bytes 1572868
  490.7 116.1 %copy-start.21 = (bf16[2,128,1024]{2,1,0:T(8,128)(2,1)S(1)}, bf16[2,128,1024]{2,1,0:T(8,128)(2,1)}, u32[]{:S(2)}) copy-start(bf16[2,128,1024]{2,1,0:T(8,128)(2,1)} %param.32) | copy-start | bytes 1572868
  657.4 92.9 %reduce-scatter.22.cloned.1.call-start = ((), (), s32[]{:S(2)}) async-start(), calls=%async_computation.30 | async-start | bytes 5242880 | tf_op jit(solution)/shard_map/reduce_scatter | solution.py:242
  662.9 134.4 %reduce-scatter.24.cloned.1.call-start = ((), (), s32[]{:S(2)}) async-start(), calls=%async_computation.31 | async-start | bytes 5242880 | tf_op jit(solution)/shard_map/reduce_scatter | solution.py:245
  668.4 175.9 %reduce-scatter.14.cloned.1.call-start = ((), (), s32[]{:S(2)}) async-start(), calls=%async_computation.26 | async-start | bytes 5242880 | tf_op jit(solution)/shard_map/reduce_scatter | solution.py:238
  680.2 9.5 copy-start.15
  706.0 185.3 %reduce-scatter.16.cloned.1.call-start = ((), (), s32[]{:S(2)}) async-start(), calls=%async_computation.27 | async-start | bytes 5242880 | tf_op jit(solution)/shard_map/reduce_scatter | solution.py:239
  706.5 231.8 %reduce-scatter.18.cloned.1.call-start = ((), (), s32[]{:S(2)}) async-start(), calls=%async_computation.28 | async-start | bytes 5242880 | tf_op jit(solution)/shard_map/reduce_scatter | solution.py:240
  707.1 321.7 %reduce-scatter.26.cloned.1.call-start = ((), (), s32[]{:S(2)}) async-start(), calls=%async_computation.32 | async-start | bytes 4718592 | tf_op jit(solution)/shard_map/reduce_scatter | solution.py:282
  721.4 399.0 %reduce-scatter.32.cloned.1.call-start = ((), (), s32[]{:S(2)}) async-start(), calls=%async_computation.35 | async-start | bytes 4718592 | tf_op jit(solution)/shard_map/reduce_scatter | solution.py:285
  725.5 486.4 %reduce-scatter.30.cloned.1.call-start = ((), (), s32[]{:S(2)}) async-start(), calls=%async_computation.34 | async-start | bytes 4718592 | tf_op jit(solution)/shard_map/reduce_scatter | solution.py:284
  804.5 499.2 %reduce-scatter.28.cloned.1.call-start = ((), (), s32[]{:S(2)}) async-start(), calls=%async_computation.33 | async-start | bytes 4718592 | tf_op jit(solution)/shard_map/reduce_scatter | solution.py:283
  963.8 624.8 %reduce-scatter.38.cloned.1.call-start = ((), (), s32[]{:S(2)}) async-start(), calls=%async_computation.38 | async-start | bytes 18874368 | tf_op jit(solution)/shard_map/reduce_scatter | solution.py:288
  964.8 3.5 collective-permute-start
  966.7 3.4 collective-permute-start.1
  981.7 892.7 %reduce-scatter.34.cloned.1.call-start = ((), (), s32[]{:S(2)}) async-start(), calls=%async_computation.36 | async-start | bytes 18874368 | tf_op jit(solution)/shard_map/reduce_scatter | solution.py:286
  991.9 1168.1 %reduce-scatter.36.cloned.1.call-start = ((), (), s32[]{:S(2)}) async-start(), calls=%async_computation.37 | async-start | bytes 18874368 | tf_op jit(solution)/shard_map/reduce_scatter | solution.py:287
  1002.8 1282.4 %all-gather.40.cloned.1.call-start = ((), (), s32[]{:S(2)}) async-start(), calls=%async_computation.25 | async-start | bytes 9437184 | tf_op jit(solution)/shard_map/all_gather | solution.py:81
  1003.4 1441.4 %all-reduce.7.cloned.1.call-start = ((), (), s32[]{:S(2)}) async-start(), calls=%async_computation.39 | async-start | bytes 16777216 | tf_op jit(solution)/shard_map/psum | solution.py:292
  2159.9 125.2 %copy-start.37 = (bf16[2,64,1024]{2,1,0:T(8,128)(2,1)S(1)}, bf16[2,64,1024]{2,1,0:T(8,128)(2,1)}, u32[]{:S(2)}) copy-start(bf16[2,64,1024]{2,1,0:T(8,128)(2,1)} %slice.133) | copy-start | bytes 786436
  2304.0 20.3 copy-start.48
  2324.3 10.5 copy-start.17
  2324.3 10.5 copy-start.23
  2324.3 10.5 copy-start.50
  (39 other events, 129.7 us)
Sparse Core Ops, SparseCore 0:
  10.2 47.8 all-gather.25
  60.2 47.7 all-gather.15
  110.1 47.7 all-gather.23
  159.9 23.7 all-gather.27
  185.7 22.8 all-gather.29
  210.6 22.8 all-gather.31
  235.6 22.5 all-gather.17
  260.3 22.5 all-gather.19
  285.1 22.5 all-gather.21
  309.7 46.8 all-gather.33
  358.7 122.9 all-gather.35
  483.7 123.1 all-gather.37
  657.5 45.6 reduce-scatter.19
  705.7 44.5 reduce-scatter.21
  752.7 44.5 reduce-scatter.23
  799.8 44.5 reduce-scatter.13
  846.7 44.5 reduce-scatter.15
  893.8 44.5 reduce-scatter.17
  942.0 86.8 reduce-scatter.25
  1032.8 87.6 reduce-scatter.31
  1124.1 87.8 reduce-scatter.29
  1216.0 87.6 reduce-scatter.27
  1307.5 281.0 reduce-scatter.37
  1592.7 281.6 reduce-scatter.33
  1878.2 281.6 reduce-scatter.35
  2162.2 122.8 all-gather.39
  2288.5 156.2 all-reduce.6
where the time goes:
time: 2470 us; the launch traced here: 2460 us
  waiting for transfers between devices  2070 us (84%)
  matrix products  151 us (6%)
  local copies, waits for them, and re-layouts  88.4 us (4%)
  other arithmetic  73 us (3%)
  blocking collectives  58.4 us (2%)
    reduce_scatter x1, waiting for transfers between devices, per_device(): lax.psum_scatter(up_grad, 'stream', scatter_dimension=0, tiled=True)  286 us
    reduce_scatter x1, waiting for transfers between devices, per_device(): lax.psum_scatter(down_grad, 'stream', scatter_dimension=0, tiled=True)  286 us
    reduce_scatter x1, waiting for transfers between devices, per_device(): lax.psum_scatter(conv_grad, 'stream', scatter_dimension=1, tiled=True)  285 us
    all_gather x1, waiting for transfers between devices, per_device(): lax.all_gather(conv_weight, 'stream', axis=1, tiled=True)  125 us
    all_gather x1, waiting for transfers between devices, per_device(): lax.all_gather(up_weight, 'stream', axis=0, tiled=True)  122 us
    psum x1, waiting for transfers between devices, per_device(): lax.psum((owned_part[0], owned_part[1], owned_part[2], owned_part[3], own...  107 us
    all_gather x1, waiting for transfers between devices, per_device(): lax.all_gather(down_weight, 'stream', axis=0, tiled=True)  95.4 us
    reduce_scatter x1, waiting for transfers between devices, per_device(): lax.psum_scatter(key_grad, 'stream', scatter_dimension=0, tiled=True)  91.7 us
  transfers between devices with their start and end apart: 29, of which 27 were waited for; matrix products, arithmetic and copies ran while one was open for 10% of the time, Pallas kernels for 0%

commit v1 on v0

v1 whole, which is shorter than its diff:
```python
import jax
import jax.numpy as jnp
from jax import lax
from jax.sharding import PartitionSpec as P

HEAD_DIM = 128
BF = jnp.bfloat16
F32 = jnp.float32


def layer_norm(rows):
    center = rows - jnp.mean(rows, axis=-1, keepdims=True)
    spread = jnp.mean(center * center, axis=-1, keepdims=True)
    inv = lax.rsqrt(spread + 1e-05)
    return center * inv, inv


def norm_back(grad, unit, inv, gain):
    c = grad * gain
    return inv * (
        c
        - jnp.mean(c, axis=-1, keepdims=True)
        - unit * jnp.mean(c * unit, axis=-1, keepdims=True)
    )


def rotate(tensor, places, sign):
    half = HEAD_DIM // 2
    frequency = 10000.0 ** (-jnp.arange(half).astype(F32) * 2.0 / HEAD_DIM)
    angles = places[:, None] * frequency[None, :]
    cosine = jnp.cos(angles)[:, None, :]
    sines = sign * jnp.sin(angles)[:, None, :]
    a = tensor[..., :half]
    b = tensor[..., half:]
    return jnp.concatenate([a * cosine - b * sines, a * sines + b * cosine], axis=-1)


def mm(a, b):
    return jnp.dot(a, b, preferred_element_type=F32)


def mmt(a, b):
    return lax.dot_general(a, b, (((a.ndim - 1,), (1,)), ((), ())), preferred_element_type=F32)


def tmm(a, b):
    dims = tuple(range(a.ndim - 1))
    return lax.dot_general(a, b, ((dims, dims), ((), ())), preferred_element_type=F32)


def per_device(
    hidden,
    memory,
    compressed,
    reset_flag,
    boundary,
    query_weight,
    key_weight,
    value_weight,
    output_weight,
    up_weight,
    down_weight,
    conv_weight,
    attn_gain,
    ffn_gain,
    grad_out,
    grad_fresh,
):
    groups = lax.axis_size("stream")
    parts = lax.axis_size("tm")
    rank = lax.axis_index("tm")
    streams, seg_rows, width = hidden.shape
    own = query_weight.shape[0]
    cols = width // parts
    heads = cols // HEAD_DIM
    ff_rows = down_weight.shape[0] // parts
    seg = seg_rows * parts
    cmem = compressed.shape[1] * parts
    mem = memory.shape[1] * parts
    front = cmem + mem

    def col(w):
        return lax.dynamic_slice_in_dim(w, rank * cols, cols, axis=w.ndim - 1)

    gains = lax.all_gather(jnp.stack([attn_gain, ffn_gain]), "stream", axis=1, tiled=True)
    gain_a = gains[0].astype(F32)
    gain_f = gains[1].astype(F32)
    near = jnp.concatenate(
        [col(query_weight), col(key_weight), col(value_weight), output_weight], axis=1
    )
    up_own = lax.dynamic_index_in_dim(
        up_weight.reshape(own, groups, parts, ff_rows), rank, 2, keepdims=False
    ).reshape(own, groups * ff_rows)
    down_own = lax.dynamic_slice_in_dim(down_weight, rank * ff_rows, ff_rows, 0)
    conv_own = col(conv_weight)
    taps = conv_own.shape[0]
    near_full = lax.all_gather(near, "stream", axis=0, tiled=True)
    wq = near_full[:, :cols]
    wk = near_full[:, cols : 2 * cols]
    wv = near_full[:, 2 * cols : 3 * cols]
    wo = near_full[:, 3 * cols :]
    up = lax.all_gather(up_own, "stream", axis=0, tiled=True)
    down = lax.all_gather(down_own, "stream", axis=0, tiled=True)
    conv = lax.all_gather(conv_own, "stream", axis=1, tiled=True)

    context = jnp.concatenate(
        [
            lax.all_gather(compressed, "tm", axis=1, tiled=True),
            lax.all_gather(memory, "tm", axis=1, tiled=True),
            lax.all_gather(hidden, "tm", axis=1, tiled=True),
        ],
        axis=1,
    )
    unit, _ = layer_norm(context.astype(F32))
    normed = (unit * gain_a).astype(BF)
    keys_n = front + seg
    places = jnp.arange(keys_n).astype(F32)
    scale = HEAD_DIM ** (-0.5)
    q = (
        rotate(mm(normed[:, front:], wq).reshape(streams, seg, heads, HEAD_DIM), places[front:], 1.0)
        * scale
    ).astype(BF)
    k = rotate(mm(normed, wk).reshape(streams, keys_n, heads, HEAD_DIM), places, 1.0).astype(BF)
    v = mm(normed, wv).astype(BF).reshape(streams, keys_n, heads, HEAD_DIM)
    documents = jnp.cumsum(boundary, axis=1)
    memory_ok = (reset_flag[:, None] == 0) & (documents == 0)
    spots = jnp.arange(seg)
    local_ok = (spots[None, None, :] <= spots[None, :, None]) & (
        documents[:, None, :] == documents[:, :, None]
    )
    visible = jnp.concatenate(
        [jnp.broadcast_to(memory_ok[:, :, None], (streams, seg, front)), local_ok], axis=2
    )
    scores = jnp.einsum("sqhd,skhd->shqk", q, k, preferred_element_type=F32)
    scores = jnp.where(visible[:, None], scores, -1e30)
    row_max = jnp.max(scores, axis=-1, keepdims=True)
    shifted = jnp.exp(scores - row_max)
    probs = shifted / jnp.sum(shifted, axis=-1, keepdims=True)
    probs_low = probs.astype(BF)
    attended = jnp.einsum("shqk,skhd->sqhd", probs_low, v, preferred_element_type=F32)
    attended = attended.reshape(streams, seg, cols).astype(BF)
    attended_rows = lax.all_to_all(attended, "tm", split_axis=1, concat_axis=2, tiled=True)
    middle = hidden.astype(F32) + mm(attended_rows, wo)
    unit_f, inv_f = layer_norm(middle)
    nf_rows = (unit_f * gain_f).astype(BF)
    nf = lax.all_gather(nf_rows, "tm", axis=1, tiled=True)
    preact = mm(nf, up)
    activated, gelu_back = jax.vjp(lambda t: jax.nn.gelu(t, approximate=False), preact)
    act = activated.astype(BF)
    down_part = mm(act, down).astype(BF)
    layer_out = (
        middle + lax.psum_scatter(down_part, "tm", scatter_dimension=1, tiled=True).astype(F32)
    ).astype(BF)

    memory_full = context[:, cmem:front]
    padded = jnp.pad(memory_full, ((0, 0), (1, 1), (0, 0)))
    stacked = jnp.concatenate([padded[:, o : o + mem : 2] for o in range(taps)], axis=2)
    fresh = mm(stacked, conv.reshape(taps * width, cols)).astype(BF)
    fresh_memory = lax.all_to_all(fresh, "tm", split_axis=1, concat_axis=2, tiled=True)
    grad_fresh_c = lax.all_to_all(grad_fresh, "tm", split_axis=2, concat_axis=1, tiled=True)
    conv_grad = (
        tmm(stacked, grad_fresh_c)
        .astype(BF)
        .reshape(taps, width, cols)
        .transpose(1, 0, 2)
        .reshape(width, taps * cols)
    )

    go = lax.all_gather(grad_out, "tm", axis=1, tiled=True)
    grad_act = mmt(go, down)
    down_grad = tmm(act, go).astype(BF)
    grad_pre = gelu_back(grad_act)[0].astype(BF)
    up_grad = tmm(nf, grad_pre).astype(BF)
    gnf_part = mmt(grad_pre, up).astype(BF)
    gnf = lax.psum_scatter(gnf_part, "tm", scatter_dimension=1, tiled=True).astype(F32)
    grad_middle = grad_out.astype(F32) + norm_back(gnf, unit_f, inv_f, gain_f)
    gm_low = grad_middle.astype(BF)
    output_part = tmm(attended_rows, gm_low).astype(BF)
    output_grad = lax.psum_scatter(output_part, "tm", scatter_dimension=1, tiled=True)
    ga_rows = mmt(gm_low, wo).astype(BF)
    ga = lax.all_to_all(ga_rows, "tm", split_axis=2, concat_axis=1, tiled=True)
    ga = ga.reshape(streams, seg, heads, HEAD_DIM)
    far = lax.psum_scatter(
        jnp.concatenate([up_grad, down_grad, conv_grad], axis=1),
        "stream",
        scatter_dimension=0,
        tiled=True,
    )

    grad_probs = jnp.einsum("sqhd,skhd->shqk", ga, v, preferred_element_type=F32)
    inner = jnp.sum(probs * grad_probs, axis=-1, keepdims=True)
    gs = (probs * (grad_probs - inner)).astype(BF)
    gq = jnp.einsum("shqk,skhd->sqhd", gs, k, preferred_element_type=F32)
    gk = jnp.einsum("shqk,sqhd->skhd", gs, q, preferred_element_type=F32)
    gv = jnp.einsum("shqk,sqhd->skhd", probs_low, ga, preferred_element_type=F32)
    gq = (rotate(gq, places[front:], -1.0) * scale).astype(BF).reshape(streams, seg, cols)
    gk = rotate(gk, places, -1.0).astype(BF).reshape(streams, keys_n, cols)
    gv = gv.astype(BF).reshape(streams, keys_n, cols)
    query_grad = tmm(normed[:, front:], gq).astype(BF)
    key_grad = tmm(normed, gk).astype(BF)
    value_grad = tmm(normed, gv).astype(BF)
    gn_part = (mmt(gq, wq) + mmt(gk[:, front:], wk) + mmt(gv[:, front:], wv)).astype(BF)
    gn = lax.psum_scatter(gn_part, "tm", scatter_dimension=1, tiled=True).astype(F32)
    unit_h, inv_h = layer_norm(hidden.astype(F32))
    grad_input = grad_middle + norm_back(gn, unit_h, inv_h, gain_a)
    close = lax.psum_scatter(
        jnp.concatenate([query_grad, key_grad, value_grad, output_grad], axis=1),
        "stream",
        scatter_dimension=0,
        tiled=True,
    )
    far_all = lax.all_gather(far, "tm", axis=0).astype(F32)
    close_all = lax.all_gather(close, "tm", axis=0).astype(F32)

    def spread_cols(t):
        return t.transpose(1, 0, 2).reshape(own, width)

    query_grad = spread_cols(close_all[:, :, :cols])
    key_grad = spread_cols(close_all[:, :, cols : 2 * cols])
    value_grad = spread_cols(close_all[:, :, 2 * cols : 3 * cols])
    output_grad = spread_cols(close_all[:, :, 3 * cols :])
    ff = groups * ff_rows
    up_grad = (
        far_all[:, :, :ff]
        .reshape(parts, own, groups, ff_rows)
        .transpose(1, 2, 0, 3)
        .reshape(own, ff * parts)
    )
    down_grad = far_all[:, :, ff : ff + width].reshape(parts * ff_rows, width)
    conv_grad = (
        far_all[:, :, ff + width :]
        .reshape(parts, own, taps, cols)
        .transpose(2, 1, 0, 3)
        .reshape(taps, own, width)
    )
    wide = lambda w: w.astype(F32)
    attn_gain_grad = jnp.sum(
        wide(query_weight) * query_grad
        + wide(key_weight) * key_grad
        + wide(value_weight) * value_grad,
        axis=1,
    ) / wide(attn_gain)
    ffn_gain_grad = jnp.sum(wide(up_weight) * up_grad, axis=1) / wide(ffn_gain)
    return (
        layer_out,
        fresh_memory,
        grad_input,
        query_grad,
        key_grad,
        value_grad,
        output_grad,
        up_grad,
        down_grad,
        conv_grad,
        attn_gain_grad,
        ffn_gain_grad,
    )


def solution(mesh):
    act = P("stream", "tm", None)
    row = P("stream", None)
    in_specs = (act, act, act, P("stream"), row) + (row,) * 6 + (
        P(None, "stream", None),
        P("stream"),
        P("stream"),
        act,
        act,
    )
    out_specs = (act, act, act) + (row,) * 6 + (
        P(None, "stream", None),
        P("stream"),
        P("stream"),
    )
    return jax.shard_map(
        per_device, mesh=mesh, in_specs=in_specs, out_specs=out_specs, check_vma=False
    )
```

time: 2470 us -> 855 us (0.35)
  waiting for transfers between devices: 2070 us -> 453 us
  local copies, waits for them, and re-layouts: 88.4 us -> 129 us
  matrix products: 151 us -> 121 us
    reduce_scatter x13 -> x4, waiting for transfers between devices: 1360 us -> 79.5 us  [the longest x1 33.2 us: per_device(): lax.psum_scatter(down_part, 'tm', scatter_dimension=1, tiled=True)]
    all_gather x13 -> x11, waiting for transfers between devices: 598 us -> 254 us  [the longest x1 52.7 us: per_device(): near_full = lax.all_gather(near, 'stream', axis=0, tiled=True)]
    psum x1 -> x0, waiting for transfers between devices: 107 us -> none  [per_device(): lax.psum((owned_part[0], owned_part[1], owned_part[2], owned_part[3], own...]
    unnamed x27 -> x19, waiting for transfers between devices: 8.04 us -> 108 us
    dot_general x26 -> x25, matrix products: 151 us -> 109 us  [the longest x7 30.2 us: tmm(): lax.dot_general(a, b, ((dims, dims), ((), ())), preferred_element_type=F32)]
    unnamed x134 -> x127, local copies, waits for them, and re-layouts: 49.9 us -> 40.8 us
  transfers between devices with their start and end apart: 29 -> 19, of which waited for: 27 -> 15; matrix products, arithmetic and copies ran while one was open for 10% -> 32% of each run, Pallas kernels for 0% -> 0%
where the time goes in v1:
time: 855 us; the launch traced here: 848 us
  waiting for transfers between devices  453 us (53%)
  local copies, waits for them, and re-layouts  129 us (15%)
  matrix products  121 us (14%)
  other arithmetic  82.6 us (10%)
  blocking collectives  37.7 us (4%)
  between operations  15.2 us (2%)
    unnamed x19, waiting for transfers between devices  108 us
    all_gather x1, waiting for transfers between devices, per_device(): near_full = lax.all_gather(near, 'stream', axis=0, tiled=True)  52.7 us
    all_gather x1, waiting for transfers between devices, per_device(): down = lax.all_gather(down_own, 'stream', axis=0, tiled=True)  49.6 us
    all_gather x1, waiting for transfers between devices, per_device(): conv = lax.all_gather(conv_own, 'stream', axis=1, tiled=True)  47.9 us
    unnamed x127, local copies, waits for them, and re-layouts  40.8 us
    reduce_scatter x1, waiting for transfers between devices, per_device(): lax.psum_scatter(down_part, 'tm', scatter_dimension=1, tiled=True)  33.2 us
    slice x4, local copies, waits for them, and re-layouts, per_device(): padded[:, o:o + mem:2]  30.7 us
    dot_general x7, matrix products, tmm(): lax.dot_general(a, b, ((dims, dims), ((), ())), preferred_element_type=F32)  30.2 us
  transfers between devices with their start and end apart: 19, of which 15 were waited for; matrix products, arithmetic and copies ran while one was open for 32% of the time, Pallas kernels for 0%

profile of v1, /device:TPU:26, one launch (start us, length us, event | category | flops | bytes accessed | tf_op | source)
XLA Modules:
  0.0 847.7 jit_solution(11433112208368553394)
XLA Ops:
  16.9 16.1 %all_gather.45 = bf16[2,1024]{1,0:T(2,128)(2,1)S(1)} all-gather(bf16[2,128]{1,0:T(2,128)(2,1)S(1)} %pad_maximum_fusion.9), channel_id=1, replica_groups=mesh['stream'=8,'tm'=4] {'stream'}, dimensions={1}, use_global_device_ids=true | all-gather | bytes 4608 | tf_op jit(solution)/shard_map/all_gather | solution.py:85
  34.3 4.5 broadcast_multiply_fusion
  42.6 14.9 %all-gather.14.cloned.1.call-done = bf16[2,512,1024]{2,1,0:T(8,128)(2,1)} async-done(((bf16[2,128,1024]{2,1,0:T(8,128)(2,1)}), bf16[2,512,1024]{2,1,0:T(8,128)(2,1)}) %all-gather.14.cloned.1.call-update) | async-done | bytes 2097168 | tf_op jit(solution)/shard_map/all_gather | solution.py:108
  57.5 24.2 %all-gather.18.cloned.1.call-done = bf16[2,512,1024]{2,1,0:T(8,128)(2,1)} async-done(((bf16[2,128,1024]{2,1,0:T(8,128)(2,1)}), bf16[2,512,1024]{2,1,0:T(8,128)(2,1)}) %all-gather.18.cloned.1.call-update) | async-done | bytes 2097168 | tf_op jit(solution)/shard_map/all_gather | solution.py:110
  81.6 4.3 convert_reduce_fusion
  86.0 5.4 fusion.3
  91.4 6.2 fusion.5
  97.7 52.7 %all-gather.20.cloned.1.call-done = bf16[1024,1792]{0,1:T(8,128)(2,1)} async-done(((bf16[128,1792]{0,1:T(8,128)(2,1)}), bf16[1024,1792]{0,1:T(8,128)(2,1)}) %all-gather.20.cloned.1.call-update) | async-done | bytes 3670032 | tf_op jit(solution)/shard_map/all_gather | solution.py:97
  158.6 4.7 fusion.84
  179.5 12.2 %fusion.94 = (f32[2,2,512]{2,1,0:T(2,128)S(1)}, f32[2,2,512,1536]{3,2,1,0:T(8,128)}) fusion(bf16[2,512,2,128]{3,1,2,0:T(8,128)(2,1)} %fusion.74, pred[2,512,1536]{2,1,0:T(8,128)(4,1)} %pad_add_fusion, bf16[2,1536,2,64]{3,1,2,0:T(8,128)(2,1)} %get-tuple-element.21, bf16[2,1536,2,64]{3,1,2,0:T(8,128)(2,1)} %get-tuple-element.20), kind=kOutput, calls=%fused_computation.189 | convolution fusion | flops 817890816 | bytes 16261120 | tf_op jit(solution)/shard_map/sub | solution.py:137
  191.6 4.7 convolution_convert_fusion
  196.3 8.2 fusion.58
  206.6 12.3 %all_to_all.69 = bf16[2,512,256]{2,0,1:T(2,128)(2,1)S(1)} all-to-all(bf16[2,512,256]{2,0,1:T(2,128)(2,1)} %copy.120), channel_id=1, replica_groups=mesh['stream'=8,'tm'=4] {'tm'}, dimensions={1} | all-to-all | bytes 1048576 | tf_op jit(solution)/shard_map/all_to_all | solution.py:142
  229.0 20.8 %all-gather.22.cloned.1.call-done = bf16[2,512,1024]{2,1,0:T(8,128)(2,1)} async-done(((bf16[2,128,1024]{2,1,0:T(8,128)(2,1)}), bf16[2,512,1024]{2,1,0:T(8,128)(2,1)}) %all-gather.22.cloned.1.call-update) | async-done | bytes 2097168 | tf_op jit(solution)/shard_map/all_gather | solution.py:146
  249.8 5.6 fusion.79
  257.5 10.6 %multiply_convert_fusion.1 = (bf16[2,512,1024]{2,1,0:T(8,128)(2,1)}, f32[2,512,1024]{2,1,0:T(8,128)}) fusion(f32[2,512,1024]{2,1,0:T(8,128)S(1)} %get-tuple-element.53, u8[512,1024]{1,0:T(8,128)(4,1)S(1)} %get-tuple-element.13, u8[512,1024]{1,0:T(8,128)(4,1)S(1)} %get-tuple-element.12), kind=kLoop, calls=%fused_computation.43 | loop fusion | flops 73400320 | bytes 11534336 | tf_op jit(solution)/shard_map/convert_element_type | solution.py:149
  268.1 5.9 all-gather.30.cloned.1.call-done
  274.0 49.6 %all-gather.26.cloned.1.call-done = bf16[1024,1024]{1,0:T(8,128)(2,1)} async-done(((bf16[128,1024]{1,0:T(8,128)(2,1)}), bf16[1024,1024]{1,0:T(8,128)(2,1)}) %all-gather.26.cloned.1.call-update) | async-done | bytes 2097168 | tf_op jit(solution)/shard_map/all_gather | solution.py:103
  323.6 8.2 fusion.20
  337.1 6.0 fusion.44
  343.1 26.2 %reduce-scatter.13.cloned.1.call-done = bf16[2,128,1024]{2,1,0:T(8,128)(2,1)} async-done(((bf16[2,512,1024]{2,1,0:T(8,128)(2,1)}), bf16[2,128,1024]{2,1,0:T(8,128)(2,1)}) %reduce-scatter.13.cloned.1.call-update) | async-done | bytes 524304 | tf_op jit(solution)/shard_map/reduce_scatter | solution.py:175
  370.7 33.2 %reduce-scatter.11.cloned.1.call-done = bf16[2,128,1024]{2,1,0:T(8,128)(2,1)} async-done(((bf16[2,512,1024]{2,1,0:T(8,128)(2,1)}), bf16[2,128,1024]{2,1,0:T(8,128)(2,1)}) %reduce-scatter.11.cloned.1.call-update) | async-done | bytes 524304 | tf_op jit(solution)/shard_map/reduce_scatter | solution.py:152
  416.3 5.4 all-to-all-done.2
  422.7 7.4 multiply_reduce_fusion
  430.1 5.9 multiply_convert_fusion
  444.6 5.6 convolution_bitcast_fusion.4
  454.5 5.7 fusion.31
  460.2 6.1 fusion.57
  466.3 5.4 fusion.56
  474.6 4.0 copy.183
  479.4 9.3 %all_to_all.70 = bf16[4,2,16384]{2,1,0:T(2,128)(2,1)} all-to-all(bf16[4,2,16384]{2,1,0:T(2,128)(2,1)S(1)} %reshape.457), channel_id=1, replica_groups=mesh['stream'=8,'tm'=4] {'tm'}, dimensions={0} | all-to-all | bytes 524288 | tf_op jit(solution)/shard_map/all_to_all | solution.py:160
  492.4 9.9 %slice.126 = bf16[2,256,1024]{2,1,0:T(8,128)(2,1)} slice(bf16[2,514,1024]{2,1,0:T(8,128)(2,1)} %pad.4), slice={[0:2:1], [3:514:2], [0:1024:1]} | slice | bytes 2097152 | tf_op jit(solution)/shard_map/slice | solution.py:157
  502.4 9.7 %slice.125 = bf16[2,256,1024]{2,1,0:T(8,128)(2,1)} slice(bf16[2,514,1024]{2,1,0:T(8,128)(2,1)} %pad.4), slice={[0:2:1], [2:514:2], [0:1024:1]} | slice | bytes 2097152 | tf_op jit(solution)/shard_map/slice | solution.py:157
  512.1 5.5 slice.124
  517.6 5.5 slice.123
  523.1 4.8 fusion.13
  531.0 4.9 bitcast_convert_fusion
  538.4 13.7 %pad_maximum_fusion.1 = bf16[1024,3072]{0,1:T(8,128)(2,1)} fusion(bf16[1024,1024]{0,1:T(8,128)(2,1)S(1)} %bitcast.197, bf16[1024,1024]{0,1:T(8,128)(2,1)S(1)} %bitcast_convert_fusion, bf16[1024,1024]{0,1:T(8,128)(2,1)S(1)} %bitcast_convert_fusion.1), kind=kLoop, calls=%fused_computation.15 | loop fusion | flops 18874368 | bytes 12582912 | tf_op jit(solution)/shard_map/concatenate | solution.py:184
  552.1 8.6 %copy.185 = bf16[1024,3072]{1,0:T(8,128)(2,1)} copy(bf16[1024,3072]{0,1:T(8,128)(2,1)} %pad_maximum_fusion.1) | data formatting | bytes 12582912
  571.7 105.4 %reduce-scatter.21.cloned.1.call-done = bf16[128,3072]{1,0:T(8,128)(2,1)} async-done(((bf16[1024,3072]{1,0:T(8,128)(2,1)}), bf16[128,3072]{1,0:T(8,128)(2,1)}) %reduce-scatter.21.cloned.1.call-update) | async-done | bytes 786448
  679.9 47.9 %all-gather.28.cloned.1.call-done = bf16[4,1024,256]{2,1,0:T(8,128)(2,1)} async-done(((bf16[4,128,256]{2,1,0:T(8,128)(2,1)}), bf16[4,1024,256]{2,1,0:T(8,128)(2,1)}) %all-gather.28.cloned.1.call-update) | async-done | bytes 2097168 | tf_op jit(solution)/shard_map/all_gather | solution.py:104
  727.7 3.9 convolution_convert_fusion.1
  736.2 6.0 all-to-all-done.1
  743.3 20.1 %reduce-scatter.15.cloned.1.call-done = bf16[2,128,1024]{2,1,0:T(8,128)(2,1)} async-done(((bf16[2,512,1024]{2,1,0:T(8,128)(2,1)}), bf16[2,128,1024]{2,1,0:T(8,128)(2,1)}) %reduce-scatter.15.cloned.1.call-update) | async-done | bytes 524304 | tf_op jit(solution)/shard_map/reduce_scatter | solution.py:203
  767.2 15.0 %all-gather.32.cloned.1.call-done = bf16[512,1024]{0,1:T(8,128)(2,1)} async-done(((bf16[128,1024]{0,1:T(8,128)(2,1)}), bf16[512,1024]{0,1:T(8,128)(2,1)}) %all-gather.32.cloned.1.call-update) | async-done | bytes 1048592 | tf_op jit(solution)/shard_map/all_gather | solution.py:213
  790.0 23.1 %all-gather.34.cloned.1.call-done = bf16[512,3072]{0,1:T(8,128)(2,1)} async-done(((bf16[128,3072]{0,1:T(8,128)(2,1)}), bf16[512,3072]{0,1:T(8,128)(2,1)}) %all-gather.34.cloned.1.call-update) | async-done | bytes 3145744 | tf_op jit(solution)/shard_map/all_gather | solution.py:212
  813.2 6.5 reshape.431
  819.7 5.8 fusion.91
  (258 shorter events, 144.6 us)
Async XLA Ops:
  7.2 220.5 %copy-start = (bf16[512,1024]{1,0:T(8,128)(2,1)S(1)}, bf16[512,1024]{1,0:T(8,128)(2,1)}, u32[]{:S(2)}) copy-start(bf16[512,1024]{1,0:T(8,128)(2,1)} %param.26) | copy-start | bytes 3145732
  7.2 6.4 copy-start.18
  7.2 9.7 %copy-start.45 = (s32[2]{0:T(128)S(1)}, s32[2]{0:T(128)}, u32[]{:S(2)}) copy-start(s32[2]{0:T(128)} %param.19) | copy-start | bytes 28
  7.2 9.7 %copy-start.46 = (bf16[128]{0:T(256)(128)(2,1)S(1)}, bf16[128]{0:T(256)(128)(2,1)}, u32[]{:S(2)}) copy-start(bf16[128]{0:T(256)(128)(2,1)} %param.28) | copy-start | bytes 772
  7.2 9.7 %copy-start.48 = (bf16[128]{0:T(256)(128)(2,1)S(1)}, bf16[128]{0:T(256)(128)(2,1)}, u32[]{:S(2)}) copy-start(bf16[128]{0:T(256)(128)(2,1)} %param.29) | copy-start | bytes 772
  7.2 25.8 %copy-start.42 = (s32[2,512]{1,0:T(2,128)S(1)}, s32[2,512]{1,0:T(2,128)}, u32[]{:S(2)}) copy-start(s32[2,512]{1,0:T(2,128)} %param.20) | copy-start | bytes 12292
  7.3 35.3 %all-gather.16.cloned.1.call-start = ((), (), s32[]{:S(2)}) async-start(), calls=%async_computation.11 | async-start | bytes 2621440 | tf_op jit(solution)/shard_map/all_gather | solution.py:109
  8.0 49.5 %all-gather.14.cloned.1.call-start = ((), (), s32[]{:S(2)}) async-start(), calls=%async_computation.10 | async-start | bytes 2621440 | tf_op jit(solution)/shard_map/all_gather | solution.py:108
  8.7 72.9 %all-gather.18.cloned.1.call-start = ((), (), s32[]{:S(2)}) async-start(), calls=%async_computation.12 | async-start | bytes 2621440 | tf_op jit(solution)/shard_map/all_gather | solution.py:110
  9.5 140.9 %all-gather.20.cloned.1.call-start = ((), (), s32[]{:S(2)}) async-start(), calls=%async_computation.13 | async-start | bytes 4128768 | tf_op jit(solution)/shard_map/all_gather | solution.py:97
  13.6 215.4 %all-gather.24.cloned.1.call-start = ((), (), s32[]{:S(2)}) async-start(), calls=%async_computation.15 | async-start | bytes 2359296 | tf_op jit(solution)/shard_map/all_gather | solution.py:102
  16.7 233.1 %all-gather.22.cloned.1.call-start = ((), (), s32[]{:S(2)}) async-start(), calls=%async_computation.14 | async-start | bytes 2621440 | tf_op jit(solution)/shard_map/all_gather | solution.py:146
  34.2 57.2 %copy-start.40 = (f32[1,1024]{1,0:T(1,128)}, f32[1,1024]{1,0:T(1,128)S(1)}, u32[]{:S(2)}) copy-start(f32[1,1024]{1,0:T(1,128)S(1)} %get-tuple-element.45) | copy-start | bytes 12292
  42.6 43.4 %copy-start.2 = (bf16[2,512,1024]{2,1,0:T(8,128)(2,1)S(1)}, bf16[2,512,1024]{2,1,0:T(8,128)(2,1)}, u32[]{:S(2)}) copy-start(bf16[2,512,1024]{2,1,0:T(8,128)(2,1)} %all-gather.16.cloned.1.call-done) | copy-start | bytes 6291460
  196.3 8.2 copy-start.50
  226.9 47.1 %all-gather.30.cloned.1.call-start = ((), (), s32[]{:S(2)}) async-start(), calls=%async_computation.19 | async-start | bytes 2621440 | tf_op jit(solution)/shard_map/all_gather | solution.py:169
  227.7 95.9 %all-gather.26.cloned.1.call-start = ((), (), s32[]{:S(2)}) async-start(), calls=%async_computation.16 | async-start | bytes 2359296 | tf_op jit(solution)/shard_map/all_gather | solution.py:103
  228.5 140.8 %reduce-scatter.13.cloned.1.call-start = ((), (), s32[]{:S(2)}) async-start(), calls=%async_computation.20 | async-start | bytes 2621440 | tf_op jit(solution)/shard_map/reduce_scatter | solution.py:175
  323.6 9.5 %copy-start.44 = (bf16[1024,1024]{1,0:T(8,128)(2,1)S(1)}, bf16[1024,1024]{1,0:T(8,128)(2,1)}, u32[]{:S(2)}) copy-start(bf16[1024,1024]{1,0:T(8,128)(2,1)} %all-gather.24.cloned.1.call-done) | copy-start | bytes 6291460
  336.9 67.1 %reduce-scatter.11.cloned.1.call-start = ((), (), s32[]{:S(2)}) async-start(), calls=%async_computation.17 | async-start | bytes 2621440 | tf_op jit(solution)/shard_map/reduce_scatter | solution.py:152
  337.1 32.3 %copy-start.8 = (f32[2,128,1024]{2,1,0:T(8,128)S(1)}, f32[2,128,1024]{2,1,0:T(8,128)}, u32[]{:S(2)}) copy-start(f32[2,128,1024]{2,1,0:T(8,128)} %copy-done.7) | copy-start | bytes 3145732
  406.6 6.3 copy-start.23
  409.4 12.3 %all-to-all-start.2 = ((bf16[2,128,1024]{1,0,2:T(2,128)(2,1)}), bf16[2,128,1024]{1,0,2:T(2,128)(2,1)S(1)}, u32[]{:S(2)}, u32[]{:S(2)}) async-start(bf16[2,128,1024]{1,0,2:T(2,128)(2,1)} %copy.128), calls=%async_computation.4 | async-start | bytes 1048576 | tf_op jit(solution)/shard_map/all_to_all | solution.py:181
  412.9 58.9 %reduce-scatter.17.cloned.1.call-start = ((), (), s32[]{:S(2)}) async-start(), calls=%async_computation.22 | async-start | bytes 2621440 | tf_op jit(solution)/shard_map/reduce_scatter | solution.py:179
  416.3 153.4 %reduce-scatter.19.cloned.1.call-start = ((), (), s32[]{:S(2)}) async-start(), calls=%async_computation.25 | async-start | bytes 2359296
  422.7 7.5 copy-start.32
  430.1 5.9 copy-start.22
  444.6 5.7 copy-start.30
  460.2 6.1 copy-start.39
  460.2 6.1 copy-start.21
  466.3 5.4 copy-start.34
  478.6 198.5 %reduce-scatter.21.cloned.1.call-start = ((), (), s32[]{:S(2)}) async-start(), calls=%async_computation.26 | async-start | bytes 7077888
  492.4 19.6 %copy-start.6 = (bf16[2,514,1024]{2,1,0:T(8,128)(2,1)S(1)}, bf16[2,514,1024]{2,1,0:T(8,128)(2,1)}, u32[]{:S(2)}) copy-start(bf16[2,514,1024]{2,1,0:T(8,128)(2,1)} %pad.4) | copy-start | bytes 6316036
  531.0 5.0 copy-start.43
  531.0 5.0 copy-start.52
  560.8 166.9 %all-gather.28.cloned.1.call-start = ((), (), s32[]{:S(2)}) async-start(), calls=%async_computation.18 | async-start | bytes 2359296 | tf_op jit(solution)/shard_map/all_gather | solution.py:104
  562.5 200.8 %reduce-scatter.15.cloned.1.call-start = ((), (), s32[]{:S(2)}) async-start(), calls=%async_computation.21 | async-start | bytes 2621440 | tf_op jit(solution)/shard_map/reduce_scatter | solution.py:203
  569.6 109.8 %copy-start.9 = (bf16[2,128,1024]{2,1,0:T(8,128)(2,1)S(1)}, bf16[2,128,1024]{2,1,0:T(8,128)(2,1)}, u32[]{:S(2)}) copy-start(bf16[2,128,1024]{2,1,0:T(8,128)(2,1)} %param.16) | copy-start | bytes 1572868
  569.6 158.2 %copy-start.29 = (bf16[2,256,1024]{2,1,0:T(8,128)(2,1)S(1)}, bf16[2,256,1024]{2,1,0:T(8,128)(2,1)}, u32[]{:S(2)}) copy-start(bf16[2,256,1024]{2,1,0:T(8,128)(2,1)} %slice.126) | copy-start | bytes 3145732
  569.6 212.6 %all-gather.32.cloned.1.call-start = ((), (), s32[]{:S(2)}) async-start(), calls=%async_computation.23 | async-start | bytes 1310720 | tf_op jit(solution)/shard_map/all_gather | solution.py:213
  571.6 241.6 %all-gather.34.cloned.1.call-start = ((), (), s32[]{:S(2)}) async-start(), calls=%async_computation.24 | async-start | bytes 3932160 | tf_op jit(solution)/shard_map/all_gather | solution.py:212
  727.7 35.6 %copy-start.41 = (f32[1,1024]{1,0:T(1,128)S(1)}, f32[1,1024]{1,0:T(1,128)}, u32[]{:S(2)}) copy-start(f32[1,1024]{1,0:T(1,128)} %copy-done.40) | copy-start | bytes 12292
  727.7 37.1 %copy-start.13 = (f32[2,128,1024]{2,1,0:T(8,128)S(1)}, f32[2,128,1024]{2,1,0:T(8,128)}, u32[]{:S(2)}) copy-start(f32[2,128,1024]{2,1,0:T(8,128)} %copy-done.12) | copy-start | bytes 3145732
  732.6 9.6 %all-to-all-start.1 = ((bf16[2,256,256]{2,0,1:T(2,128)(2,1)}), bf16[2,256,256]{2,0,1:T(2,128)(2,1)S(1)}, u32[]{:S(2)}, u32[]{:S(2)}) async-start(bf16[2,256,256]{2,0,1:T(2,128)(2,1)} %copy.124), calls=%async_computation.2 | async-start | bytes 524288 | tf_op jit(solution)/shard_map/all_to_all | solution.py:159
  787.7 32.0 %copy-start.24 = (f32[16,8,4,256]{3,1,2,0:T(8,128)}, f32[16,8,4,256]{3,1,2,0:T(8,128)S(1)}, u32[]{:S(2)}) copy-start(f32[16,8,4,256]{3,1,2,0:T(8,128)S(1)} %copy.201) | copy-start | bytes 1572868
  788.1 31.6 %copy-start.25 = (f32[16,8,4,256]{3,1,2,0:T(8,128)}, f32[16,8,4,256]{3,1,2,0:T(8,128)S(1)}, u32[]{:S(2)}) copy-start(f32[16,8,4,256]{3,1,2,0:T(8,128)S(1)} %copy.200) | copy-start | bytes 1572868
  833.5 7.5 copy-start.1
  836.0 4.4 copy-start.49
  (24 other events, 71.4 us)
Sparse Core Ops, SparseCore 0:
  9.6 23.5 all-gather.15
  34.8 22.5 all-gather.13
  59.0 22.5 all-gather.17
  84.1 66.2 all-gather.19
  152.9 47.8 all-gather.23
  227.0 22.7 all-gather.21
  251.4 22.5 all-gather.29
  276.7 46.8 all-gather.25
  337.0 32.3 reduce-scatter.12
  372.4 31.4 reduce-scatter.10
  416.8 32.8 reduce-scatter.16
  478.7 65.5 reduce-scatter.18
  560.9 116.1 reduce-scatter.20
  680.0 47.7 all-gather.27
  730.8 32.4 reduce-scatter.14
  765.3 16.8 all-gather.31
  784.2 28.9 all-gather.33

commit v2 on v1

v2 whole, which is shorter than its diff:
```python
import functools

import jax
import jax.numpy as jnp
from jax import lax
from jax.experimental import pallas as pl
from jax.experimental.pallas import tpu as pltpu
from jax.sharding import PartitionSpec as P

HEAD_DIM = 128
PARTS = 4
BF = jnp.bfloat16
F32 = jnp.float32
MESH = pl.DeviceIdType.MESH

QKV, WO, UP, DOWN, CONV = range(5)
(T_CTX0, T_CTX1, T_CTX2, T_GO, T_GF, T_WO, T_ATT0, T_ATT1, T_NF0, T_NF1, T_GNF0, T_GNF1) = range(12)
(T_OUT0, T_OUT1, T_GA, T_OP, T_GN0, T_GN1, T_FR) = range(12, 19)
T_COUNT = 19


def dot(a, b, ca=1, cb=0):
    return lax.dot_general(a, b, (((ca,), (cb,)), ((), ())), preferred_element_type=F32)


def loop(n, body):
    def step(i, carry):
        body(i)
        return carry

    lax.fori_loop(0, n, step, 0)


def ds(start, size):
    return pl.ds(pl.multiple_of(start, size), size)


def mean(x):
    return jnp.sum(x, axis=-1, keepdims=True) * (1.0 / x.shape[-1])


def layer_norm(rows):
    center = rows - mean(rows)
    inv = lax.rsqrt(mean(center * center) + 1e-05)
    return center * inv, inv


def norm_back(c, unit, inv):
    return inv * (c - mean(c) - unit * mean(c * unit))


def kernel(
    n_z,
    own,
    hidden,
    memory,
    compressed,
    query_weight,
    key_weight,
    value_weight,
    output_weight,
    up_own,
    down_weight,
    conv_weight,
    grad_out,
    grad_fresh,
    gain_a,
    gain_f,
    cosines,
    sines,
    row_info,
    doc_k,
    layer_out,
    fresh_out,
    grad_input,
    out_q,
    out_k,
    out_v,
    out_o,
    out_up,
    out_down,
    out_conv,
    conv_all,
    unit,
    memraw,
    wqkv,
    wo,
    up,
    down,
    qs,
    kv,
    probs,
    att_own,
    att_rows,
    middle,
    nf,
    go,
    gf,
    act,
    gpre,
    ga,
    gm,
    gm_low,
    gnp,
    d_a,
    y_a,
    d_b,
    y_b,
    d_o,
    y_o,
    l_o,
    l_conv,
    x_qkv,
    x_o,
    x_up,
    x_down,
    x_conv,
    z_qkv,
    z_o,
    z_up,
    z_down,
    z_conv,
    t_v,
    t_q,
    loc,
    tm_s,
    tm_r,
    ag_s,
    ag_r,
    rx_s,
    rx_r,
    rz_s,
    rz_r,
    fin_s,
    fin_r,
):
    st = lax.axis_index("stream")
    r = lax.axis_index("tm")
    z = lax.div(st, 2)
    x = lax.rem(st, 2)
    core = lax.rem(r, 2)
    r1 = r + 1 - 2 * core
    r2 = lax.rem(r + 2, 4)
    r3 = lax.rem(r1 + 2, 4)
    xn = z * 2 + 1 - x
    seg = 512
    col = 256

    def zpeer(dz):
        return lax.rem(z + dz, n_z)

    def zfrom(dz):
        return lax.rem(z + n_z - dz, n_z)

    def load(src, dst, i):
        d = pltpu.make_async_copy(src, dst, loc.at[i])
        d.start()
        return d

    own_rows = ds(st * own, own)
    rcol = ds(r * col, col)
    ld_q = load(query_weight.at[:, rcol], wqkv.at[own_rows, pl.ds(0, col)], 0)
    ld_k = load(key_weight.at[:, rcol], wqkv.at[own_rows, pl.ds(col, col)], 1)
    ld_v = load(value_weight.at[:, rcol], wqkv.at[own_rows, pl.ds(2 * col, col)], 2)
    ld_o = load(output_weight.at[:, rcol], wo.at[own_rows, rcol], 3)
    ld_up = load(up_own, up.at[own_rows], 4)
    ld_dn = load(down_weight.at[ds(r * own, own)], down.at[own_rows], 5)
    ld_cv = [
        load(conv_weight.at[k, :, rcol], conv_all.at[own_rows, pl.ds(k * col, col)], 6 + k)
        for k in range(4)
    ]
    tslot = ds(r * 128, 128)
    ld_c = [
        load(compressed, unit.at[0, :, tslot], 10),
        load(memory, memraw.at[:, :, ds(r * 64, 64)], 11),
        load(hidden, unit.at[2, :, tslot], 12),
        load(hidden, gm_low, 13),
    ]
    ld_go = load(grad_out, go.at[:, tslot], 14)
    ld_gf = load(grad_fresh.at[:, :, rcol], gf.at[:, ds(r * 64, 64)], 15)

    barrier = pltpu.get_barrier_semaphore()
    for peer in (r1, r2, r3):
        pl.semaphore_signal(barrier, 1, device_id=(st, peer), device_id_type=MESH)
    pl.semaphore_signal(barrier, 1, device_id=(xn, r), device_id_type=MESH)

    def greet(i):
        pl.semaphore_signal(
            barrier, 1, device_id=(zpeer(i + 1) * 2 + x, r), device_id_type=MESH
        )

    loop(n_z - 1, greet)
    pl.semaphore_wait(barrier, 4 + n_z - 1)

    def tm_copy(src, dst, op, i, peer):
        return pltpu.make_async_remote_copy(
            src, dst, tm_s.at[op, i], tm_r.at[op, i], device_id=(st, peer), device_id_type=MESH
        )

    def gather_start(op, src, slot):
        tm_copy(src, slot(r), op, 1, r2).start()
        tm_copy(src, slot(r), op, 0, r1).start()

    def gather_forward(op, slot):
        tm_copy(slot(r2), slot(r2), op, 1, r2).wait_recv()
        tm_copy(slot(r2), slot(r2), op, 2, r1).start()

    def gather_finish(op, slot):
        tm_copy(slot(r1), slot(r1), op, 0, r1).wait_recv()
        tm_copy(slot(r3), slot(r3), op, 2, r1).wait_recv()

    def gather_drain(op, slot):
        tm_copy(slot(r), slot(r), op, 0, r1).wait_send()
        tm_copy(slot(r), slot(r), op, 1, r2).wait_send()
        tm_copy(slot(r2), slot(r2), op, 2, r1).wait_send()

    peers = ((0, r1), (1, r2), (2, r3))

    def swap_start(op, src, dst):
        for i, p in peers[::-1]:
            tm_copy(src(p), dst(r), op, i, p).start()

    def swap_finish(op, dst):
        for i, p in peers:
            tm_copy(dst(p), dst(p), op, i, p).wait_recv()

    def swap_drain(op, src):
        for i, p in peers:
            tm_copy(src(p), src(p), op, i, p).wait_send()

    def reduce_start(op, part, far, near):
        tm_copy(part(r3), far, op, 0, r1).start()
        tm_copy(part(r1), near, op, 1, r1).start()

    def reduce_mid(op, part, far, land):
        tm_copy(far, far, op, 0, r1).wait_recv()
        far[...] = (far[...].astype(F32) + part(r2)[...].astype(F32)).astype(BF)
        tm_copy(far, land, op, 2, r2).start()

    def reduce_end(op, part, near, land):
        tm_copy(near, near, op, 1, r1).wait_recv()
        tm_copy(land, land, op, 2, r2).wait_recv()
        return part(r)[...].astype(F32) + near[...].astype(F32) + land[...].astype(F32)

    def reduce_drain(op, part, far):
        tm_copy(part(r3), far, op, 0, r1).wait_send()
        tm_copy(part(r1), far, op, 1, r1).wait_send()
        tm_copy(far, far, op, 2, r2).wait_send()

    held = {
        QKV: wqkv,
        WO: wo.at[:, rcol],
        UP: up,
        DOWN: down,
        CONV: conv_all,
    }

    def wslot(g, s):
        return held[g].at[ds(s * own, own)]

    def w_copy(g, s, i, dev):
        return pltpu.make_async_remote_copy(
            wslot(g, s), wslot(g, s), ag_s.at[g, i], ag_r.at[g, i], device_id=(dev, r), device_id_type=MESH
        )

    def w_send(g):
        w_copy(g, st, 0, xn).start()
        loop(n_z - 1, lambda i: w_copy(g, st, i + 1, zpeer(i + 1) * 2 + x).start())

    def w_forward(g):
        def one(i):
            s = zfrom(i + 1) * 2 + x
            w_copy(g, s, i + 1, st).wait_recv()
            w_copy(g, s, n_z + i, xn).start()

        loop(n_z - 1, one)

    def w_finish(g):
        w_copy(g, xn, 0, xn).wait_recv()
        loop(n_z - 1, lambda i: w_copy(g, zfrom(i + 1) * 2 + 1 - x, n_z + i, xn).wait_recv())

    def w_drain(g):
        loop(2 * n_z - 1, lambda i: w_copy(g, st, i, xn).wait_send())

    x_buf = {QKV: x_qkv, WO: x_o, UP: x_up, DOWN: x_down, CONV: x_conv}
    z_buf = {QKV: z_qkv, WO: z_o, UP: z_up, DOWN: z_down, CONV: z_conv}
    grads = {QKV: act.at[:, pl.ds(0, 3 * col)], WO: l_o, UP: up, DOWN: down, CONV: l_conv}

    def gx_copy(g, zz):
        return pltpu.make_async_remote_copy(
            grads[g].at[ds((zz * 2 + 1 - x) * own, own)],
            x_buf[g].at[ds(zz * own, own)],
            rx_s.at[g, zz],
            rx_r.at[g, zz],
            device_id=(xn, r),
            device_id_type=MESH,
        )

    def gx_start(g):
        loop(n_z, lambda i: gx_copy(g, zpeer(i + 1)).start())

    def gz_copy(g, dz, zz):
        return pltpu.make_async_remote_copy(
            x_buf[g].at[ds(zz * own, own)],
            z_buf[g].at[ds((dz - 1) * own, own)],
            rz_s.at[g, dz],
            rz_r.at[g, dz],
            device_id=(zz * 2 + x, r),
            device_id_type=MESH,
        )

    def gz_start(g):
        def one(i):
            zz = zpeer(i + 1)
            gx_copy(g, zz).wait_recv()
            rows = ds(zz * own, own)
            x_buf[g][rows] = (
                x_buf[g][rows].astype(F32) + grads[g][ds((zz * 2 + x) * own, own)].astype(F32)
            ).astype(BF)
            gz_copy(g, i + 1, zz).start()

        loop(n_z - 1, one)

    outs = {
        WO: (((0, col), lambda p: out_o.at[:, ds(p * col, col)]),),
        QKV: (
            ((0, col), lambda p: out_q.at[:, ds(p * col, col)]),
            ((col, col), lambda p: out_k.at[:, ds(p * col, col)]),
            ((2 * col, col), lambda p: out_v.at[:, ds(p * col, col)]),
        ),
        UP: (((0, 1024), lambda p: out_up.at[p]),),
        DOWN: (((0, 1024), lambda p: out_down.at[ds(p * own, own)]),),
        CONV: tuple(
            ((k * col, col), (lambda k: lambda p: out_conv.at[k, :, ds(p * col, col)])(k))
            for k in range(4)
        ),
    }
    fin_base = {QKV: 0, WO: 3, UP: 4, DOWN: 5, CONV: 6}

    def fin_copy(g, j, i, p, slot_rank):
        (lane, size), slot = outs[g][j]
        n = fin_base[g] + j
        return pltpu.make_async_remote_copy(
            x_buf[g].at[ds(z * own, own), pl.ds(lane, size)],
            slot(slot_rank),
            fin_s.at[n, i],
            fin_r.at[n, i],
            device_id=(st, p),
            device_id_type=MESH,
        )

    def g_final(g, gain):
        gx_copy(g, z).wait_recv()
        rows = ds(z * own, own)
        total = x_buf[g][rows].astype(F32) + grads[g][ds((z * 2 + x) * own, own)].astype(F32)
        for dz in range(1, n_z):
            gz_copy(g, dz, zpeer(dz)).wait_recv()
            total = total + z_buf[g][pl.ds((dz - 1) * own, own)].astype(F32)
        if gain is not None:
            total = total * gain[...]
        x_buf[g][rows] = total.astype(BF)
        for j in range(len(outs[g])):
            for i, p in peers[::-1]:
                fin_copy(g, j, i, p, r).start()
            (lane, size), slot = outs[g][j]
            pltpu.make_async_copy(
                x_buf[g].at[rows, pl.ds(lane, size)], slot(r), loc.at[fin_base[g] + j]
            ).start()

    def g_drain(g):
        loop(n_z, lambda i: gx_copy(g, i).wait_send())
        loop(n_z - 1, lambda i: gz_copy(g, i + 1, zpeer(i + 1)).wait_send())
        for j in range(len(outs[g])):
            for i, p in peers:
                d = fin_copy(g, j, i, p, p)
                d.wait_recv()
                d.wait_send()
            (lane, size), slot = outs[g][j]
            pltpu.make_async_copy(
                x_buf[g].at[ds(z * own, own), pl.ds(lane, size)], slot(r), loc.at[fin_base[g] + j]
            ).wait()

    ctx_slot = (
        lambda p: unit.at[0, :, ds(p * 128, 128)],
        lambda p: memraw.at[:, :, ds(p * 64, 64)],
        lambda p: unit.at[2, :, ds(p * 128, 128)],
    )
    ctx_src = (compressed, memory, hidden)
    for p in range(3):
        gather_start(T_CTX0 + p, ctx_src[p], ctx_slot[p])

    for d in (ld_q, ld_k, ld_v):
        d.wait()
    wqkv[own_rows] = (wqkv[own_rows].astype(F32) * gain_a[...]).astype(BF)
    w_send(QKV)
    ld_o.wait()
    w_send(WO)
    ld_up.wait()
    up[own_rows] = (up[own_rows].astype(F32) * gain_f[...]).astype(BF)
    w_send(UP)
    ld_dn.wait()
    w_send(DOWN)
    for d in ld_cv:
        d.wait()
    w_send(CONV)
    for d in ld_c:
        d.wait()
    ld_go.wait()
    ld_gf.wait()

    def norm_block(p, rank):
        def one(s):
            if p == 1:
                for half in range(2):
                    raw = memraw[s, half, ds(rank * 64, 64), :]
                    unit[p, s, ds(half * 256 + rank * 64, 64), :] = layer_norm(raw.astype(F32))[
                        0
                    ].astype(BF)
            else:
                rows = ds(rank * 128, 128)
                unit[p, s, rows, :] = layer_norm(unit[p, s, rows, :].astype(F32))[0].astype(BF)

        loop(2, one)

    def context(p):
        op, slot = T_CTX0 + p, ctx_slot[p]
        norm_block(p, r)
        gather_forward(op, slot)
        tm_copy(slot(r1), slot(r1), op, 0, r1).wait_recv()
        norm_block(p, r1)
        tm_copy(slot(r3), slot(r3), op, 2, r1).wait_recv()
        norm_block(p, r3)
        tm_copy(slot(r2), slot(r2), op, 2, r1).wait_send()
        norm_block(p, r2)

    def project(p):
        def one(i):
            s = lax.div(i, 2)
            at = lax.rem(i, 2) * 256
            rows = ds(at, 256)
            place = pl.ds(pl.multiple_of(p * seg + at, 256), 256)
            a = unit[p, s, rows, :]
            cs = cosines[place, :]
            sn = sines[place, :]

            def rot(t):
                return t * cs + pltpu.roll(t, 64, 1) * sn

            both = dot(a, wqkv[:, pl.ds(col, 2 * col)])
            for h in range(2):
                kv[s, place, pl.ds(h * 128, 128)] = rot(both[:, h * 128 : h * 128 + 128]).astype(BF)
            kv[s, place, pl.ds(col, col)] = both[:, col:].astype(BF)
            if p == 2:
                q = dot(a, wqkv[:, pl.ds(0, col)])
                for h in range(2):
                    qs[s, rows, pl.ds(h * 128, 128)] = (
                        rot(q[:, h * 128 : h * 128 + 128]) * HEAD_DIM ** (-0.5)
                    ).astype(BF)

        loop(4, one)

    context(0)
    w_forward(QKV)
    context(1)
    w_forward(WO)
    w_finish(QKV)
    project(0)
    project(1)
    context(2)
    go_slot = lambda p: go.at[:, ds(p * 128, 128)]
    gather_start(T_GO, grad_out, go_slot)
    gf_src = lambda p: grad_fresh.at[:, :, ds(p * col, col)]
    gf_dst = lambda p: gf.at[:, ds(p * 64, 64)]
    swap_start(T_GF, gf_src, gf_dst)
    project(2)
    w_finish(WO)
    wo_slot = lambda p: wo.at[:, ds(p * col, col)]
    gather_start(T_WO, wo_slot(r), wo_slot)

    def attend(s):
        def one(qt):
            rows = ds(qt * 128, 128)
            shape = (128, seg)
            below = lax.broadcasted_iota(jnp.int32, shape, 1) <= (
                lax.broadcasted_iota(jnp.int32, shape, 0) + qt * 128
            )
            info = row_info[s, rows, :]
            same = doc_k[s] == info[:, 0:1]
            seen = below & same
            bias = info[:, 1:2]
            for h in range(2):
                lanes = pl.ds(h * 128, 128)
                q = qs[s, rows, lanes]
                far = dot(q, kv[s, pl.ds(0, 1024), lanes], 1, 1) + bias
                near = jnp.where(seen, dot(q, kv[s, pl.ds(1024, seg), lanes], 1, 1), -1e30)
                top = jnp.maximum(
                    jnp.max(far, axis=-1, keepdims=True), jnp.max(near, axis=-1, keepdims=True)
                )
                far = jnp.exp(far - top)
                near = jnp.exp(near - top)
                inv = 1.0 / (
                    jnp.sum(far, axis=-1, keepdims=True) + jnp.sum(near, axis=-1, keepdims=True)
                )
                far = (far * inv).astype(BF)
                near = (near * inv).astype(BF)
                probs[s, h, rows, pl.ds(0, 1024)] = far
                probs[s, h, rows, pl.ds(1024, seg)] = near
                vl = pl.ds(col + h * 128, 128)
                o = dot(far, kv[s, pl.ds(0, 1024), vl]) + dot(near, kv[s, pl.ds(1024, seg), vl])
                att_own[s, rows, lanes] = o.astype(BF)

        loop(4, one)

    att_src = lambda s: lambda p: att_own.at[s, ds(p * 128, 128)]
    att_dst = lambda s: lambda p: att_rows.at[s, :, ds(p * col, col)]

    def attend_send(s):
        swap_start(T_ATT0 + s, att_src(s), att_dst(s))
        att_rows[s, :, rcol] = att_own[s, tslot, :]

    attend(0)
    attend_send(0)
    gather_forward(T_GO, go_slot)
    w_forward(UP)
    gather_forward(T_WO, wo_slot)
    attend(1)
    attend_send(1)
    w_finish(UP)

    swap_finish(T_GF, gf_dst)

    def conv_grads(i):
        c = ds(i * 256, 256)
        even_acc = jnp.zeros((256, 512), F32)
        odd_acc = jnp.zeros((256, 512), F32)
        for s in range(2):
            g = gf[s].astype(F32)
            at = lax.broadcasted_iota(jnp.int32, g.shape, 0)
            ahead = jnp.where(at == 255, 0.0, pltpu.roll(g, 255, 0))
            behind = jnp.where(at == 0, 0.0, pltpu.roll(g, 1, 0))
            low = gf[s]
            odd_acc += dot(memraw[s, 1, :, c], jnp.concatenate([ahead.astype(BF), low], 1), 0, 0)
            even_acc += dot(memraw[s, 0, :, c], jnp.concatenate([low, behind.astype(BF)], 1), 0, 0)
        l_conv[c, pl.ds(0, col)] = odd_acc[:, :col].astype(BF)
        l_conv[c, pl.ds(col, col)] = even_acc[:, :col].astype(BF)
        l_conv[c, pl.ds(2 * col, col)] = odd_acc[:, col:].astype(BF)
        l_conv[c, pl.ds(3 * col, col)] = even_acc[:, col:].astype(BF)

    loop(4, conv_grads)
    gx_start(CONV)

    swap_finish(T_ATT0, att_dst(0))
    swap_finish(T_ATT1, att_dst(1))
    gather_finish(T_WO, wo_slot)
    gather_finish(T_GO, go_slot)

    def project_out(i):
        c = ds(i * 256, 256)
        mid = dot(att_rows[...].reshape(256, 1024), wo[:, c]).reshape(2, 128, 256)
        middle[:, :, c] = gm_low[:, :, c].astype(F32) + mid

    loop(4, project_out)
    nf_slot = lambda s: lambda p: nf.at[s, ds(p * 128, 128)]
    for s in range(2):
        nf[s, tslot, :] = layer_norm(middle[s])[0].astype(BF)
        gather_start(T_NF0 + s, nf_slot(s)(r), nf_slot(s))
    w_forward(DOWN)
    for s in range(2):
        gather_forward(T_NF0 + s, nf_slot(s))
    w_finish(DOWN)

    def ffn(s):
        def one(i):
            c = ds(i * 256, 256)
            pre = dot(nf[s], up[:, c])
            g_act = dot(go[s], down[c, :], 1, 1)
            phi = 0.5 + 0.5 * lax.erf(pre * 0.7071067811865476)
            act[pl.ds(s * seg, seg), c] = (pre * phi).astype(BF)
            slope = phi + pre * (jnp.exp(pre * pre * -0.5) * 0.3989422804014327)
            gpre[pl.ds(s * seg, seg), c] = (g_act * slope).astype(BF)

        loop(4, one)

        def back(i):
            c = ds(i * 256, 256)
            gnp[pl.ds(s * seg, seg), c] = dot(
                gpre[pl.ds(s * seg, seg), :], up[c, :], 1, 1
            ).astype(BF)

        loop(4, back)

    def rows_of(buf, s):
        return lambda p: buf.at[pl.ds(pl.multiple_of(s * seg + p * 128, 128), 128)]

    for s in range(2):
        gather_finish(T_NF0 + s, nf_slot(s))
        ffn(s)
        reduce_start(T_GNF0 + s, rows_of(gnp, s), d_b.at[s, 1], d_b.at[s, 0])
    for s in range(2):
        reduce_mid(T_GNF0 + s, rows_of(gnp, s), d_b.at[s, 1], y_b.at[s])
    w_forward(CONV)

    w_drain(UP)
    nf2 = nf

    def up_grads(i):
        c = ds(i * 256, 256)
        up[c, :] = (
            dot(nf2[0, :, c], gpre[pl.ds(0, seg), :], 0, 0)
            + dot(nf2[1, :, c], gpre[pl.ds(seg, seg), :], 0, 0)
        ).astype(BF)

    loop(4, up_grads)
    gx_start(UP)

    for s in range(2):
        c = reduce_end(T_GNF0 + s, rows_of(gnp, s), d_b.at[s, 0], y_b.at[s])
        u, inv = layer_norm(middle[s])
        g = go[s, tslot, :].astype(F32) + norm_back(c, u, inv)
        gm[s] = g
        gm_low[s] = g.astype(BF)
        reduce_drain(T_GNF0 + s, rows_of(gnp, s), d_b.at[s, 1])
    for s in range(2):
        swap_drain(T_ATT0 + s, att_src(s))

    def attended_grads(i):
        part = dot(gm_low[...].reshape(256, 1024), wo[ds(i * 256, 256), :], 1, 1)
        att_own[:, ds(i * 128, 128), :] = part.astype(BF).reshape(2, 128, col)

    loop(4, attended_grads)
    ga_src = lambda p: att_own.at[:, ds(p * 128, 128)]
    ga_dst = lambda p: ga.at[:, ds(p * 128, 128)]
    swap_start(T_GA, ga_src, ga_dst)
    ga[:, tslot, :] = att_own[:, tslot, :]
    for s in range(2):
        gather_drain(T_NF0 + s, nf_slot(s))

    def output_grads(i):
        c = ds(i * 256, 256)
        part = dot(att_rows[:, :, c].reshape(256, 256), gm_low[...].reshape(256, 1024), 0, 0)
        nf[lax.div(i, 2), ds(lax.rem(i, 2) * 256, 256), :] = part.astype(BF)

    loop(4, output_grads)
    op_part = lambda p: nf.at[:, :, ds(p * col, col)]
    reduce_start(T_OP, op_part, d_o.at[1], d_o.at[0])

    def out_parts(i):
        s = lax.div(i, 4)
        rows = ds(s * seg, seg)
        c = ds(lax.rem(i, 4) * 256, 256)
        gpre[rows, c] = dot(act[rows, :], down[:, c]).astype(BF)

    loop(8, out_parts)
    for s in range(2):
        reduce_start(T_OUT0 + s, rows_of(gpre, s), d_a.at[s, 1], d_a.at[s, 0])
    w_drain(DOWN)

    def down_grads(i):
        c = ds(i * 256, 256)
        down[c, :] = (
            dot(act[pl.ds(0, seg), c], go[0], 0, 0) + dot(act[pl.ds(seg, seg), c], go[1], 0, 0)
        ).astype(BF)

    loop(4, down_grads)
    gx_start(DOWN)
    swap_finish(T_GA, ga_dst)
    gz_start(CONV)
    w_finish(CONV)

    def attend_back(s):
        for h in range(2):
            lanes = pl.ds(h * 128, 128)
            vl = pl.ds(col + h * 128, 128)

            def values(i):
                c = ds(i * 512, 512)
                t_v[c, :] = dot(probs[s, h, :, c], ga[s, :, lanes], 0, 0).astype(BF)

            loop(3, values)

            def scores(i):
                rows = ds(i * 128, 128)
                p = probs[s, h, rows, :].astype(F32)
                gp = dot(ga[s, rows, lanes], kv[s, :, vl], 1, 1)
                inner = jnp.sum(p * gp, axis=-1, keepdims=True)
                gs = (p * (gp - inner)).astype(BF)
                probs[s, h, rows, :] = gs
                place = pl.ds(pl.multiple_of(1024 + i * 128, 128), 128)
                t = dot(gs, kv[s, :, lanes])
                t = t * cosines[place, :] - pltpu.roll(t, 64, 1) * sines[place, :]
                t_q[rows, :] = (t * HEAD_DIM ** (-0.5)).astype(BF)

            loop(4, scores)

            def keys(i):
                c = ds(i * 512, 512)
                t = dot(probs[s, h, :, c], qs[s, :, lanes], 0, 0)
                t = t * cosines[c, :] - pltpu.roll(t, 64, 1) * sines[c, :]
                kv[s, c, lanes] = t.astype(BF)
                kv[s, c, vl] = t_v[c, :]

            loop(3, keys)
            qs[s, :, lanes] = t_q[...]

    attend_back(0)
    reduce_mid(T_OP, op_part, d_o.at[1], y_o)
    for s in range(2):
        reduce_mid(T_OUT0 + s, rows_of(gpre, s), d_a.at[s, 1], y_a.at[s])
    gz_start(UP)
    attend_back(1)

    reduce_drain(T_OP, op_part, d_o.at[1])
    l_o[...] = reduce_end(T_OP, op_part, d_o.at[0], y_o).astype(BF).reshape(1024, col)
    gx_start(WO)

    def kv_grads(i):
        c = ds(i * 256, 256)
        total = jnp.zeros((256, 2 * col), F32)
        for p in range(3):
            for s in range(2):
                total += dot(unit[p, s, :, c], kv[s, pl.ds(p * seg, seg), :], 0, 0)
        act[c, pl.ds(col, 2 * col)] = total.astype(BF)
        act[c, pl.ds(0, col)] = (
            dot(unit[2, 0, :, c], qs[0], 0, 0) + dot(unit[2, 1, :, c], qs[1], 0, 0)
        ).astype(BF)

    loop(4, kv_grads)
    gx_start(QKV)

    def hidden_grads(i):
        s = lax.div(i, 4)
        c = ds(lax.rem(i, 4) * 256, 256)
        part = dot(kv[s, pl.ds(1024, seg), :], wqkv[c, pl.ds(col, 2 * col)], 1, 1) + dot(
            qs[s], wqkv[c, pl.ds(0, col)], 1, 1
        )
        gnp[ds(s * seg, seg), c] = part.astype(BF)

    loop(8, hidden_grads)
    for s in range(2):
        reduce_start(T_GN0 + s, rows_of(gnp, s), d_b.at[s, 1], d_b.at[s, 0])
    ld_h = load(hidden, gm_low, 13)
    g_final(CONV, None)
    gz_start(DOWN)
    for s in range(2):
        reduce_mid(T_GN0 + s, rows_of(gnp, s), d_b.at[s, 1], y_b.at[s])

    gather_drain(T_GO, go_slot)
    ld_w = [
        load(conv_all.at[pl.ds(i * seg, seg)], go.at[i], 14 + i) for i in range(2)
    ]
    for s in range(2):
        out = reduce_end(T_OUT0 + s, rows_of(gpre, s), d_a.at[s, 0], y_a.at[s])
        reduce_drain(T_OUT0 + s, rows_of(gpre, s), d_a.at[s, 1])
        y_a[s] = (middle[s] + out).astype(BF)
    st_out = load(y_a, layer_out, 16)
    for d in ld_w:
        d.wait()
    swap_drain(T_GA, ga_src)
    w_tap = lambda i, k: go[i, :, pl.ds(k * col, col)]

    def fresh(s, carry):
        taps = []
        for k in range(4):
            rows = memraw.at[s, 1 - k % 2]
            taps.append(
                dot(rows[:, pl.ds(0, seg)], w_tap(0, k)) + dot(rows[:, pl.ds(seg, seg)], w_tap(1, k))
            )
        at = lax.broadcasted_iota(jnp.int32, taps[0].shape, 0)
        total = taps[1] + taps[2]
        total += jnp.where(at == 0, 0.0, pltpu.roll(taps[0], 1, 0))
        total += jnp.where(at == 255, 0.0, pltpu.roll(taps[3], 255, 0))
        att_own[s, pl.ds(0, 256), :] = total.astype(BF)
        return carry

    lax.fori_loop(0, 2, fresh, 0)
    fr_src = lambda p: att_own.at[:, ds(p * 64, 64)]
    fr_dst = lambda p: fresh_out.at[:, :, ds(p * col, col)]
    swap_start(T_FR, fr_src, fr_dst)
    st_fr = load(fr_src(r), fr_dst(r), 17)

    g_final(UP, gain_f)
    gz_start(WO)
    gz_start(QKV)
    for s in range(2):
        c = reduce_end(T_GN0 + s, rows_of(gnp, s), d_b.at[s, 0], y_b.at[s])
        if s == 0:
            ld_h.wait()
        u, inv = layer_norm(gm_low[s].astype(F32))
        gm[s] = gm[s] + norm_back(c, u, inv)
    st_gi = load(gm, grad_input, 18)
    g_final(DOWN, None)
    g_final(WO, None)
    g_final(QKV, gain_a)

    for p in range(3):
        tm_copy(ctx_src[p], ctx_slot[p](r), T_CTX0 + p, 0, r1).wait_send()
        tm_copy(ctx_src[p], ctx_slot[p](r), T_CTX0 + p, 1, r2).wait_send()
    swap_drain(T_GF, gf_src)
    gather_drain(T_WO, wo_slot)
    for s in range(2):
        reduce_drain(T_GN0 + s, rows_of(gnp, s), d_b.at[s, 1])
    swap_finish(T_FR, fr_dst)
    swap_drain(T_FR, fr_src)
    for d in (st_out, st_fr, st_gi):
        d.wait()
    for g in (QKV, WO, CONV):
        w_drain(g)
    for g in range(5):
        g_drain(g)


def per_device(
    hidden,
    memory,
    compressed,
    reset_flag,
    boundary,
    query_weight,
    key_weight,
    value_weight,
    output_weight,
    up_weight,
    down_weight,
    conv_weight,
    attn_gain,
    ffn_gain,
    grad_out,
    grad_fresh,
):
    groups = lax.axis_size("stream")
    rank = lax.axis_index("tm")
    streams, seg_rows, width = hidden.shape
    own = query_weight.shape[0]
    seg = seg_rows * PARTS
    cols = width // PARTS
    n_z = groups // 2
    ff_rows = down_weight.shape[0] // PARTS
    up_own = lax.dynamic_index_in_dim(
        up_weight.reshape(own, groups, PARTS, ff_rows), rank, 2, keepdims=False
    ).reshape(own, groups * ff_rows)
    halves = memory.reshape(streams, seg_rows // 2, 2, width).transpose(0, 2, 1, 3)
    gain_a = attn_gain.astype(F32)[:, None]
    gain_f = ffn_gain.astype(F32)[:, None]
    spots = jnp.arange(seg)
    places = jnp.concatenate([spots, seg + spots[::2], seg + spots[1::2], 2 * seg + spots])
    half = HEAD_DIM // 2
    frequency = 10000.0 ** (-jnp.arange(half).astype(F32) * 2.0 / HEAD_DIM)
    angles = places.astype(F32)[:, None] * frequency[None, :]
    cosine = jnp.cos(angles)
    sine = jnp.sin(angles)
    cosines = jnp.concatenate([cosine, cosine], axis=1)
    sines = jnp.concatenate([-sine, sine], axis=1)
    documents = jnp.cumsum(boundary, axis=1)
    memory_ok = (reset_flag[:, None] == 0) & (documents == 0)
    docs = documents.astype(F32)
    row_info = jnp.stack([docs, jnp.where(memory_ok, 0.0, -1e30)], axis=2)
    doc_k = docs[:, None, :]

    hbm = pl.BlockSpec(memory_space=pl.ANY)
    vmem = pl.BlockSpec(memory_space=pltpu.VMEM)
    big = (seg * streams, width)
    out_shape = (
        jax.ShapeDtypeStruct(hidden.shape, BF),
        jax.ShapeDtypeStruct(grad_fresh.shape, BF),
        jax.ShapeDtypeStruct(hidden.shape, F32),
        jax.ShapeDtypeStruct((own, width), BF),
        jax.ShapeDtypeStruct((own, width), BF),
        jax.ShapeDtypeStruct((own, width), BF),
        jax.ShapeDtypeStruct((own, width), BF),
        jax.ShapeDtypeStruct((PARTS, own, width), BF),
        jax.ShapeDtypeStruct((PARTS * own, width), BF),
        jax.ShapeDtypeStruct((4, own, width), BF),
        jax.ShapeDtypeStruct((width, width), BF),
    )

    def v(shape, dtype=BF):
        return pltpu.VMEM(shape, dtype)

    seg2 = (streams, seg, cols)
    rows2 = (streams, seg_rows, width)
    wide = (3 * cols, cols, width, width, width)
    sem = pltpu.SemaphoreType.DMA
    scratch = (
        [
            v((3, streams, seg, width)),
            v((streams, 2, seg // 2, width)),
            v((width, 3 * cols)),
            v((width, width)),
            v(big),
            v(big),
            v(seg2),
            v((streams, 3 * seg, 2 * cols)),
            v((streams, 2, seg, 3 * seg)),
            v(seg2),
            v(rows2),
            v(rows2, F32),
            v((streams, seg, width)),
            v((streams, seg, width)),
            v((streams, seg // 2, cols)),
            v(big),
            v(big),
            v(seg2),
            v(rows2, F32),
            v(rows2),
            v(big),
            v((streams, 2, seg_rows, width)),
            v(rows2),
            v((streams, 2, seg_rows, width)),
            v(rows2),
            v((2, streams, seg, cols)),
            v(seg2),
            v((width, cols)),
            v(big),
        ]
        + [v((n_z * own, c)) for c in wide]
        + [v(((n_z - 1) * own, c)) for c in wide]
        + [
            v((3 * seg, HEAD_DIM)),
            v((seg, HEAD_DIM)),
            sem((20,)),
            sem((T_COUNT, 3)),
            sem((T_COUNT, 3)),
            sem((5, 2 * n_z)),
            sem((5, 2 * n_z)),
            sem((5, n_z)),
            sem((5, n_z)),
            sem((5, n_z)),
            sem((5, n_z)),
            sem((10, 3)),
            sem((10, 3)),
        ]
    )
    results = pl.pallas_call(
        functools.partial(kernel, n_z, own),
        out_shape=out_shape,
        in_specs=[hbm] * 12 + [vmem] * 6,
        out_specs=tuple([hbm] * len(out_shape)),
        scratch_shapes=scratch,
        compiler_params=pltpu.CompilerParams(
            collective_id=0, has_side_effects=True, vmem_limit_bytes=64000 * 1024
        ),
        name="layer",
    )(
        hidden,
        halves,
        compressed,
        query_weight,
        key_weight,
        value_weight,
        output_weight,
        up_own,
        down_weight,
        conv_weight,
        grad_out,
        grad_fresh,
        gain_a,
        gain_f,
        cosines,
        sines,
        row_info,
        doc_k,
    )
    layer_out, fresh, grad_input, g_q, g_k, g_v, g_o, g_up, g_down, g_conv, _ = results
    wide = lambda t: t.astype(F32)
    g_up = g_up.reshape(PARTS, own, groups, ff_rows).transpose(1, 2, 0, 3).reshape(up_weight.shape)
    g_q, g_k, g_v, g_o, g_up, g_down, g_conv = map(wide, (g_q, g_k, g_v, g_o, g_up, g_down, g_conv))
    attn_gain_grad = jnp.sum(
        wide(query_weight) * g_q + wide(key_weight) * g_k + wide(value_weight) * g_v, axis=1
    ) / wide(attn_gain)
    ffn_gain_grad = jnp.sum(wide(up_weight) * g_up, axis=1) / wide(ffn_gain)
    return (
        layer_out,
        fresh,
        grad_input,
        g_q,
        g_k,
        g_v,
        g_o,
        g_up,
        g_down,
        g_conv,
        attn_gain_grad,
        ffn_gain_grad,
    )


def solution(mesh):
    act = P("stream", "tm", None)
    row = P("stream", None)
    in_specs = (act, act, act, P("stream"), row) + (row,) * 6 + (
        P(None, "stream", None),
        P("stream"),
        P("stream"),
        act,
        act,
    )
    out_specs = (act, act, act) + (row,) * 6 + (
        P(None, "stream", None),
        P("stream"),
        P("stream"),
    )
    return jax.shard_map(
        per_device, mesh=mesh, in_specs=in_specs, out_specs=out_specs, check_vma=False
    )
```

time: 855 us -> 306 us (0.36)
  waiting for transfers between devices: 453 us -> 0 us
  Pallas kernels: 0 us -> 272 us
  matrix products: 121 us -> 0 us
  local copies, waits for them, and re-layouts: 129 us -> 17 us
  other arithmetic: 82.6 us -> 15.9 us
  blocking collectives: 37.7 us -> 0 us
  between operations: 15.2 us -> 0.88 us
    pallas_call x0 -> x1, Pallas kernels: none -> 272 us  [per_device(): pl.pallas_call(functools.partial(kernel, n_z, own), out_shape=out_shape,...]
    all_gather x11 -> x0, waiting for transfers between devices: 254 us -> none  [the longest x1 52.7 us: per_device(): near_full = lax.all_gather(near, 'stream', axis=0, tiled=True)]
    dot_general x25 -> x0, matrix products: 109 us -> none  [the longest x7 30.2 us: tmm(): lax.dot_general(a, b, ((dims, dims), ((), ())), preferred_element_type=F32)]
    unnamed x19 -> x0, waiting for transfers between devices: 108 us -> none
    reduce_scatter x4 -> x0, waiting for transfers between devices: 79.5 us -> none  [the longest x1 33.2 us: per_device(): lax.psum_scatter(down_part, 'tm', scatter_dimension=1, tiled=True)]
    slice x10 -> x3, local copies, waits for them, and re-layouts: 42.6 us -> 0.66 us  [the longest x1 0.22 us: per_device(): spots[1::2]]
    unnamed x127 -> x34, local copies, waits for them, and re-layouts: 40.8 us -> 5.22 us
    all_to_all x2 -> x0, blocking collectives: 21.6 us -> none  [the longest x1 12.3 us: per_device(): lax.all_to_all(attended, 'tm', split_axis=1, concat_axis=2, tiled=True)]
  transfers between devices with their start and end apart: 19 -> 0, of which waited for: 15 -> 0; matrix products, arithmetic and copies ran while one was open for 32% -> 0% of each run, Pallas kernels for 0% -> 0%
where the time goes in v2:
time: 306 us
  Pallas kernels  272 us (89%)
  local copies, waits for them, and re-layouts  17 us (6%)
  other arithmetic  15.9 us (5%)
    pallas_call x1, Pallas kernels, per_device(): pl.pallas_call(functools.partial(kernel, n_z, own), out_shape=out_shape,...  272 us

profile of v2, /device:TPU:26, one launch (start us, length us, event | category | flops | bytes accessed | tf_op | source)
XLA Modules:
  0.0 306.0 jit_solution(5124109983825107313)
XLA Ops:
  0.6 0.7 reshape.170
  1.3 0.6 reduce-window.6
  2.0 0.2 slice_reduce_fusion
  2.2 0.2 reduce-window.9
  2.3 0.1 add_convert_fusion.1
  2.4 0.4 convert_element_type.111
  2.8 0.1 add_compare_fusion
  2.9 0.5 eq.24
  3.3 0.7 broadcast_compare_fusion
  4.0 0.1 and_select_fusion
  4.1 1.0 pad_maximum_fusion.2.row_info
  5.1 0.2 slice.12
  5.4 0.2 slice.13
  5.6 0.0 copy-start.1
  5.7 2.8 fusion
  8.5 1.2 pad_maximum_fusion.1.sines
  9.6 0.8 reshape.168
  10.4 0.0 copy-start.7
  10.4 1.5 dynamic-slice_reduce_fusion
  11.9 0.0 copy-start.12
  12.0 0.0 copy-start.13
  12.0 0.8 copy.63
  12.7 1.2 pad_maximum_fusion.cosines
  13.9 0.5 copy.49
  14.4 1.0 copy.62
  15.4 0.7 copy.54.gain_a
  16.1 0.7 copy.55.gain_f
  16.9 272.1 %layer.1 = (bf16[2,128,1024]{2,1,0:T(8,128)(2,1)}, bf16[2,64,1024]{2,1,0:T(8,128)(2,1)}, f32[2,128,1024]{2,1,0:T(8,128)}, bf16[128,1024]{1,0:T(8,128)(2,1)}, bf1...) custom-call(bf16[2,128,1024]{2,1,0:T(8,128)(2,1)} %hidden.1, ...), custom_call_target="tpu_custom_call" | custom-call | tf_op jit(solution)/shard_map/layer/pallas_call | solution.py:933
  289.0 0.0 copy-start.4
  289.0 0.0 copy-done.6
  289.0 2.7 add_reduce_fusion
  291.8 0.5 convert_divide_fusion.1
  292.3 0.3 copy.59
  292.6 0.1 bitcast_bitcast_fusion
  292.7 2.7 copy.56
  295.4 2.1 reshape.172
  297.5 0.0 copy-start
  297.5 0.3 multiply_reduce_fusion
  297.8 0.5 convert_divide_fusion
  298.4 1.1 copy-done.3
  299.5 1.6 convert_element_type.102
  301.1 0.0 copy-done
  301.1 0.0 copy-done.2
  301.1 1.6 convert_element_type.103
  302.7 0.8 convert_element_type.97
  303.5 0.8 copy.67
  304.3 0.7 copy.68
  305.0 1.0 copy.69
  (27 shorter events, 0.1 us)
Async XLA Ops:
  2.4 6.1 %copy-start.11 = (f32[2,4,128]{2,1,0:T(4,128)}, f32[2,4,128]{2,1,0:T(4,128)S(1)}, u32[]{:S(2)}) copy-start(f32[2,4,128]{2,1,0:T(4,128)S(1)} %add_convert_fusion.1) | copy-start | bytes 12292
  5.6 4.0 %copy-start.1 = (bf16[128,4096]{1,0:T(8,128)(2,1)S(1)}, bf16[128,4096]{1,0:T(8,128)(2,1)}, u32[]{:S(2)}) copy-start(bf16[128,4096]{1,0:T(8,128)(2,1)} %param.25) | copy-start | bytes 3145732
  10.4 3.5 %copy-start.7 = (bf16[2,128,1024]{2,1,0:T(8,128)(2,1)S(1)}, bf16[2,128,1024]{2,1,0:T(8,128)(2,1)}, u32[]{:S(2)}) copy-start(bf16[2,128,1024]{2,1,0:T(8,128)(2,1)} %param.17) | copy-start | bytes 1572868
  11.9 3.4 %copy-start.12 = (bf16[128]{0:T(256)(128)(2,1)S(1)}, bf16[128]{0:T(256)(128)(2,1)}, u32[]{:S(2)}) copy-start(bf16[128]{0:T(256)(128)(2,1)} %param.28) | copy-start | bytes 772
  12.0 4.2 %copy-start.13 = (bf16[128]{0:T(256)(128)(2,1)S(1)}, bf16[128]{0:T(256)(128)(2,1)}, u32[]{:S(2)}) copy-start(bf16[128]{0:T(256)(128)(2,1)} %param.29) | copy-start | bytes 772
  16.9 272.2 %copy-start.6 = (bf16[128,1024]{1,0:T(8,128)(2,1)S(1)}, bf16[128,1024]{1,0:T(8,128)(2,1)}, u32[]{:S(2)}) copy-start(bf16[128,1024]{1,0:T(8,128)(2,1)} %query_weight.1) | copy-start | bytes 786436
  289.0 3.3 %copy-start.4 = (bf16[4,128,1024]{2,1,0:T(8,128)(2,1)S(1)}, bf16[4,128,1024]{2,1,0:T(8,128)(2,1)}, u32[]{:S(2)}) copy-start(bf16[4,128,1024]{2,1,0:T(8,128)(2,1)} %get-tuple-element.29) | copy-start | bytes 3145732
  297.5 3.6 %copy-start = (f32[128,4096]{1,0:T(8,128)}, f32[128,4096]{1,0:T(8,128)S(1)}, u32[]{:S(2)}) copy-start(f32[128,4096]{1,0:T(8,128)S(1)} %reshape.172) | copy-start | bytes 6291460
  297.5 2.0 copy-start.3
  297.8 3.2 %copy-start.2 = (bf16[4,128,1024]{2,1,0:T(8,128)(2,1)S(1)}, bf16[4,128,1024]{2,1,0:T(8,128)(2,1)}, u32[]{:S(2)}) copy-start(bf16[4,128,1024]{2,1,0:T(8,128)(2,1)} %get-tuple-element.31) | copy-start | bytes 3145732
  301.1 1.6 copy-start.9
  301.1 2.4 copy-start.8
  301.1 3.2 %copy-start.10 = (bf16[2,64,1024]{2,1,0:T(8,128)(2,1)S(1)}, bf16[2,64,1024]{2,1,0:T(8,128)(2,1)}, u32[]{:S(2)}) copy-start(bf16[2,64,1024]{2,1,0:T(8,128)(2,1)} %get-tuple-element.54) | copy-start | bytes 786436
  301.1 3.9 %copy-start.5 = (f32[2,128,1024]{2,1,0:T(8,128)S(1)}, f32[2,128,1024]{2,1,0:T(8,128)}, u32[]{:S(2)}) copy-start(f32[2,128,1024]{2,1,0:T(8,128)} %get-tuple-element.55) | copy-start | bytes 3145732

commit v3 on v2

--- a/solution.py
+++ b/solution.py
@@ -2,6 +2,7 @@
 
 import jax
 import jax.numpy as jnp
+import numpy as np
 from jax import lax
 from jax.experimental import pallas as pl
 from jax.experimental.pallas import tpu as pltpu
@@ -52,6 +53,7 @@
 def kernel(
     n_z,
     own,
+    pieces,
     hidden,
     memory,
     compressed,
@@ -59,17 +61,16 @@
     key_weight,
     value_weight,
     output_weight,
-    up_own,
+    up_weight,
     down_weight,
     conv_weight,
     grad_out,
     grad_fresh,
-    gain_a,
-    gain_f,
+    reset_flag,
+    boundary,
+    gains,
     cosines,
     sines,
-    row_info,
-    doc_k,
     layer_out,
     fresh_out,
     grad_input,
@@ -120,8 +121,16 @@
     z_up,
     z_down,
     z_conv,
+    r_qkv,
+    r_o,
+    r_up,
+    r_down,
+    r_conv,
     t_v,
     t_q,
+    gain_cols,
+    row_info,
+    doc_k,
     loc,
     tm_s,
     tm_r,
@@ -133,6 +142,7 @@
     rz_r,
     fin_s,
     fin_r,
+    fin_l,
 ):
     st = lax.axis_index("stream")
     r = lax.axis_index("tm")
@@ -163,19 +173,30 @@
     ld_k = load(key_weight.at[:, rcol], wqkv.at[own_rows, pl.ds(col, col)], 1)
     ld_v = load(value_weight.at[:, rcol], wqkv.at[own_rows, pl.ds(2 * col, col)], 2)
     ld_o = load(output_weight.at[:, rcol], wo.at[own_rows, rcol], 3)
-    ld_up = load(up_own, up.at[own_rows], 4)
+    if pieces > 1:
+        size = 1024 // pieces
+        ld_up = [
+            load(
+                up_weight.at[:, ds((i * PARTS + r) * size, size)],
+                up.at[own_rows, pl.ds(i * size, size)],
+                18 + i,
+            )
+            for i in range(pieces)
+        ]
+    else:
+        ld_up = [load(up_weight, up.at[own_rows], 4)]
     ld_dn = load(down_weight.at[ds(r * own, own)], down.at[own_rows], 5)
     ld_cv = [
         load(conv_weight.at[k, :, rcol], conv_all.at[own_rows, pl.ds(k * col, col)], 6 + k)
         for k in range(4)
     ]
     tslot = ds(r * 128, 128)
-    ld_c = [
-        load(compressed, unit.at[0, :, tslot], 10),
-        load(memory, memraw.at[:, :, ds(r * 64, 64)], 11),
-        load(hidden, unit.at[2, :, tslot], 12),
-        load(hidden, gm_low, 13),
-    ]
+    ld_m = load(memory, att_rows, 11)
+    ld_c = {
+        0: load(compressed, unit.at[0, :, tslot], 10),
+        2: load(hidden, unit.at[2, :, tslot], 12),
+    }
+    ld_h = load(hidden, gm_low, 13)
     ld_go = load(grad_out, go.at[:, tslot], 14)
     ld_gf = load(grad_fresh.at[:, :, rcol], gf.at[:, ds(r * 64, 64)], 15)
 
@@ -258,31 +279,135 @@
     def wslot(g, s):
         return held[g].at[ds(s * own, own)]
 
-    def w_copy(g, s, i, dev):
+    def w_copy(g, s, i, dev, j=None):
         return pltpu.make_async_remote_copy(
-            wslot(g, s), wslot(g, s), ag_s.at[g, i], ag_r.at[g, i], device_id=(dev, r), device_id_type=MESH
+            wslot(g, s),
+            wslot(g, s),
+            ag_s.at[g, i],
+            ag_r.at[g, i if j is None else j],
+            device_id=(dev, r),
+            device_id_type=MESH,
         )
+
+    relay = n_z == 4
+    inner = (z == 1) | (z == 2)
+
+    def direct(dz):
+        zz = zpeer(dz)
+        return (z + 3 != zz) & (zz + 3 != z)
 
     def w_send(g):
         w_copy(g, st, 0, xn).start()
-        loop(n_z - 1, lambda i: w_copy(g, st, i + 1, zpeer(i + 1) * 2 + x).start())
+        if relay:
+            for dz in (2, 1, 3):
+
+                @pl.when(direct(dz))
+                def _():
+                    w_copy(g, st, dz, zpeer(dz) * 2 + x).start()
+        else:
+            loop(n_z - 1, lambda i: w_copy(g, st, i + 1, zpeer(i + 1) * 2 + x).start())
+
+    def w_pass(g, dz):
+        s = zfrom(dz) * 2 + x
+        w_copy(g, s, dz, st).wait_recv()
+        w_copy(g, s, n_z + dz - 1, xn).start()
+
+    def w_relay(g):
+        s = zfrom(2) * 2 + x
+        return w_copy(g, s, 2 * n_z - 1, 3 * (z - 1) * 2 + x, 2 * z - 1)
+
+    last = jnp.where(z == 0, 1, 3)
 
     def w_forward(g):
-        def one(i):
-            s = zfrom(i + 1) * 2 + x
-            w_copy(g, s, i + 1, st).wait_recv()
-            w_copy(g, s, n_z + i, xn).start()
-
-        loop(n_z - 1, one)
+        if relay:
+            s = zfrom(2) * 2 + x
+            w_copy(g, s, 2, st).wait_recv()
+
+            @pl.when(inner)
+            def _():
+                w_relay(g).start()
+
+            w_copy(g, s, n_z + 1, xn).start()
+            w_pass(g, 4 - last)
+        else:
+            loop(n_z - 1, lambda i: w_pass(g, i + 1))
+
+    def w_forward_last(g):
+        if relay:
+            w_pass(g, last)
+
+    def w_cross(g):
+        w_copy(g, xn, 0, xn).wait_recv()
+        if relay:
+            for dz in (2, 1, 3):
+
+                @pl.when(direct(dz))
+                def _():
+                    w_copy(g, xn, n_z + dz - 1, zpeer(dz) * 2 + x).start()
+        else:
+            loop(n_z - 1, lambda i: w_copy(g, xn, n_z + i, zpeer(i + 1) * 2 + x).start())
+
+    def w_relay_cross(g):
+        s = zfrom(2) * 2 + 1 - x
+        return w_copy(g, s, 2 * n_z, 3 * (z - 1) * 2 + x, n_z + 2 * z - 2)
+
+    def w_cross_pass(g):
+        if relay:
+            w_copy(g, zfrom(2) * 2 + x, 2, st).wait_recv()
+            w_copy(g, zfrom(2) * 2 + 1 - x, n_z + 1, st).wait_recv()
+
+            @pl.when(inner)
+            def _():
+                w_relay(g).start()
+                w_relay_cross(g).start()
+
+    def w_cross_finish(g):
+        rest = (1, 3) if relay else range(1, n_z)
+        for dz in rest:
+            w_copy(g, zfrom(dz) * 2 + x, dz, st).wait_recv()
+            w_copy(g, zfrom(dz) * 2 + 1 - x, n_z + dz - 1, st).wait_recv()
+
+    def w_cross_drain(g):
+        w_copy(g, st, 0, xn).wait_send()
+        for dz in range(1, n_z):
+            if relay:
+
+                @pl.when(direct(dz))
+                def _():
+                    w_copy(g, st, dz, xn).wait_send()
+                    w_copy(g, st, n_z + dz - 1, xn).wait_send()
+            else:
+                w_copy(g, st, dz, xn).wait_send()
+                w_copy(g, st, n_z + dz - 1, xn).wait_send()
+        if relay:
+
+            @pl.when(inner)
+            def _():
+                w_relay(g).wait_send()
+                w_relay_cross(g).wait_send()
 
     def w_finish(g):
         w_copy(g, xn, 0, xn).wait_recv()
         loop(n_z - 1, lambda i: w_copy(g, zfrom(i + 1) * 2 + 1 - x, n_z + i, xn).wait_recv())
 
     def w_drain(g):
-        loop(2 * n_z - 1, lambda i: w_copy(g, st, i, xn).wait_send())
+        w_copy(g, st, 0, xn).wait_send()
+        loop(n_z - 1, lambda i: w_copy(g, st, n_z + i, xn).wait_send())
+        if relay:
+            for dz in (1, 2, 3):
+
+                @pl.when(direct(dz))
+                def _():
+                    w_copy(g, st, dz, xn).wait_send()
+
+            @pl.when(inner)
+            def _():
+                w_relay(g).wait_send()
+        else:
+            loop(n_z - 1, lambda i: w_copy(g, st, i + 1, xn).wait_send())
 
     x_buf = {QKV: x_qkv, WO: x_o, UP: x_up, DOWN: x_down, CONV: x_conv}
+    r_buf = {QKV: r_qkv, WO: r_o, UP: r_up, DOWN: r_down, CONV: r_conv}
     z_buf = {QKV: z_qkv, WO: z_o, UP: z_up, DOWN: z_down, CONV: z_conv}
     grads = {QKV: act.at[:, pl.ds(0, 3 * col)], WO: l_o, UP: up, DOWN: down, CONV: l_conv}
 
@@ -309,17 +434,61 @@
             device_id_type=MESH,
         )
 
+    def gz_fold(g, zz):
+        gx_copy(g, zz).wait_recv()
+        rows = ds(zz * own, own)
+        x_buf[g][rows] = (
+            x_buf[g][rows].astype(F32) + grads[g][ds((zz * 2 + x) * own, own)].astype(F32)
+        ).astype(BF)
+
+    def gz_far(g, dz, zz):
+        return pltpu.make_async_remote_copy(
+            x_buf[g].at[ds(zz * own, own)],
+            r_buf[g],
+            rz_s.at[g, dz],
+            rz_r.at[g, 0],
+            device_id=(jnp.where(z == 0, 1, 2) * 2 + x, r),
+            device_id_type=MESH,
+        )
+
     def gz_start(g):
-        def one(i):
-            zz = zpeer(i + 1)
-            gx_copy(g, zz).wait_recv()
-            rows = ds(zz * own, own)
-            x_buf[g][rows] = (
-                x_buf[g][rows].astype(F32) + grads[g][ds((zz * 2 + x) * own, own)].astype(F32)
-            ).astype(BF)
-            gz_copy(g, i + 1, zz).start()
-
-        loop(n_z - 1, one)
+        if not relay:
+
+            def one(i):
+                zz = zpeer(i + 1)
+                gz_fold(g, zz)
+                gz_copy(g, i + 1, zz).start()
+
+            loop(n_z - 1, one)
+            return
+        for dz in (1, 3):
+            zz = zpeer(dz)
+            gz_fold(g, zz)
+
+            @pl.when(direct(dz))
+            def _():
+                gz_copy(g, dz, zz).start()
+
+            @pl.when(jnp.logical_not(direct(dz)))
+            def _():
+                gz_far(g, dz, zz).start()
+
+        @pl.when(jnp.logical_not(inner))
+        def _():
+            gz_fold(g, zpeer(2))
+            gz_copy(g, 2, zpeer(2)).start()
+
+    def gz_relay(g):
+        if relay:
+
+            @pl.when(inner)
+            def _():
+                zz = zpeer(2)
+                gz_fold(g, zz)
+                gz_far(g, 2, zz).wait_recv()
+                rows = ds(zz * own, own)
+                x_buf[g][rows] = (x_buf[g][rows].astype(F32) + r_buf[g][...].astype(F32)).astype(BF)
+                gz_copy(g, 2, zz).start()
 
     outs = {
         WO: (((0, col), lambda p: out_o.at[:, ds(p * col, col)]),),
@@ -328,14 +497,20 @@
             ((col, col), lambda p: out_k.at[:, ds(p * col, col)]),
             ((2 * col, col), lambda p: out_v.at[:, ds(p * col, col)]),
         ),
-        UP: (((0, 1024), lambda p: out_up.at[p]),),
+        UP: tuple(
+            (
+                (i * (1024 // pieces), 1024 // pieces),
+                (lambda i: lambda p: out_up.at[:, ds((i * PARTS + p) * (1024 // pieces), 1024 // pieces)])(i),
+            )
+            for i in range(pieces)
+        ),
         DOWN: (((0, 1024), lambda p: out_down.at[ds(p * own, own)]),),
         CONV: tuple(
             ((k * col, col), (lambda k: lambda p: out_conv.at[k, :, ds(p * col, col)])(k))
             for k in range(4)
         ),
     }
-    fin_base = {QKV: 0, WO: 3, UP: 4, DOWN: 5, CONV: 6}
+    fin_base = {QKV: 0, WO: 3, DOWN: 4, CONV: 5, UP: 9}
 
     def fin_copy(g, j, i, p, slot_rank):
         (lane, size), slot = outs[g][j]
@@ -349,64 +524,115 @@
             device_id_type=MESH,
         )
 
+    def g_keep(g, j):
+        (lane, size), slot = outs[g][j]
+        return pltpu.make_async_copy(
+            x_buf[g].at[ds(z * own, own), pl.ds(lane, size)], slot(r), fin_l.at[fin_base[g] + j]
+        )
+
     def g_final(g, gain):
         gx_copy(g, z).wait_recv()
         rows = ds(z * own, own)
         total = x_buf[g][rows].astype(F32) + grads[g][ds((z * 2 + x) * own, own)].astype(F32)
         for dz in range(1, n_z):
-            gz_copy(g, dz, zpeer(dz)).wait_recv()
+            if relay:
+
+                @pl.when(direct(n_z - dz))
+                def _():
+                    gz_copy(g, dz, zpeer(dz)).wait_recv()
+            else:
+                gz_copy(g, dz, zpeer(dz)).wait_recv()
             total = total + z_buf[g][pl.ds((dz - 1) * own, own)].astype(F32)
         if gain is not None:
-            total = total * gain[...]
+            total = total * gain
         x_buf[g][rows] = total.astype(BF)
         for j in range(len(outs[g])):
-            for i, p in peers[::-1]:
-                fin_copy(g, j, i, p, r).start()
-            (lane, size), slot = outs[g][j]
-            pltpu.make_async_copy(
-                x_buf[g].at[rows, pl.ds(lane, size)], slot(r), loc.at[fin_base[g] + j]
-            ).start()
+            fin_copy(g, j, 1, r2, r).start()
+            fin_copy(g, j, 0, r1, r).start()
+            g_keep(g, j).start()
+
+    def fin_pass(g, j):
+        slot = outs[g][j][1](r2)
+        n = fin_base[g] + j
+        return pltpu.make_async_remote_copy(
+            slot, slot, fin_s.at[n, 2], fin_r.at[n, 2], device_id=(st, r1), device_id_type=MESH
+        )
+
+    def g_pass(g):
+        for j in range(len(outs[g])):
+            fin_copy(g, j, 1, r2, r2).wait_recv()
+            fin_pass(g, j).start()
 
     def g_drain(g):
         loop(n_z, lambda i: gx_copy(g, i).wait_send())
         loop(n_z - 1, lambda i: gz_copy(g, i + 1, zpeer(i + 1)).wait_send())
         for j in range(len(outs[g])):
-            for i, p in peers:
-                d = fin_copy(g, j, i, p, p)
-                d.wait_recv()
-                d.wait_send()
-            (lane, size), slot = outs[g][j]
-            pltpu.make_async_copy(
-                x_buf[g].at[ds(z * own, own), pl.ds(lane, size)], slot(r), loc.at[fin_base[g] + j]
-            ).wait()
+            fin_copy(g, j, 0, r1, r1).wait()
+            fin_copy(g, j, 1, r2, r).wait_send()
+            fin_pass(g, j).wait()
+            g_keep(g, j).wait()
 
     ctx_slot = (
         lambda p: unit.at[0, :, ds(p * 128, 128)],
         lambda p: memraw.at[:, :, ds(p * 64, 64)],
         lambda p: unit.at[2, :, ds(p * 128, 128)],
     )
-    ctx_src = (compressed, memory, hidden)
-    for p in range(3):
-        gather_start(T_CTX0 + p, ctx_src[p], ctx_slot[p])
-
+    gather_start(T_CTX0, compressed, ctx_slot[0])
     for d in (ld_q, ld_k, ld_v):
         d.wait()
-    wqkv[own_rows] = (wqkv[own_rows].astype(F32) * gain_a[...]).astype(BF)
+    eye = lax.broadcasted_iota(jnp.int32, (own, own), 0) == lax.broadcasted_iota(
+        jnp.int32, (own, own), 1
+    )
+    gain_cols[...] = dot(eye.astype(F32).astype(BF), gains[...], 1, 1)
+    gain_a = gain_cols[:, 0:1]
+    gain_f = gain_cols[:, 1:2]
+    wqkv[own_rows] = (wqkv[own_rows].astype(F32) * gain_a).astype(BF)
     w_send(QKV)
+    ld_m.wait()
+    row = lax.broadcasted_iota(jnp.int32, (128, 128), 0)
+    source = 2 * lax.rem(row, 64) + lax.div(row, 64)
+    pick = (lax.broadcasted_iota(jnp.int32, (128, 128), 1) == source).astype(F32).astype(BF)
+    for s in range(2):
+        split = dot(pick, att_rows[s]).astype(BF)
+        memraw[s, 0, ds(r * 64, 64), :] = split[:64]
+        memraw[s, 1, ds(r * 64, 64), :] = split[64:]
+    gather_start(T_CTX1, ctx_slot[1](r), ctx_slot[1])
+    gather_start(T_CTX2, hidden, ctx_slot[2])
+    ctx_src = (compressed, ctx_slot[1](r), hidden)
+    gf_src = lambda p: grad_fresh.at[:, :, ds(p * col, col)]
+    gf_dst = lambda p: gf.at[:, ds(p * 64, 64)]
+    swap_start(T_GF, gf_src, gf_dst)
     ld_o.wait()
     w_send(WO)
-    ld_up.wait()
-    up[own_rows] = (up[own_rows].astype(F32) * gain_f[...]).astype(BF)
+    for d in ld_up:
+        d.wait()
+    up[own_rows] = (up[own_rows].astype(F32) * gain_f).astype(BF)
     w_send(UP)
     ld_dn.wait()
     w_send(DOWN)
     for d in ld_cv:
         d.wait()
     w_send(CONV)
-    for d in ld_c:
-        d.wait()
-    ld_go.wait()
-    ld_gf.wait()
+
+    if relay:
+        for end, dz in ((0, 1), (3, 3)):
+
+            @pl.when(z == end)
+            def _():
+                for g in range(5):
+                    z_buf[g][pl.ds((dz - 1) * own, own)] = jnp.zeros((own, z_buf[g].shape[1]), BF)
+
+    before = lax.broadcasted_iota(jnp.int32, (seg, seg), 1) <= lax.broadcasted_iota(
+        jnp.int32, (seg, seg), 0
+    )
+    before = before.astype(F32).astype(BF)
+    starts = boundary[...].astype(F32).astype(BF)
+    docs = dot(before, starts, 1, 1)
+    doc_k[...] = dot(starts, before, 1, 1)
+    for s in range(2):
+        row_info[s, :, 0:1] = docs[:, s : s + 1]
+        away = docs[:, s : s + 1] + reset_flag[s].astype(F32)
+        row_info[s, :, 1:2] = jnp.where(away == 0.0, 0.0, -1e30)
 
     def norm_block(p, rank):
         def one(s):
@@ -424,6 +650,8 @@
 
     def context(p):
         op, slot = T_CTX0 + p, ctx_slot[p]
+        if p in ld_c:
+            ld_c[p].wait()
         norm_block(p, r)
         gather_forward(op, slot)
         tm_copy(slot(r1), slot(r1), op, 0, r1).wait_recv()
@@ -463,15 +691,37 @@
     w_forward(QKV)
     context(1)
     w_forward(WO)
+    w_forward_last(QKV)
     w_finish(QKV)
     project(0)
     project(1)
+    w_cross(CONV)
+
+    ld_gf.wait()
+    swap_finish(T_GF, gf_dst)
+
+    def conv_grads(i):
+        c = ds(i * 256, 256)
+        even_acc = jnp.zeros((256, 512), F32)
+        odd_acc = jnp.zeros((256, 512), F32)
+        for s in range(2):
+            g = gf[s].astype(F32)
+            at = lax.broadcasted_iota(jnp.int32, g.shape, 0)
+            ahead = jnp.where(at == 255, 0.0, pltpu.roll(g, 255, 0))
+            behind = jnp.where(at == 0, 0.0, pltpu.roll(g, 1, 0))
+            low = gf[s]
+            odd_acc += dot(memraw[s, 1, :, c], jnp.concatenate([ahead.astype(BF), low], 1), 0, 0)
+            even_acc += dot(memraw[s, 0, :, c], jnp.concatenate([low, behind.astype(BF)], 1), 0, 0)
+        l_conv[c, pl.ds(0, col)] = odd_acc[:, :col].astype(BF)
+        l_conv[c, pl.ds(col, col)] = even_acc[:, :col].astype(BF)
+        l_conv[c, pl.ds(2 * col, col)] = odd_acc[:, col:].astype(BF)
+        l_conv[c, pl.ds(3 * col, col)] = even_acc[:, col:].astype(BF)
+
+    loop(4, conv_grads)
+
+    w_forward_last(WO)
+    w_forward(UP)
     context(2)
-    go_slot = lambda p: go.at[:, ds(p * 128, 128)]
-    gather_start(T_GO, grad_out, go_slot)
-    gf_src = lambda p: grad_fresh.at[:, :, ds(p * col, col)]
-    gf_dst = lambda p: gf.at[:, ds(p * 64, 64)]
-    swap_start(T_GF, gf_src, gf_dst)
     project(2)
     w_finish(WO)
     wo_slot = lambda p: wo.at[:, ds(p * col, col)]
@@ -485,7 +735,7 @@
                 lax.broadcasted_iota(jnp.int32, shape, 0) + qt * 128
             )
             info = row_info[s, rows, :]
-            same = doc_k[s] == info[:, 0:1]
+            same = doc_k[pl.ds(s, 1), :] == info[:, 0:1]
             seen = below & same
             bias = info[:, 1:2]
             for h in range(2):
@@ -520,39 +770,18 @@
 
     attend(0)
     attend_send(0)
-    gather_forward(T_GO, go_slot)
-    w_forward(UP)
+    w_forward_last(UP)
     gather_forward(T_WO, wo_slot)
     attend(1)
     attend_send(1)
-    w_finish(UP)
-
-    swap_finish(T_GF, gf_dst)
-
-    def conv_grads(i):
-        c = ds(i * 256, 256)
-        even_acc = jnp.zeros((256, 512), F32)
-        odd_acc = jnp.zeros((256, 512), F32)
-        for s in range(2):
-            g = gf[s].astype(F32)
-            at = lax.broadcasted_iota(jnp.int32, g.shape, 0)
-            ahead = jnp.where(at == 255, 0.0, pltpu.roll(g, 255, 0))
-            behind = jnp.where(at == 0, 0.0, pltpu.roll(g, 1, 0))
-            low = gf[s]
-            odd_acc += dot(memraw[s, 1, :, c], jnp.concatenate([ahead.astype(BF), low], 1), 0, 0)
-            even_acc += dot(memraw[s, 0, :, c], jnp.concatenate([low, behind.astype(BF)], 1), 0, 0)
-        l_conv[c, pl.ds(0, col)] = odd_acc[:, :col].astype(BF)
-        l_conv[c, pl.ds(col, col)] = even_acc[:, :col].astype(BF)
-        l_conv[c, pl.ds(2 * col, col)] = odd_acc[:, col:].astype(BF)
-        l_conv[c, pl.ds(3 * col, col)] = even_acc[:, col:].astype(BF)
-
-    loop(4, conv_grads)
-    gx_start(CONV)
+    go_slot = lambda p: go.at[:, ds(p * 128, 128)]
+    gather_start(T_GO, grad_out, go_slot)
+    w_forward(DOWN)
 
     swap_finish(T_ATT0, att_dst(0))
     swap_finish(T_ATT1, att_dst(1))
     gather_finish(T_WO, wo_slot)
-    gather_finish(T_GO, go_slot)
+    ld_h.wait()
 
     def project_out(i):
         c = ds(i * 256, 256)
@@ -564,9 +793,14 @@
     for s in range(2):
         nf[s, tslot, :] = layer_norm(middle[s])[0].astype(BF)
         gather_start(T_NF0 + s, nf_slot(s)(r), nf_slot(s))
-    w_forward(DOWN)
+    w_forward_last(DOWN)
+    gather_forward(T_GO, go_slot)
+    ld_go.wait()
     for s in range(2):
         gather_forward(T_NF0 + s, nf_slot(s))
+    gather_finish(T_GO, go_slot)
+    gx_start(CONV)
+    w_finish(UP)
     w_finish(DOWN)
 
     def ffn(s):
@@ -598,7 +832,7 @@
         reduce_start(T_GNF0 + s, rows_of(gnp, s), d_b.at[s, 1], d_b.at[s, 0])
     for s in range(2):
         reduce_mid(T_GNF0 + s, rows_of(gnp, s), d_b.at[s, 1], y_b.at[s])
-    w_forward(CONV)
+    w_cross_pass(CONV)
 
     w_drain(UP)
     nf2 = nf
@@ -664,11 +898,9 @@
     loop(4, down_grads)
     gx_start(DOWN)
     swap_finish(T_GA, ga_dst)
-    gz_start(CONV)
-    w_finish(CONV)
-
-    def attend_back(s):
-        for h in range(2):
+
+    def attend_back(s, h):
+        if True:
             lanes = pl.ds(h * 128, 128)
             vl = pl.ds(col + h * 128, 128)
 
@@ -702,12 +934,17 @@
             loop(3, keys)
             qs[s, :, lanes] = t_q[...]
 
-    attend_back(0)
+    gz_start(CONV)
+    attend_back(0, 0)
     reduce_mid(T_OP, op_part, d_o.at[1], y_o)
     for s in range(2):
         reduce_mid(T_OUT0 + s, rows_of(gpre, s), d_a.at[s, 1], y_a.at[s])
+    gz_relay(CONV)
+    attend_back(0, 1)
+    attend_back(1, 0)
     gz_start(UP)
-    attend_back(1)
+    attend_back(1, 1)
+    g_final(CONV, None)
 
     reduce_drain(T_OP, op_part, d_o.at[1])
     l_o[...] = reduce_end(T_OP, op_part, d_o.at[0], y_o).astype(BF).reshape(1024, col)
@@ -739,11 +976,7 @@
     for s in range(2):
         reduce_start(T_GN0 + s, rows_of(gnp, s), d_b.at[s, 1], d_b.at[s, 0])
     ld_h = load(hidden, gm_low, 13)
-    g_final(CONV, None)
-    gz_start(DOWN)
-    for s in range(2):
-        reduce_mid(T_GN0 + s, rows_of(gnp, s), d_b.at[s, 1], y_b.at[s])
-
+    w_cross_finish(CONV)
     gather_drain(T_GO, go_slot)
     ld_w = [
         load(conv_all.at[pl.ds(i * seg, seg)], go.at[i], 14 + i) for i in range(2)
@@ -753,6 +986,8 @@
         reduce_drain(T_OUT0 + s, rows_of(gpre, s), d_a.at[s, 1])
         y_a[s] = (middle[s] + out).astype(BF)
     st_out = load(y_a, layer_out, 16)
+    for s in range(2):
+        reduce_mid(T_GN0 + s, rows_of(gnp, s), d_b.at[s, 1], y_b.at[s])
     for d in ld_w:
         d.wait()
     swap_drain(T_GA, ga_src)
@@ -778,9 +1013,6 @@
     swap_start(T_FR, fr_src, fr_dst)
     st_fr = load(fr_src(r), fr_dst(r), 17)
 
-    g_final(UP, gain_f)
-    gz_start(WO)
-    gz_start(QKV)
     for s in range(2):
         c = reduce_end(T_GN0 + s, rows_of(gnp, s), d_b.at[s, 0], y_b.at[s])
         if s == 0:
@@ -788,9 +1020,22 @@
         u, inv = layer_norm(gm_low[s].astype(F32))
         gm[s] = gm[s] + norm_back(c, u, inv)
     st_gi = load(gm, grad_input, 18)
+    gz_relay(UP)
+    g_pass(CONV)
+    gz_start(DOWN)
+    g_final(UP, gain_f)
+    gz_relay(DOWN)
+    gz_start(WO)
+    gz_start(QKV)
+    g_pass(UP)
+    gz_relay(WO)
     g_final(DOWN, None)
+    gz_relay(QKV)
     g_final(WO, None)
+    g_pass(DOWN)
     g_final(QKV, gain_a)
+    g_pass(WO)
+    g_pass(QKV)
 
     for p in range(3):
         tm_copy(ctx_src[p], ctx_slot[p](r), T_CTX0 + p, 0, r1).wait_send()
@@ -803,10 +1048,24 @@
     swap_drain(T_FR, fr_src)
     for d in (st_out, st_fr, st_gi):
         d.wait()
-    for g in (QKV, WO, CONV):
-        w_drain(g)
+    w_drain(QKV)
+    w_drain(WO)
+    w_cross_drain(CONV)
     for g in range(5):
         g_drain(g)
+
+
+def widen(*refs):
+    ins, weights, outs = refs[:10], refs[10:14], refs[14:]
+    for src, dst in zip(ins, outs):
+        dst[...] = src[...].astype(dst.dtype)
+    total = jnp.zeros(outs[10].shape, F32)
+    for w, g in zip(weights[:3], ins[3:6]):
+        total += jnp.sum(w[...].astype(F32) * g[...].astype(F32), axis=-1, keepdims=True)
+    outs[10][...] = total
+    outs[11][...] = jnp.sum(
+        weights[3][...].astype(F32) * ins[7][...].astype(F32), axis=-1, keepdims=True
+    )
 
 
 def per_device(
@@ -835,26 +1094,22 @@
     cols = width // PARTS
     n_z = groups // 2
     ff_rows = down_weight.shape[0] // PARTS
-    up_own = lax.dynamic_index_in_dim(
-        up_weight.reshape(own, groups, PARTS, ff_rows), rank, 2, keepdims=False
-    ).reshape(own, groups * ff_rows)
-    halves = memory.reshape(streams, seg_rows // 2, 2, width).transpose(0, 2, 1, 3)
-    gain_a = attn_gain.astype(F32)[:, None]
-    gain_f = ffn_gain.astype(F32)[:, None]
-    spots = jnp.arange(seg)
-    places = jnp.concatenate([spots, seg + spots[::2], seg + spots[1::2], 2 * seg + spots])
+    pieces = groups if ff_rows % 128 == 0 else 1
+    up_in = up_weight
+    if pieces == 1:
+        up_in = lax.dynamic_index_in_dim(
+            up_weight.reshape(own, groups, PARTS, ff_rows), rank, 2, keepdims=False
+        ).reshape(own, groups * ff_rows)
+    gains = jnp.stack([attn_gain, ffn_gain])
+    spots = np.arange(seg)
+    places = np.concatenate([spots, seg + spots[::2], seg + spots[1::2], 2 * seg + spots])
     half = HEAD_DIM // 2
-    frequency = 10000.0 ** (-jnp.arange(half).astype(F32) * 2.0 / HEAD_DIM)
-    angles = places.astype(F32)[:, None] * frequency[None, :]
-    cosine = jnp.cos(angles)
-    sine = jnp.sin(angles)
-    cosines = jnp.concatenate([cosine, cosine], axis=1)
-    sines = jnp.concatenate([-sine, sine], axis=1)
-    documents = jnp.cumsum(boundary, axis=1)
-    memory_ok = (reset_flag[:, None] == 0) & (documents == 0)
-    docs = documents.astype(F32)
-    row_info = jnp.stack([docs, jnp.where(memory_ok, 0.0, -1e30)], axis=2)
-    doc_k = docs[:, None, :]
+    frequency = 10000.0 ** (-np.arange(half) * 2.0 / HEAD_DIM)
+    angles = places[:, None] * frequency[None, :]
+    cosine = np.cos(angles).astype(np.float32)
+    sine = np.sin(angles).astype(np.float32)
+    cosines = np.concatenate([cosine, cosine], axis=1)
+    sines = np.concatenate([-sine, sine], axis=1)
 
     hbm = pl.BlockSpec(memory_space=pl.ANY)
     vmem = pl.BlockSpec(memory_space=pltpu.VMEM)
@@ -867,7 +1122,7 @@
         jax.ShapeDtypeStruct((own, width), BF),
         jax.ShapeDtypeStruct((own, width), BF),
         jax.ShapeDtypeStruct((own, width), BF),
-        jax.ShapeDtypeStruct((PARTS, own, width), BF),
+        jax.ShapeDtypeStruct((own, width * PARTS), BF),
         jax.ShapeDtypeStruct((PARTS * own, width), BF),
         jax.ShapeDtypeStruct((4, own, width), BF),
         jax.ShapeDtypeStruct((width, width), BF),
@@ -914,26 +1169,31 @@
         ]
         + [v((n_z * own, c)) for c in wide]
         + [v(((n_z - 1) * own, c)) for c in wide]
+        + [v((own, c)) for c in wide]
         + [
             v((3 * seg, HEAD_DIM)),
             v((seg, HEAD_DIM)),
-            sem((20,)),
+            v((own, 2), F32),
+            v((streams, seg, 2), F32),
+            v((streams, seg), F32),
+            sem((18 + pieces,)),
             sem((T_COUNT, 3)),
             sem((T_COUNT, 3)),
-            sem((5, 2 * n_z)),
-            sem((5, 2 * n_z)),
+            sem((5, 2 * n_z + 1)),
+            sem((5, 2 * n_z + 1)),
             sem((5, n_z)),
             sem((5, n_z)),
             sem((5, n_z)),
             sem((5, n_z)),
-            sem((10, 3)),
-            sem((10, 3)),
+            sem((9 + pieces, 3)),
+            sem((9 + pieces, 3)),
+            sem((9 + pieces,)),
         ]
     )
     results = pl.pallas_call(
-        functools.partial(kernel, n_z, own),
+        functools.partial(kernel, n_z, own, pieces),
         out_shape=out_shape,
-        in_specs=[hbm] * 12 + [vmem] * 6,
+        in_specs=[hbm] * 12 + [pl.BlockSpec(memory_space=pltpu.SMEM)] + [vmem] * 4,
         out_specs=tuple([hbm] * len(out_shape)),
         scratch_shapes=scratch,
         compiler_params=pltpu.CompilerParams(
@@ -942,46 +1202,55 @@
         name="layer",
     )(
         hidden,
-        halves,
+        memory,
         compressed,
         query_weight,
         key_weight,
         value_weight,
         output_weight,
-        up_own,
+        up_in,
         down_weight,
         conv_weight,
         grad_out,
         grad_fresh,
-        gain_a,
-        gain_f,
+        reset_flag,
+        boundary,
+        gains,
         cosines,
         sines,
-        row_info,
-        doc_k,
     )
-    layer_out, fresh, grad_input, g_q, g_k, g_v, g_o, g_up, g_down, g_conv, _ = results
-    wide = lambda t: t.astype(F32)
-    g_up = g_up.reshape(PARTS, own, groups, ff_rows).transpose(1, 2, 0, 3).reshape(up_weight.shape)
-    g_q, g_k, g_v, g_o, g_up, g_down, g_conv = map(wide, (g_q, g_k, g_v, g_o, g_up, g_down, g_conv))
-    attn_gain_grad = jnp.sum(
-        wide(query_weight) * g_q + wide(key_weight) * g_k + wide(value_weight) * g_v, axis=1
-    ) / wide(attn_gain)
-    ffn_gain_grad = jnp.sum(wide(up_weight) * g_up, axis=1) / wide(ffn_gain)
-    return (
-        layer_out,
-        fresh,
-        grad_input,
-        g_q,
-        g_k,
-        g_v,
-        g_o,
-        g_up,
-        g_down,
-        g_conv,
-        attn_gain_grad,
-        ffn_gain_grad,
-    )
+    g_up = results[7]
+    if pieces == 1:
+        g_up = (
+            g_up.reshape(own, PARTS, groups, ff_rows)
+            .transpose(0, 2, 1, 3)
+            .reshape(up_weight.shape)
+        )
+    steps = max(1, own // 32)
+    moved = [*results[:7], g_up, *results[8:10]]
+    weights = (query_weight, key_weight, value_weight, up_weight)
+
+    def cut(t):
+        shape = list(t.shape)
+        dim = len(shape) - 2
+        shape[dim] //= steps
+        return pl.BlockSpec(tuple(shape), lambda i: (0,) * dim + (i, 0))
+
+    out_types = (BF, BF) + (F32,) * 8
+    sums = jax.ShapeDtypeStruct((own, 1), F32)
+    done = pl.pallas_call(
+        widen,
+        grid=(steps,),
+        out_shape=tuple(jax.ShapeDtypeStruct(t.shape, d) for t, d in zip(moved, out_types))
+        + (sums, sums),
+        in_specs=[cut(t) for t in moved] + [cut(t) for t in weights],
+        out_specs=tuple([cut(t) for t in moved] + [cut(sums)] * 2),
+        compiler_params=pltpu.CompilerParams(vmem_limit_bytes=64000 * 1024),
+        name="widen",
+    )(*moved, *weights)
+    attn_gain_grad = done[10][:, 0] / attn_gain.astype(F32)
+    ffn_gain_grad = done[11][:, 0] / ffn_gain.astype(F32)
+    return tuple(done[:10]) + (attn_gain_grad, ffn_gain_grad)
 
 
 def solution(mesh):

time: 306 us -> 259 us (0.85)
  Pallas kernels: 272 us -> 253 us
  local copies, waits for them, and re-layouts: 17 us -> 0.01 us
  other arithmetic: 15.9 us -> 3.61 us
    pallas_call x1 -> x2, Pallas kernels: 272 us -> 253 us  [the longest x1 246 us: per_device(): pl.pallas_call(functools.partial(kernel, n_z, own, pieces), out_shape=out...]
    convert_element_type x4 -> x0, local copies, waits for them, and re-layouts: 5.26 us -> none  [the longest x3 4.91 us: per_device(): wide = lambda t: t.astype(F32)]
    unnamed x34 -> x4, local copies, waits for them, and re-layouts: 5.22 us -> 0.01 us
    convert_element_type x5 -> x0, other arithmetic: 4.06 us -> none  [the longest x3 3.97 us: per_device(): wide = lambda t: t.astype(F32)]
where the time goes in v3:
time: 259 us; the launch traced here: 257 us
  Pallas kernels  253 us (98%)
  other arithmetic  3.61 us (1%)
    pallas_call x1, Pallas kernels, per_device(): pl.pallas_call(functools.partial(kernel, n_z, own, pieces), out_shape=out...  246 us
    pallas_call x1, Pallas kernels, per_device(): pl.pallas_call(widen, grid=(steps,), out_shape=tuple((jax.ShapeDtypeStruc...  7.59 us

profile of v3, /device:TPU:26, one launch (start us, length us, event | category | flops | bytes accessed | tf_op | source)
XLA Modules:
  0.0 257.4 jit_solution(10919352031430389086)
XLA Ops:
  0.6 1.2 pad_maximum_fusion.gains
  1.8 245.5 %layer.1 = (bf16[2,128,1024]{2,1,0:T(8,128)(2,1)}, bf16[2,64,1024]{2,1,0:T(8,128)(2,1)}, f32[2,128,1024]{2,1,0:T(8,128)}, bf16[128,1024]{1,0:T(8,128)(2,1)}, bf1...) custom-call(bf16[2,128,1024]{2,1,0:T(8,128)(2,1)} %hidden.1, ...), custom_call_target="tpu_custom_call" | custom-call | tf_op jit(solution)/shard_map/layer/pallas_call | solution.py:1193
  247.4 0.0 copy-start
  247.4 0.0 copy-start.1
  247.4 7.6 %widen.1 = (bf16[2,128,1024]{2,1,0:T(8,128)(2,1)}, bf16[2,64,1024]{2,1,0:T(8,128)(2,1)}, f32[2,128,1024]{2,1,0:T(8,128)}, f32[128,1024]{1,0:T(8,128)}, f32[128,1...) custom-call(bf16[2,128,1024]{2,1,0:T(8,128)(2,1)} %get-tuple-element, ...), custom_call_target="tpu_custom_call" | custom-call | tf_op jit(solution)/shard_map/widen/pallas_call | solution.py:1241
  255.0 0.9 reduce
  255.9 1.0 reduce.1
  256.9 0.0 copy-done
  256.9 0.0 copy-done.1
  256.9 0.5 convert_divide_fusion
Async XLA Ops:
  247.4 9.5 %copy-start = (bf16[128]{0:T(256)(128)(2,1)S(1)}, bf16[128]{0:T(256)(128)(2,1)}, u32[]{:S(2)}) copy-start(bf16[128]{0:T(256)(128)(2,1)} %param.31) | copy-start | bytes 772
  247.4 9.5 %copy-start.1 = (bf16[128]{0:T(256)(128)(2,1)S(1)}, bf16[128]{0:T(256)(128)(2,1)}, u32[]{:S(2)}) copy-start(bf16[128]{0:T(256)(128)(2,1)} %param.30) | copy-start | bytes 772

commit v4 on v3

--- a/solution.py
+++ b/solution.py
@@ -296,8 +296,10 @@
         zz = zpeer(dz)
         return (z + 3 != zz) & (zz + 3 != z)
 
-    def w_send(g):
+    def w_send_x(g):
         w_copy(g, st, 0, xn).start()
+
+    def w_send_z(g):
         if relay:
             for dz in (2, 1, 3):
 
@@ -422,7 +424,11 @@
         )
 
     def gx_start(g):
-        loop(n_z, lambda i: gx_copy(g, zpeer(i + 1)).start())
+        if relay:
+            for dz in (1, 3, 2, 0):
+                gx_copy(g, zpeer(dz)).start()
+        else:
+            loop(n_z, lambda i: gx_copy(g, zpeer(i + 1)).start())
 
     def gz_copy(g, dz, zz):
         return pltpu.make_async_remote_copy(
@@ -587,7 +593,8 @@
     gain_a = gain_cols[:, 0:1]
     gain_f = gain_cols[:, 1:2]
     wqkv[own_rows] = (wqkv[own_rows].astype(F32) * gain_a).astype(BF)
-    w_send(QKV)
+    w_send_x(QKV)
+    w_send_z(QKV)
     ld_m.wait()
     row = lax.broadcasted_iota(jnp.int32, (128, 128), 0)
     source = 2 * lax.rem(row, 64) + lax.div(row, 64)
@@ -603,17 +610,14 @@
     gf_dst = lambda p: gf.at[:, ds(p * 64, 64)]
     swap_start(T_GF, gf_src, gf_dst)
     ld_o.wait()
-    w_send(WO)
+    w_send_x(WO)
+    w_send_z(WO)
     for d in ld_up:
         d.wait()
     up[own_rows] = (up[own_rows].astype(F32) * gain_f).astype(BF)
-    w_send(UP)
+    w_send_z(UP)
     ld_dn.wait()
-    w_send(DOWN)
-    for d in ld_cv:
-        d.wait()
-    w_send(CONV)
-
+    w_send_z(DOWN)
     if relay:
         for end, dz in ((0, 1), (3, 3)):
 
@@ -648,12 +652,14 @@
 
         loop(2, one)
 
-    def context(p):
+    def context(p, meanwhile=None):
         op, slot = T_CTX0 + p, ctx_slot[p]
         if p in ld_c:
             ld_c[p].wait()
         norm_block(p, r)
         gather_forward(op, slot)
+        if meanwhile is not None:
+            meanwhile()
         tm_copy(slot(r1), slot(r1), op, 0, r1).wait_recv()
         norm_block(p, r1)
         tm_copy(slot(r3), slot(r3), op, 2, r1).wait_recv()
@@ -689,13 +695,31 @@
 
     context(0)
     w_forward(QKV)
+    w_forward(WO)
+    for d in ld_cv:
+        d.wait()
+    w_send_x(CONV)
+    w_send_z(CONV)
     context(1)
-    w_forward(WO)
     w_forward_last(QKV)
+    w_forward_last(WO)
+    w_send_x(UP)
+    w_send_x(DOWN)
     w_finish(QKV)
     project(0)
     project(1)
+    w_forward(UP)
     w_cross(CONV)
+    wo_slot = lambda p: wo.at[:, ds(p * col, col)]
+    go_slot = lambda p: go.at[:, ds(p * 128, 128)]
+
+    def gather_wo():
+        w_finish(WO)
+        gather_start(T_WO, wo_slot(r), wo_slot)
+
+    context(2, gather_wo)
+    w_forward_last(UP)
+    project(2)
 
     ld_gf.wait()
     swap_finish(T_GF, gf_dst)
@@ -718,14 +742,6 @@
         l_conv[c, pl.ds(3 * col, col)] = even_acc[:, col:].astype(BF)
 
     loop(4, conv_grads)
-
-    w_forward_last(WO)
-    w_forward(UP)
-    context(2)
-    project(2)
-    w_finish(WO)
-    wo_slot = lambda p: wo.at[:, ds(p * col, col)]
-    gather_start(T_WO, wo_slot(r), wo_slot)
 
     def attend(s):
         def one(qt):
@@ -768,15 +784,16 @@
         swap_start(T_ATT0 + s, att_src(s), att_dst(s))
         att_rows[s, :, rcol] = att_own[s, tslot, :]
 
+    gather_start(T_GO, grad_out, go_slot)
     attend(0)
     attend_send(0)
-    w_forward_last(UP)
+    w_forward(DOWN)
     gather_forward(T_WO, wo_slot)
     attend(1)
     attend_send(1)
-    go_slot = lambda p: go.at[:, ds(p * 128, 128)]
-    gather_start(T_GO, grad_out, go_slot)
-    w_forward(DOWN)
+    w_forward_last(DOWN)
+    gx_start(CONV)
+    gather_forward(T_GO, go_slot)
 
     swap_finish(T_ATT0, att_dst(0))
     swap_finish(T_ATT1, att_dst(1))
@@ -793,13 +810,10 @@
     for s in range(2):
         nf[s, tslot, :] = layer_norm(middle[s])[0].astype(BF)
         gather_start(T_NF0 + s, nf_slot(s)(r), nf_slot(s))
-    w_forward_last(DOWN)
-    gather_forward(T_GO, go_slot)
     ld_go.wait()
     for s in range(2):
         gather_forward(T_NF0 + s, nf_slot(s))
     gather_finish(T_GO, go_slot)
-    gx_start(CONV)
     w_finish(UP)
     w_finish(DOWN)
 
@@ -846,6 +860,7 @@
 
     loop(4, up_grads)
     gx_start(UP)
+    gz_start(CONV)
 
     for s in range(2):
         c = reduce_end(T_GNF0 + s, rows_of(gnp, s), d_b.at[s, 0], y_b.at[s])
@@ -897,6 +912,7 @@
 
     loop(4, down_grads)
     gx_start(DOWN)
+    gz_relay(CONV)
     swap_finish(T_GA, ga_dst)
 
     def attend_back(s, h):
@@ -934,17 +950,17 @@
             loop(3, keys)
             qs[s, :, lanes] = t_q[...]
 
-    gz_start(CONV)
     attend_back(0, 0)
     reduce_mid(T_OP, op_part, d_o.at[1], y_o)
+    gz_start(UP)
+    attend_back(0, 1)
     for s in range(2):
         reduce_mid(T_OUT0 + s, rows_of(gpre, s), d_a.at[s, 1], y_a.at[s])
-    gz_relay(CONV)
-    attend_back(0, 1)
+    g_final(CONV, None)
     attend_back(1, 0)
-    gz_start(UP)
+    gz_relay(UP)
     attend_back(1, 1)
-    g_final(CONV, None)
+    gz_start(DOWN)
 
     reduce_drain(T_OP, op_part, d_o.at[1])
     l_o[...] = reduce_end(T_OP, op_part, d_o.at[0], y_o).astype(BF).reshape(1024, col)
@@ -963,6 +979,8 @@
 
     loop(4, kv_grads)
     gx_start(QKV)
+    g_final(UP, gain_f)
+    gz_relay(DOWN)
 
     def hidden_grads(i):
         s = lax.div(i, 4)
@@ -976,6 +994,11 @@
     for s in range(2):
         reduce_start(T_GN0 + s, rows_of(gnp, s), d_b.at[s, 1], d_b.at[s, 0])
     ld_h = load(hidden, gm_low, 13)
+    g_pass(CONV)
+    for s in range(2):
+        reduce_mid(T_GN0 + s, rows_of(gnp, s), d_b.at[s, 1], y_b.at[s])
+    gz_start(WO)
+    gz_relay(WO)
     w_cross_finish(CONV)
     gather_drain(T_GO, go_slot)
     ld_w = [
@@ -986,8 +1009,6 @@
         reduce_drain(T_OUT0 + s, rows_of(gpre, s), d_a.at[s, 1])
         y_a[s] = (middle[s] + out).astype(BF)
     st_out = load(y_a, layer_out, 16)
-    for s in range(2):
-        reduce_mid(T_GN0 + s, rows_of(gnp, s), d_b.at[s, 1], y_b.at[s])
     for d in ld_w:
         d.wait()
     swap_drain(T_GA, ga_src)
@@ -1012,6 +1033,10 @@
     fr_dst = lambda p: fresh_out.at[:, :, ds(p * col, col)]
     swap_start(T_FR, fr_src, fr_dst)
     st_fr = load(fr_src(r), fr_dst(r), 17)
+    gz_start(QKV)
+    g_pass(UP)
+    g_final(DOWN, None)
+    gz_relay(QKV)
 
     for s in range(2):
         c = reduce_end(T_GN0 + s, rows_of(gnp, s), d_b.at[s, 0], y_b.at[s])
@@ -1020,17 +1045,6 @@
         u, inv = layer_norm(gm_low[s].astype(F32))
         gm[s] = gm[s] + norm_back(c, u, inv)
     st_gi = load(gm, grad_input, 18)
-    gz_relay(UP)
-    g_pass(CONV)
-    gz_start(DOWN)
-    g_final(UP, gain_f)
-    gz_relay(DOWN)
-    gz_start(WO)
-    gz_start(QKV)
-    g_pass(UP)
-    gz_relay(WO)
-    g_final(DOWN, None)
-    gz_relay(QKV)
     g_final(WO, None)
     g_pass(DOWN)
     g_final(QKV, gain_a)

time: 259 us -> 213 us (0.82)
  Pallas kernels: 253 us -> 206 us
    pallas_call x1, Pallas kernels: 246 us -> 198 us  [per_device(): pl.pallas_call(functools.partial(kernel, n_z, own, pieces), out_shape=out...]
where the time goes in v4:
time: 213 us; the launch traced here: 210 us
  Pallas kernels  206 us (97%)
  other arithmetic  3.61 us (2%)
    pallas_call x1, Pallas kernels, per_device(): pl.pallas_call(functools.partial(kernel, n_z, own, pieces), out_shape=out...  198 us
    pallas_call x1, Pallas kernels, per_device(): pl.pallas_call(widen, grid=(steps,), out_shape=tuple((jax.ShapeDtypeStruc...  7.59 us

profile of v4, /device:TPU:26, one launch (start us, length us, event | category | flops | bytes accessed | tf_op | source)
XLA Modules:
  0.0 210.3 jit_solution(7241213906215546901)
XLA Ops:
  0.6 1.2 pad_maximum_fusion.gains
  1.8 198.4 %layer.1 = (bf16[2,128,1024]{2,1,0:T(8,128)(2,1)}, bf16[2,64,1024]{2,1,0:T(8,128)(2,1)}, f32[2,128,1024]{2,1,0:T(8,128)}, bf16[128,1024]{1,0:T(8,128)(2,1)}, bf1...) custom-call(bf16[2,128,1024]{2,1,0:T(8,128)(2,1)} %hidden.1, ...), custom_call_target="tpu_custom_call" | custom-call | tf_op jit(solution)/shard_map/layer/pallas_call | solution.py:1207
  200.3 0.0 copy-start
  200.3 0.0 copy-start.1
  200.3 7.6 %widen.1 = (bf16[2,128,1024]{2,1,0:T(8,128)(2,1)}, bf16[2,64,1024]{2,1,0:T(8,128)(2,1)}, f32[2,128,1024]{2,1,0:T(8,128)}, f32[128,1024]{1,0:T(8,128)}, f32[128,1...) custom-call(bf16[2,128,1024]{2,1,0:T(8,128)(2,1)} %get-tuple-element, ...), custom_call_target="tpu_custom_call" | custom-call | tf_op jit(solution)/shard_map/widen/pallas_call | solution.py:1255
  207.9 0.9 reduce
  208.8 1.0 reduce.1
  209.8 0.0 copy-done
  209.8 0.0 copy-done.1
  209.8 0.5 convert_divide_fusion
Async XLA Ops:
  200.3 9.5 %copy-start = (bf16[128]{0:T(256)(128)(2,1)S(1)}, bf16[128]{0:T(256)(128)(2,1)}, u32[]{:S(2)}) copy-start(bf16[128]{0:T(256)(128)(2,1)} %param.31) | copy-start | bytes 772
  200.3 9.5 %copy-start.1 = (bf16[128]{0:T(256)(128)(2,1)S(1)}, bf16[128]{0:T(256)(128)(2,1)}, u32[]{:S(2)}) copy-start(bf16[128]{0:T(256)(128)(2,1)} %param.30) | copy-start | bytes 772

commit v5 on v4

--- a/solution.py
+++ b/solution.py
@@ -16,8 +16,8 @@
 
 QKV, WO, UP, DOWN, CONV = range(5)
 (T_CTX0, T_CTX1, T_CTX2, T_GO, T_GF, T_WO, T_ATT0, T_ATT1, T_NF0, T_NF1, T_GNF0, T_GNF1) = range(12)
-(T_OUT0, T_OUT1, T_GA, T_OP, T_GN0, T_GN1, T_FR) = range(12, 19)
-T_COUNT = 19
+(T_OUT0, T_OUT1, T_GA, T_OP, T_GN0, T_GN1, T_FR, T_GO1) = range(12, 20)
+T_COUNT = 20
 
 
 def dot(a, b, ca=1, cb=0):
@@ -66,11 +66,11 @@
     conv_weight,
     grad_out,
     grad_fresh,
+    boundary_in,
+    gains_in,
+    cosines_in,
+    sines_in,
     reset_flag,
-    boundary,
-    gains,
-    cosines,
-    sines,
     layer_out,
     fresh_out,
     grad_input,
@@ -131,6 +131,10 @@
     gain_cols,
     row_info,
     doc_k,
+    boundary,
+    gains,
+    cosines,
+    sines,
     loc,
     tm_s,
     tm_r,
@@ -169,6 +173,8 @@
 
     own_rows = ds(st * own, own)
     rcol = ds(r * col, col)
+    ld_g = load(gains_in, gains, 16)
+    ld_b = load(boundary_in, boundary, 17)
     ld_q = load(query_weight.at[:, rcol], wqkv.at[own_rows, pl.ds(0, col)], 0)
     ld_k = load(key_weight.at[:, rcol], wqkv.at[own_rows, pl.ds(col, col)], 1)
     ld_v = load(value_weight.at[:, rcol], wqkv.at[own_rows, pl.ds(2 * col, col)], 2)
@@ -197,6 +203,7 @@
         2: load(hidden, unit.at[2, :, tslot], 12),
     }
     ld_h = load(hidden, gm_low, 13)
+    ld_t = [load(cosines_in, cosines, 18 + pieces), load(sines_in, sines, 19 + pieces)]
     ld_go = load(grad_out, go.at[:, tslot], 14)
     ld_gf = load(grad_fresh.at[:, :, rcol], gf.at[:, ds(r * 64, 64)], 15)
 
@@ -211,6 +218,30 @@
         )
 
     loop(n_z - 1, greet)
+
+    ld_g.wait()
+    eye = lax.broadcasted_iota(jnp.int32, (own, own), 0) == lax.broadcasted_iota(
+        jnp.int32, (own, own), 1
+    )
+    gain_cols[...] = dot(eye.astype(F32).astype(BF), gains[...].astype(BF), 1, 1)
+    gain_a = gain_cols[:, 0:1]
+    gain_f = gain_cols[:, 1:2]
+    for d in (ld_q, ld_k, ld_v):
+        d.wait()
+    wqkv[own_rows] = (wqkv[own_rows].astype(F32) * gain_a).astype(BF)
+    ld_m.wait()
+    row = lax.broadcasted_iota(jnp.int32, (128, 128), 0)
+    source = 2 * lax.rem(row, 64) + lax.div(row, 64)
+    pick = (lax.broadcasted_iota(jnp.int32, (128, 128), 1) == source).astype(F32).astype(BF)
+    for s in range(2):
+        split = dot(pick, att_rows[s]).astype(BF)
+        memraw[s, 0, ds(r * 64, 64), :] = split[:64]
+        memraw[s, 1, ds(r * 64, 64), :] = split[64:]
+    for d in ld_up:
+        d.wait()
+    up[own_rows] = (up[own_rows].astype(F32) * gain_f).astype(BF)
+    for d in (ld_o, ld_dn):
+        d.wait()
     pl.semaphore_wait(barrier, 4 + n_z - 1)
 
     def tm_copy(src, dst, op, i, peer):
@@ -584,39 +615,17 @@
         lambda p: unit.at[2, :, ds(p * 128, 128)],
     )
     gather_start(T_CTX0, compressed, ctx_slot[0])
-    for d in (ld_q, ld_k, ld_v):
-        d.wait()
-    eye = lax.broadcasted_iota(jnp.int32, (own, own), 0) == lax.broadcasted_iota(
-        jnp.int32, (own, own), 1
-    )
-    gain_cols[...] = dot(eye.astype(F32).astype(BF), gains[...], 1, 1)
-    gain_a = gain_cols[:, 0:1]
-    gain_f = gain_cols[:, 1:2]
-    wqkv[own_rows] = (wqkv[own_rows].astype(F32) * gain_a).astype(BF)
     w_send_x(QKV)
     w_send_z(QKV)
-    ld_m.wait()
-    row = lax.broadcasted_iota(jnp.int32, (128, 128), 0)
-    source = 2 * lax.rem(row, 64) + lax.div(row, 64)
-    pick = (lax.broadcasted_iota(jnp.int32, (128, 128), 1) == source).astype(F32).astype(BF)
-    for s in range(2):
-        split = dot(pick, att_rows[s]).astype(BF)
-        memraw[s, 0, ds(r * 64, 64), :] = split[:64]
-        memraw[s, 1, ds(r * 64, 64), :] = split[64:]
     gather_start(T_CTX1, ctx_slot[1](r), ctx_slot[1])
     gather_start(T_CTX2, hidden, ctx_slot[2])
     ctx_src = (compressed, ctx_slot[1](r), hidden)
     gf_src = lambda p: grad_fresh.at[:, :, ds(p * col, col)]
     gf_dst = lambda p: gf.at[:, ds(p * 64, 64)]
     swap_start(T_GF, gf_src, gf_dst)
-    ld_o.wait()
     w_send_x(WO)
     w_send_z(WO)
-    for d in ld_up:
-        d.wait()
-    up[own_rows] = (up[own_rows].astype(F32) * gain_f).astype(BF)
     w_send_z(UP)
-    ld_dn.wait()
     w_send_z(DOWN)
     if relay:
         for end, dz in ((0, 1), (3, 3)):
@@ -630,6 +639,7 @@
         jnp.int32, (seg, seg), 0
     )
     before = before.astype(F32).astype(BF)
+    ld_b.wait()
     starts = boundary[...].astype(F32).astype(BF)
     docs = dot(before, starts, 1, 1)
     doc_k[...] = dot(starts, before, 1, 1)
@@ -700,6 +710,8 @@
         d.wait()
     w_send_x(CONV)
     w_send_z(CONV)
+    for d in ld_t:
+        d.wait()
     context(1)
     w_forward_last(QKV)
     w_forward_last(WO)
@@ -711,7 +723,7 @@
     w_forward(UP)
     w_cross(CONV)
     wo_slot = lambda p: wo.at[:, ds(p * col, col)]
-    go_slot = lambda p: go.at[:, ds(p * 128, 128)]
+    go_slot = lambda s: lambda p: go.at[s, ds(p * 128, 128)]
 
     def gather_wo():
         w_finish(WO)
@@ -784,7 +796,7 @@
         swap_start(T_ATT0 + s, att_src(s), att_dst(s))
         att_rows[s, :, rcol] = att_own[s, tslot, :]
 
-    gather_start(T_GO, grad_out, go_slot)
+    gather_start(T_GO, grad_out.at[0], go_slot(0))
     attend(0)
     attend_send(0)
     w_forward(DOWN)
@@ -793,7 +805,7 @@
     attend_send(1)
     w_forward_last(DOWN)
     gx_start(CONV)
-    gather_forward(T_GO, go_slot)
+    gather_forward(T_GO, go_slot(0))
 
     swap_finish(T_ATT0, att_dst(0))
     swap_finish(T_ATT1, att_dst(1))
@@ -810,10 +822,10 @@
     for s in range(2):
         nf[s, tslot, :] = layer_norm(middle[s])[0].astype(BF)
         gather_start(T_NF0 + s, nf_slot(s)(r), nf_slot(s))
+    gather_start(T_GO1, grad_out.at[1], go_slot(1))
     ld_go.wait()
-    for s in range(2):
-        gather_forward(T_NF0 + s, nf_slot(s))
-    gather_finish(T_GO, go_slot)
+    gather_forward(T_NF0, nf_slot(0))
+    gather_finish(T_GO, go_slot(0))
     w_finish(UP)
     w_finish(DOWN)
 
@@ -840,14 +852,25 @@
     def rows_of(buf, s):
         return lambda p: buf.at[pl.ds(pl.multiple_of(s * seg + p * 128, 128), 128)]
 
-    for s in range(2):
-        gather_finish(T_NF0 + s, nf_slot(s))
-        ffn(s)
+    def gnf_start(s):
         reduce_start(T_GNF0 + s, rows_of(gnp, s), d_b.at[s, 1], d_b.at[s, 0])
-    for s in range(2):
+
+    def gnf_mid(s):
         reduce_mid(T_GNF0 + s, rows_of(gnp, s), d_b.at[s, 1], y_b.at[s])
+
+    gather_finish(T_NF0, nf_slot(0))
+    gather_forward(T_NF1, nf_slot(1))
+    ffn(0)
+    gnf_start(0)
+    gather_forward(T_GO1, go_slot(1))
+    gnf_mid(0)
+    gather_finish(T_NF1, nf_slot(1))
+    gather_finish(T_GO1, go_slot(1))
+    ffn(1)
+    gnf_start(1)
+    gnf_mid(1)
+
     w_cross_pass(CONV)
-
     w_drain(UP)
     nf2 = nf
 
@@ -913,6 +936,7 @@
     loop(4, down_grads)
     gx_start(DOWN)
     gz_relay(CONV)
+    reduce_mid(T_OP, op_part, d_o.at[1], y_o)
     swap_finish(T_GA, ga_dst)
 
     def attend_back(s, h):
@@ -951,11 +975,10 @@
             qs[s, :, lanes] = t_q[...]
 
     attend_back(0, 0)
-    reduce_mid(T_OP, op_part, d_o.at[1], y_o)
+    for s in range(2):
+        reduce_mid(T_OUT0 + s, rows_of(gpre, s), d_a.at[s, 1], y_a.at[s])
     gz_start(UP)
     attend_back(0, 1)
-    for s in range(2):
-        reduce_mid(T_OUT0 + s, rows_of(gpre, s), d_a.at[s, 1], y_a.at[s])
     g_final(CONV, None)
     attend_back(1, 0)
     gz_relay(UP)
@@ -1000,7 +1023,8 @@
     gz_start(WO)
     gz_relay(WO)
     w_cross_finish(CONV)
-    gather_drain(T_GO, go_slot)
+    gather_drain(T_GO, go_slot(0))
+    gather_drain(T_GO1, go_slot(1))
     ld_w = [
         load(conv_all.at[pl.ds(i * seg, seg)], go.at[i], 14 + i) for i in range(2)
     ]
@@ -1069,17 +1093,30 @@
         g_drain(g)
 
 
-def widen(*refs):
-    ins, weights, outs = refs[:10], refs[10:14], refs[14:]
+def widen(steps, *refs):
+    ins, weights, gains, outs, kept = refs[:10], refs[10:14], refs[14], refs[15:27], refs[27]
     for src, dst in zip(ins, outs):
         dst[...] = src[...].astype(dst.dtype)
-    total = jnp.zeros(outs[10].shape, F32)
+    step = pl.program_id(0)
+    block = weights[0].shape[0]
+    rows = pl.ds(pl.multiple_of(step * block, block), block)
+    total = jnp.zeros((block, 1), F32)
     for w, g in zip(weights[:3], ins[3:6]):
         total += jnp.sum(w[...].astype(F32) * g[...].astype(F32), axis=-1, keepdims=True)
-    outs[10][...] = total
-    outs[11][...] = jnp.sum(
+    kept[rows, 0:1] = total
+    kept[rows, 1:2] = jnp.sum(
         weights[3][...].astype(F32) * ins[7][...].astype(F32), axis=-1, keepdims=True
     )
+
+    @pl.when(step == steps - 1)
+    def _():
+        own = kept.shape[0]
+        eye = lax.broadcasted_iota(jnp.int32, (own, own), 0) == lax.broadcasted_iota(
+            jnp.int32, (own, own), 1
+        )
+        for i in range(2):
+            line = jnp.sum(jnp.where(eye, kept[:, i : i + 1], 0.0), axis=0, keepdims=True)
+            outs[10 + i][...] = line / gains[i : i + 1, :]
 
 
 def per_device(
@@ -1114,7 +1151,7 @@
         up_in = lax.dynamic_index_in_dim(
             up_weight.reshape(own, groups, PARTS, ff_rows), rank, 2, keepdims=False
         ).reshape(own, groups * ff_rows)
-    gains = jnp.stack([attn_gain, ffn_gain])
+    gains = jnp.stack([attn_gain, ffn_gain]).astype(F32)
     spots = np.arange(seg)
     places = np.concatenate([spots, seg + spots[::2], seg + spots[1::2], 2 * seg + spots])
     half = HEAD_DIM // 2
@@ -1126,7 +1163,6 @@
     sines = np.concatenate([-sine, sine], axis=1)
 
     hbm = pl.BlockSpec(memory_space=pl.ANY)
-    vmem = pl.BlockSpec(memory_space=pltpu.VMEM)
     big = (seg * streams, width)
     out_shape = (
         jax.ShapeDtypeStruct(hidden.shape, BF),
@@ -1190,7 +1226,11 @@
             v((own, 2), F32),
             v((streams, seg, 2), F32),
             v((streams, seg), F32),
-            sem((18 + pieces,)),
+            v(boundary.shape, jnp.int32),
+            v(gains.shape, F32),
+            v(cosines.shape, F32),
+            v(sines.shape, F32),
+            sem((20 + pieces,)),
             sem((T_COUNT, 3)),
             sem((T_COUNT, 3)),
             sem((5, 2 * n_z + 1)),
@@ -1207,7 +1247,7 @@
     results = pl.pallas_call(
         functools.partial(kernel, n_z, own, pieces),
         out_shape=out_shape,
-        in_specs=[hbm] * 12 + [pl.BlockSpec(memory_space=pltpu.SMEM)] + [vmem] * 4,
+        in_specs=[hbm] * 16 + [pl.BlockSpec(memory_space=pltpu.SMEM)],
         out_specs=tuple([hbm] * len(out_shape)),
         scratch_shapes=scratch,
         compiler_params=pltpu.CompilerParams(
@@ -1227,11 +1267,11 @@
         conv_weight,
         grad_out,
         grad_fresh,
-        reset_flag,
         boundary,
         gains,
         cosines,
         sines,
+        reset_flag,
     )
     g_up = results[7]
     if pieces == 1:
@@ -1251,20 +1291,20 @@
         return pl.BlockSpec(tuple(shape), lambda i: (0,) * dim + (i, 0))
 
     out_types = (BF, BF) + (F32,) * 8
-    sums = jax.ShapeDtypeStruct((own, 1), F32)
+    line = jax.ShapeDtypeStruct((1, own), F32)
+    whole = lambda t: pl.BlockSpec(t.shape, lambda i: (0, 0))
     done = pl.pallas_call(
-        widen,
+        functools.partial(widen, steps),
         grid=(steps,),
         out_shape=tuple(jax.ShapeDtypeStruct(t.shape, d) for t, d in zip(moved, out_types))
-        + (sums, sums),
-        in_specs=[cut(t) for t in moved] + [cut(t) for t in weights],
-        out_specs=tuple([cut(t) for t in moved] + [cut(sums)] * 2),
+        + (line, line),
+        in_specs=[cut(t) for t in moved] + [cut(t) for t in weights] + [whole(gains)],
+        out_specs=tuple([cut(t) for t in moved] + [whole(line)] * 2),
+        scratch_shapes=[pltpu.VMEM((own, 2), F32)],
         compiler_params=pltpu.CompilerParams(vmem_limit_bytes=64000 * 1024),
         name="widen",
-    )(*moved, *weights)
-    attn_gain_grad = done[10][:, 0] / attn_gain.astype(F32)
-    ffn_gain_grad = done[11][:, 0] / ffn_gain.astype(F32)
-    return tuple(done[:10]) + (attn_gain_grad, ffn_gain_grad)
+    )(*moved, *weights, gains)
+    return tuple(done[:10]) + (done[10].reshape(own), done[11].reshape(own))
 
 
 def solution(mesh):

time: 213 us -> 209 us (0.981)
  other arithmetic: 3.61 us -> 1.26 us
where the time goes in v5:
time: 209 us; the launch traced here: 206 us
  Pallas kernels  204 us (98%)
    pallas_call x1, Pallas kernels, per_device(): pl.pallas_call(functools.partial(kernel, n_z, own, pieces), out_shape=out...  197 us
    pallas_call x1, Pallas kernels, per_device(): pl.pallas_call(functools.partial(widen, steps), grid=(steps,), out_shape=...  7.66 us

profile of v5, /device:TPU:26, one launch (start us, length us, event | category | flops | bytes accessed | tf_op | source)
XLA Modules:
  0.0 206.4 jit_solution(1979000453634593524)
XLA Ops:
  0.6 1.3 maximum_convert_fusion.gains_in.refs_14_
  1.9 196.7 %layer.1 = (bf16[2,128,1024]{2,1,0:T(8,128)(2,1)}, bf16[2,64,1024]{2,1,0:T(8,128)(2,1)}, f32[2,128,1024]{2,1,0:T(8,128)}, bf16[128,1024]{1,0:T(8,128)(2,1)}, bf1...) custom-call(bf16[2,128,1024]{2,1,0:T(8,128)(2,1)} %hidden.1, ...), custom_call_target="tpu_custom_call" | custom-call | tf_op jit(solution)/shard_map/layer/pallas_call | solution.py:1247
  198.6 7.7 %widen.1 = (bf16[2,128,1024]{2,1,0:T(8,128)(2,1)}, bf16[2,64,1024]{2,1,0:T(8,128)(2,1)}, f32[2,128,1024]{2,1,0:T(8,128)}, f32[128,1024]{1,0:T(8,128)}, f32[128,1...) custom-call(bf16[2,128,1024]{2,1,0:T(8,128)(2,1)} %get-tuple-element, ...), custom_call_target="tpu_custom_call" | custom-call | tf_op jit(solution)/shard_map/widen/pallas_call | solution.py:1296

commit v6 on v5

--- a/solution.py
+++ b/solution.py
@@ -74,9 +74,7 @@
     layer_out,
     fresh_out,
     grad_input,
-    out_q,
-    out_k,
-    out_v,
+    out_qkv,
     out_o,
     out_up,
     out_down,
@@ -528,26 +526,13 @@
                 gz_copy(g, 2, zz).start()
 
     outs = {
-        WO: (((0, col), lambda p: out_o.at[:, ds(p * col, col)]),),
-        QKV: (
-            ((0, col), lambda p: out_q.at[:, ds(p * col, col)]),
-            ((col, col), lambda p: out_k.at[:, ds(p * col, col)]),
-            ((2 * col, col), lambda p: out_v.at[:, ds(p * col, col)]),
-        ),
-        UP: tuple(
-            (
-                (i * (1024 // pieces), 1024 // pieces),
-                (lambda i: lambda p: out_up.at[:, ds((i * PARTS + p) * (1024 // pieces), 1024 // pieces)])(i),
-            )
-            for i in range(pieces)
-        ),
+        QKV: (((0, 3 * col), lambda p: out_qkv.at[p]),),
+        WO: (((0, col), lambda p: out_o.at[p]),),
+        UP: (((0, 1024), lambda p: out_up.at[p]),),
         DOWN: (((0, 1024), lambda p: out_down.at[ds(p * own, own)]),),
-        CONV: tuple(
-            ((k * col, col), (lambda k: lambda p: out_conv.at[k, :, ds(p * col, col)])(k))
-            for k in range(4)
-        ),
+        CONV: (((0, 1024), lambda p: out_conv.at[p]),),
     }
-    fin_base = {QKV: 0, WO: 3, DOWN: 4, CONV: 5, UP: 9}
+    fin_base = {g: g for g in range(5)}
 
     def fin_copy(g, j, i, p, slot_rank):
         (lane, size), slot = outs[g][j]
@@ -1093,20 +1078,35 @@
         g_drain(g)
 
 
-def widen(steps, *refs):
-    ins, weights, gains, outs, kept = refs[:10], refs[10:14], refs[14], refs[15:27], refs[27]
-    for src, dst in zip(ins, outs):
-        dst[...] = src[...].astype(dst.dtype)
+def widen(steps, pieces, *refs):
+    ins, weights, gains, outs, kept = refs[:8], refs[8:12], refs[12], refs[13:25], refs[25]
+    for src, dst in zip(ins[:3], outs):
+        dst[...] = src[...]
+    qkv, o, up, down, conv = ins[3:]
+    outs[8][...] = down[...].astype(F32)
+    if len(up.shape) == 2:
+        outs[7][...] = up[...].astype(F32)
+    else:
+        for p in range(PARTS):
+            size = up.shape[2] // pieces
+            for i in range(pieces):
+                there = pl.ds((i * PARTS + p) * size, size)
+                outs[7][:, there] = up[p, :, pl.ds(i * size, size)].astype(F32)
+    for p in range(PARTS):
+        here = pl.ds(p * 256, 256)
+        for i in range(3):
+            outs[3 + i][:, here] = qkv[p, :, pl.ds(i * 256, 256)].astype(F32)
+        outs[6][:, here] = o[p].astype(F32)
+        for k in range(4):
+            outs[9][k, :, here] = conv[p, :, pl.ds(k * 256, 256)].astype(F32)
     step = pl.program_id(0)
     block = weights[0].shape[0]
     rows = pl.ds(pl.multiple_of(step * block, block), block)
     total = jnp.zeros((block, 1), F32)
-    for w, g in zip(weights[:3], ins[3:6]):
-        total += jnp.sum(w[...].astype(F32) * g[...].astype(F32), axis=-1, keepdims=True)
+    for w, g in zip(weights[:3], outs[3:6]):
+        total += jnp.sum(w[...].astype(F32) * g[...], axis=-1, keepdims=True)
     kept[rows, 0:1] = total
-    kept[rows, 1:2] = jnp.sum(
-        weights[3][...].astype(F32) * ins[7][...].astype(F32), axis=-1, keepdims=True
-    )
+    kept[rows, 1:2] = jnp.sum(weights[3][...].astype(F32) * outs[7][...], axis=-1, keepdims=True)
 
     @pl.when(step == steps - 1)
     def _():
@@ -1168,13 +1168,11 @@
         jax.ShapeDtypeStruct(hidden.shape, BF),
         jax.ShapeDtypeStruct(grad_fresh.shape, BF),
         jax.ShapeDtypeStruct(hidden.shape, F32),
-        jax.ShapeDtypeStruct((own, width), BF),
-        jax.ShapeDtypeStruct((own, width), BF),
-        jax.ShapeDtypeStruct((own, width), BF),
-        jax.ShapeDtypeStruct((own, width), BF),
-        jax.ShapeDtypeStruct((own, width * PARTS), BF),
+        jax.ShapeDtypeStruct((PARTS, own, 3 * cols), BF),
+        jax.ShapeDtypeStruct((PARTS, own, cols), BF),
+        jax.ShapeDtypeStruct((PARTS, own, width), BF),
         jax.ShapeDtypeStruct((PARTS * own, width), BF),
-        jax.ShapeDtypeStruct((4, own, width), BF),
+        jax.ShapeDtypeStruct((PARTS, own, width), BF),
         jax.ShapeDtypeStruct((width, width), BF),
     )
 
@@ -1239,9 +1237,9 @@
             sem((5, n_z)),
             sem((5, n_z)),
             sem((5, n_z)),
-            sem((9 + pieces, 3)),
-            sem((9 + pieces, 3)),
-            sem((9 + pieces,)),
+            sem((5, 3)),
+            sem((5, 3)),
+            sem((5,)),
         ]
     )
     results = pl.pallas_call(
@@ -1273,15 +1271,20 @@
         sines,
         reset_flag,
     )
-    g_up = results[7]
+    g_up = results[5]
     if pieces == 1:
         g_up = (
-            g_up.reshape(own, PARTS, groups, ff_rows)
-            .transpose(0, 2, 1, 3)
+            g_up.reshape(PARTS, own, groups, ff_rows)
+            .transpose(1, 2, 0, 3)
             .reshape(up_weight.shape)
         )
-    steps = max(1, own // 32)
-    moved = [*results[:7], g_up, *results[8:10]]
+    steps = max(1, own // 64)
+    moved = [*results[:5], g_up, *results[6:8]]
+    square = jax.ShapeDtypeStruct((own, width), F32)
+    grads = (square,) * 4 + tuple(
+        jax.ShapeDtypeStruct(w.shape, F32) for w in (up_weight, down_weight, conv_weight)
+    )
+    shapes = tuple(jax.ShapeDtypeStruct(t.shape, t.dtype) for t in results[:3]) + grads
     weights = (query_weight, key_weight, value_weight, up_weight)
 
     def cut(t):
@@ -1290,16 +1293,14 @@
         shape[dim] //= steps
         return pl.BlockSpec(tuple(shape), lambda i: (0,) * dim + (i, 0))
 
-    out_types = (BF, BF) + (F32,) * 8
     line = jax.ShapeDtypeStruct((1, own), F32)
     whole = lambda t: pl.BlockSpec(t.shape, lambda i: (0, 0))
     done = pl.pallas_call(
-        functools.partial(widen, steps),
+        functools.partial(widen, steps, pieces),
         grid=(steps,),
-        out_shape=tuple(jax.ShapeDtypeStruct(t.shape, d) for t, d in zip(moved, out_types))
-        + (line, line),
+        out_shape=shapes + (line, line),
         in_specs=[cut(t) for t in moved] + [cut(t) for t in weights] + [whole(gains)],
-        out_specs=tuple([cut(t) for t in moved] + [whole(line)] * 2),
+        out_specs=tuple([cut(t) for t in shapes] + [whole(line)] * 2),
         scratch_shapes=[pltpu.VMEM((own, 2), F32)],
         compiler_params=pltpu.CompilerParams(vmem_limit_bytes=64000 * 1024),
         name="widen",

time: 209 us -> 208 us (level)
  no operation moved by 1% of the time
where the time goes in v6:
time: 208 us; the launch traced here: 205 us
  Pallas kernels  202 us (97%)
    pallas_call x1, Pallas kernels, per_device(): pl.pallas_call(functools.partial(kernel, n_z, own, pieces), out_shape=out...  196 us
    pallas_call x1, Pallas kernels, per_device(): pl.pallas_call(functools.partial(widen, steps, pieces), grid=(steps,), ou...  6.54 us

profile of v6, /device:TPU:26, one launch (start us, length us, event | category | flops | bytes accessed | tf_op | source)
XLA Modules:
  0.0 204.5 jit_solution(5553768321739798669)
XLA Ops:
  0.6 1.3 maximum_convert_fusion.gains_in.refs_12_
  1.9 195.9 %layer.1 = (bf16[2,128,1024]{2,1,0:T(8,128)(2,1)}, bf16[2,64,1024]{2,1,0:T(8,128)(2,1)}, f32[2,128,1024]{2,1,0:T(8,128)}, bf16[4,128,768]{2,1,0:T(8,128)(2,1)}, ...) custom-call(bf16[2,128,1024]{2,1,0:T(8,128)(2,1)} %hidden.1, ...), custom_call_target="tpu_custom_call" | custom-call | tf_op jit(solution)/shard_map/layer/pallas_call | solution.py:1245
  197.8 6.5 %widen.1 = (bf16[2,128,1024]{2,1,0:T(8,128)(2,1)}, bf16[2,64,1024]{2,1,0:T(8,128)(2,1)}, f32[2,128,1024]{2,1,0:T(8,128)}, f32[128,1024]{1,0:T(8,128)}, f32[128,1...) custom-call(bf16[2,128,1024]{2,1,0:T(8,128)(2,1)} %get-tuple-element, ...), custom_call_target="tpu_custom_call" | custom-call | tf_op jit(solution)/shard_map/widen/pallas_call | solution.py:1298

commit v7 on v6

--- a/solution.py
+++ b/solution.py
@@ -330,7 +330,7 @@
 
     def w_send_z(g):
         if relay:
-            for dz in (2, 1, 3):
+            for dz in (1, 3, 2):
 
                 @pl.when(direct(dz))
                 def _():
@@ -960,64 +960,13 @@
             qs[s, :, lanes] = t_q[...]
 
     attend_back(0, 0)
-    for s in range(2):
-        reduce_mid(T_OUT0 + s, rows_of(gpre, s), d_a.at[s, 1], y_a.at[s])
-    gz_start(UP)
-    attend_back(0, 1)
-    g_final(CONV, None)
-    attend_back(1, 0)
-    gz_relay(UP)
-    attend_back(1, 1)
-    gz_start(DOWN)
-
-    reduce_drain(T_OP, op_part, d_o.at[1])
-    l_o[...] = reduce_end(T_OP, op_part, d_o.at[0], y_o).astype(BF).reshape(1024, col)
-    gx_start(WO)
-
-    def kv_grads(i):
-        c = ds(i * 256, 256)
-        total = jnp.zeros((256, 2 * col), F32)
-        for p in range(3):
-            for s in range(2):
-                total += dot(unit[p, s, :, c], kv[s, pl.ds(p * seg, seg), :], 0, 0)
-        act[c, pl.ds(col, 2 * col)] = total.astype(BF)
-        act[c, pl.ds(0, col)] = (
-            dot(unit[2, 0, :, c], qs[0], 0, 0) + dot(unit[2, 1, :, c], qs[1], 0, 0)
-        ).astype(BF)
-
-    loop(4, kv_grads)
-    gx_start(QKV)
-    g_final(UP, gain_f)
-    gz_relay(DOWN)
-
-    def hidden_grads(i):
-        s = lax.div(i, 4)
-        c = ds(lax.rem(i, 4) * 256, 256)
-        part = dot(kv[s, pl.ds(1024, seg), :], wqkv[c, pl.ds(col, 2 * col)], 1, 1) + dot(
-            qs[s], wqkv[c, pl.ds(0, col)], 1, 1
-        )
-        gnp[ds(s * seg, seg), c] = part.astype(BF)
-
-    loop(8, hidden_grads)
-    for s in range(2):
-        reduce_start(T_GN0 + s, rows_of(gnp, s), d_b.at[s, 1], d_b.at[s, 0])
-    ld_h = load(hidden, gm_low, 13)
-    g_pass(CONV)
-    for s in range(2):
-        reduce_mid(T_GN0 + s, rows_of(gnp, s), d_b.at[s, 1], y_b.at[s])
-    gz_start(WO)
-    gz_relay(WO)
     w_cross_finish(CONV)
+
     gather_drain(T_GO, go_slot(0))
     gather_drain(T_GO1, go_slot(1))
     ld_w = [
         load(conv_all.at[pl.ds(i * seg, seg)], go.at[i], 14 + i) for i in range(2)
     ]
-    for s in range(2):
-        out = reduce_end(T_OUT0 + s, rows_of(gpre, s), d_a.at[s, 0], y_a.at[s])
-        reduce_drain(T_OUT0 + s, rows_of(gpre, s), d_a.at[s, 1])
-        y_a[s] = (middle[s] + out).astype(BF)
-    st_out = load(y_a, layer_out, 16)
     for d in ld_w:
         d.wait()
     swap_drain(T_GA, ga_src)
@@ -1042,6 +991,59 @@
     fr_dst = lambda p: fresh_out.at[:, :, ds(p * col, col)]
     swap_start(T_FR, fr_src, fr_dst)
     st_fr = load(fr_src(r), fr_dst(r), 17)
+
+    for s in range(2):
+        reduce_mid(T_OUT0 + s, rows_of(gpre, s), d_a.at[s, 1], y_a.at[s])
+    gz_start(UP)
+    attend_back(0, 1)
+    g_final(CONV, None)
+    attend_back(1, 0)
+    gz_relay(UP)
+    attend_back(1, 1)
+    gz_start(DOWN)
+
+    reduce_drain(T_OP, op_part, d_o.at[1])
+    l_o[...] = reduce_end(T_OP, op_part, d_o.at[0], y_o).astype(BF).reshape(1024, col)
+    gx_start(WO)
+
+    def kv_grads(i):
+        c = ds(i * 256, 256)
+        total = jnp.zeros((256, 2 * col), F32)
+        for p in range(3):
+            for s in range(2):
+                total += dot(unit[p, s, :, c], kv[s, pl.ds(p * seg, seg), :], 0, 0)
+        act[c, pl.ds(col, 2 * col)] = total.astype(BF)
+        act[c, pl.ds(0, col)] = (
+            dot(unit[2, 0, :, c], qs[0], 0, 0) + dot(unit[2, 1, :, c], qs[1], 0, 0)
+        ).astype(BF)
+
+    loop(4, kv_grads)
+    gx_start(QKV)
+    g_final(UP, gain_f)
+    gz_relay(DOWN)
+
+    def hidden_grads(i):
+        s = lax.div(i, 4)
+        c = ds(lax.rem(i, 4) * 256, 256)
+        part = dot(kv[s, pl.ds(1024, seg), :], wqkv[c, pl.ds(col, 2 * col)], 1, 1) + dot(
+            qs[s], wqkv[c, pl.ds(0, col)], 1, 1
+        )
+        gnp[ds(s * seg, seg), c] = part.astype(BF)
+
+    loop(8, hidden_grads)
+    for s in range(2):
+        reduce_start(T_GN0 + s, rows_of(gnp, s), d_b.at[s, 1], d_b.at[s, 0])
+    ld_h = load(hidden, gm_low, 13)
+    g_pass(CONV)
+    for s in range(2):
+        reduce_mid(T_GN0 + s, rows_of(gnp, s), d_b.at[s, 1], y_b.at[s])
+    gz_start(WO)
+    gz_relay(WO)
+    for s in range(2):
+        out = reduce_end(T_OUT0 + s, rows_of(gpre, s), d_a.at[s, 0], y_a.at[s])
+        reduce_drain(T_OUT0 + s, rows_of(gpre, s), d_a.at[s, 1])
+        y_a[s] = (middle[s] + out).astype(BF)
+    st_out = load(y_a, layer_out, 16)
     gz_start(QKV)
     g_pass(UP)
     g_final(DOWN, None)

time: 208 us -> 209 us (level)
  no operation moved by 1% of the time
where the time goes in v7:
time: 209 us; the launch traced here: 205 us
  Pallas kernels  203 us (97%)
    pallas_call x1, Pallas kernels, per_device(): pl.pallas_call(functools.partial(kernel, n_z, own, pieces), out_shape=out...  197 us
    pallas_call x1, Pallas kernels, per_device(): pl.pallas_call(functools.partial(widen, steps, pieces), grid=(steps,), ou...  6.54 us

profile of v7, /device:TPU:26, one launch (start us, length us, event | category | flops | bytes accessed | tf_op | source)
XLA Modules:
  0.0 205.4 jit_solution(2117614074661590558)
XLA Ops:
  0.6 1.3 maximum_convert_fusion.gains_in.refs_12_
  1.9 196.8 %layer.1 = (bf16[2,128,1024]{2,1,0:T(8,128)(2,1)}, bf16[2,64,1024]{2,1,0:T(8,128)(2,1)}, f32[2,128,1024]{2,1,0:T(8,128)}, bf16[4,128,768]{2,1,0:T(8,128)(2,1)}, ...) custom-call(bf16[2,128,1024]{2,1,0:T(8,128)(2,1)} %hidden.1, ...), custom_call_target="tpu_custom_call" | custom-call | tf_op jit(solution)/shard_map/layer/pallas_call | solution.py:1247
  198.7 6.5 %widen.1 = (bf16[2,128,1024]{2,1,0:T(8,128)(2,1)}, bf16[2,64,1024]{2,1,0:T(8,128)(2,1)}, f32[2,128,1024]{2,1,0:T(8,128)}, f32[128,1024]{1,0:T(8,128)}, f32[128,1...) custom-call(bf16[2,128,1024]{2,1,0:T(8,128)(2,1)} %get-tuple-element, ...), custom_call_target="tpu_custom_call" | custom-call | tf_op jit(solution)/shard_map/widen/pallas_call | solution.py:1300
